TPU v7x, 128 devices: a whole 4x4x4 slice. The times are simulated.
128 devices in a mesh: section: 2 (over x_lo), rows: 8 (over y, x_hi), chan: 8 (over z, core).
Axes of the slice: x: 4 (x_hi: 2, x_lo: 2; x = x_hi * 2 + x_lo), y: 4, z: 4, core: 2. Of those that a mesh axis runs over, the one named last changes fastest.
Arguments:
- condition: float32 [12, 128, 1024], P(None, 'rows'), may hold values from -6 to 6
- target: float32 [12, 128, 1024], P(None, 'rows'), may hold values from -6 to 6
- noise_draw: float32 [12, 128, 1024], P(None, 'rows'), may hold values from -6 to 6
- sigma_index: int32 [1], replicated, may hold values from 0 to 31
- reg_first: bfloat16 [3, 3, 12, 128], P(None, None, None, 'chan'), may hold values from -0.625 to 0.625
- reg_second: bfloat16 [3, 3, 128, 12], P(None, None, 'chan'), may hold values from -0.1875 to 0.1875
- first_kernel: bfloat16 [3, 3, 24, 128], P(None, None, None, ('section', 'chan')), may hold values from -0.4375 to 0.4375
- second_kernel: bfloat16 [3, 3, 128, 128], P(None, None, None, ('section', 'chan')), may hold values from -0.1875 to 0.1875
- third_kernel: bfloat16 [3, 3, 128, 12], P(None, None, ('section', 'chan')), may hold values from -0.1875 to 0.1875
- film_scale: bfloat16 [128], P(('section', 'chan')), may hold values from -4 to 4
Outputs:
- denoised: bfloat16 [12, 128, 1024], P(None, 'rows')
- grad_first: float32 [3, 3, 24, 128], P(None, None, None, ('section', 'chan'))
- grad_second: float32 [3, 3, 128, 128], P(None, None, None, ('section', 'chan'))
- grad_third: float32 [3, 3, 128, 12], P(None, None, ('section', 'chan'))
- grad_film: float32 [128], P(('section', 'chan'))
Inputs may be any that keep to these rules, and one draw needn't show every extreme that they name: `sigma_index`: an index into the table of 32 noise levels.
All inputs are finite; a program needn't handle non-finite values.
Results may differ from a plain program's by a relative error of at most 0.008.
Values may be sent and summed in bfloat16 or wider, within the bound.
No kernel may reach another device: no remote copies, remote signals or barrier semaphores. Data moves between devices by JAX's collectives and lax.ppermute only.
A program may use at most 128 MiB of HBM per device.

v0:
```python
import math

import jax
import jax.numpy as jnp
from jax import lax
from jax.sharding import PartitionSpec as P

COUT = 12
NSIG = 32


sigma_low = 0.25
sigma_high = 4.0
rho_power = 7.0
sigma_data = 0.5


def padded(array, sides, width):
    for axis, dim in sides:
        size, length = (lax.axis_size(axis), array.shape[dim])
        up = [(i, (i + 1) % size) for i in range(size - 1)]
        down = [(j, i) for i, j in up]
        last = lax.slice_in_dim(array, length - width, length, axis=dim)
        leading = lax.slice_in_dim(array, 0, width, axis=dim)
        before = lax.ppermute(last, axis, up)
        after = lax.ppermute(leading, axis, down)
        array = jnp.concatenate([before, array, after], axis=dim)
    return array


def noise_terms(sigma_index):
    steps_at = jnp.arange(NSIG, dtype=jnp.float32) / (NSIG - 1)
    high_root = sigma_high ** (1.0 / rho_power)
    low_root = sigma_low ** (1.0 / rho_power)
    levels = (high_root + steps_at * (low_root - high_root)) ** rho_power
    picked = jnp.arange(NSIG, dtype=jnp.int32) == sigma_index[0]
    sigma_level = jnp.sum(jnp.where(picked, levels, jnp.zeros_like(levels)))
    total_var = sigma_level * sigma_level + sigma_data * sigma_data
    skip_coef = sigma_data * sigma_data / total_var
    out_coef = sigma_level * sigma_data / jnp.sqrt(total_var)
    in_coef = 1.0 / jnp.sqrt(total_var)
    noise_coef = jnp.log(8.0 * sigma_level) / 4.0
    loss_weight = total_var / (sigma_level * sigma_data) ** 2
    return (sigma_level, skip_coef, out_coef, in_coef, noise_coef, loss_weight)


def conv_rows(grid_field, kernel):
    result_conv = lax.conv_general_dilated(
        grid_field[None],
        kernel,
        (1, 1),
        ((0, 0), (1, 1)),
        dimension_numbers=("NCHW", "HWIO", "NCHW"),
        preferred_element_type=jnp.float32,
    )
    return result_conv[0]


def kernel_grad(grid_field, delta_in):
    result_conv = lax.conv_general_dilated(
        grid_field[:, None],
        delta_in[:, None],
        (1, 1),
        ((0, 0), (1, 1)),
        dimension_numbers=("NCHW", "OIHW", "NCHW"),
        preferred_element_type=jnp.float32,
    )
    return jnp.transpose(result_conv, (2, 3, 0, 1))


def turned(kernel):
    return jnp.transpose(jnp.flip(kernel, (0, 1)), (0, 1, 3, 2))


def silu_slope(pre_act):
    sigmoid_at = jax.nn.sigmoid(pre_act)
    return sigmoid_at * (1.0 + pre_act * (1.0 - sigmoid_at))


def grid_rows(grid_field, first_row, total_rows):
    places = first_row + jnp.arange(grid_field.shape[1], dtype=jnp.int32)
    inside = (places >= 0) & (places < total_rows)
    return jnp.where(inside[None, :, None], grid_field, jnp.zeros_like(grid_field))


def shards(
    condition,
    target,
    noise_draw,
    sigma_index,
    reg_first,
    reg_second,
    first_kernel,
    second_kernel,
    third_kernel,
    film_scale,
):
    rows_dev = condition.shape[1]
    grid_width = condition.shape[2]
    total_rows = rows_dev * lax.axis_size("rows")
    slab_start = lax.axis_index("rows") * rows_dev
    section_id = lax.axis_index("section")
    member = lax.axis_index(("section", "chan"))
    local_ch = film_scale.shape[0]
    sigma_level, skip_coef, out_coef, in_coef, noise_coef, loss_weight = noise_terms(sigma_index)
    grad_scale = 1.0 / math.sqrt(COUT * total_rows * grid_width)
    cond_low = condition.astype(jnp.bfloat16)
    cond_rim = padded(cond_low, (("rows", 1),), 2)
    half_rows = rows_dev // lax.axis_size("section")
    half_start = section_id * half_rows
    reg_input = lax.dynamic_slice_in_dim(cond_rim, half_start, half_rows + 4, 1)
    reg_hidden = jax.nn.silu(conv_rows(reg_input, reg_first))
    reg_hidden = grid_rows(reg_hidden, slab_start + half_start - 1, total_rows).astype(jnp.bfloat16)
    mean_part = conv_rows(reg_hidden, reg_second)
    mean_half = lax.psum(mean_part, "chan").astype(jnp.bfloat16)
    mean_field = lax.all_gather(mean_half, "section", axis=1, tiled=True)
    resid_field = target - mean_field.astype(jnp.float32)
    noisy_field = resid_field + sigma_level * noise_draw
    scaled_in = (in_coef * noisy_field).astype(jnp.bfloat16)
    film_gain = 1.0 + noise_coef * film_scale.astype(jnp.float32)
    input_rim = padded(scaled_in, (("rows", 1),), 2)
    stacked = jnp.concatenate([input_rim, cond_rim], 0)
    whole_first, whole_film = (
        lax.all_gather(first_kernel, ("section", "chan"), axis=3, tiled=True),
        lax.all_gather(film_scale, ("section", "chan"), axis=0, tiled=True),
    )
    first_all = conv_rows(stacked, whole_first)
    gain_all = (1.0 + noise_coef * whole_film.astype(jnp.float32))[:, None, None]
    hidden_full = grid_rows(jax.nn.silu(first_all * gain_all), slab_start - 1, total_rows).astype(
        jnp.bfloat16
    )
    first_mine = lax.dynamic_slice_in_dim(first_all, member * local_ch, local_ch, 0)[:, 1:-1]
    second_act = conv_rows(hidden_full, second_kernel)
    second_hidden = jax.nn.silu(second_act).astype(jnp.bfloat16)
    second_rim = padded(second_hidden, (("rows", 1),), 1)
    out_part = conv_rows(second_rim, third_kernel)
    out_full = lax.psum(out_part, ("section", "chan"))
    den_value = skip_coef * noisy_field + out_coef * out_full
    out_delta = (2.0 * loss_weight * out_coef * grad_scale * (den_value - resid_field)).astype(
        jnp.bfloat16
    )
    out_delta_rim = padded(out_delta, (("rows", 1),), 1)
    grad_third = kernel_grad(second_rim, out_delta)
    second_delta = (conv_rows(out_delta_rim, turned(third_kernel)) * silu_slope(second_act)).astype(
        jnp.bfloat16
    )
    second_delta_rim = padded(second_delta, (("rows", 1),), 1)
    grad_second = kernel_grad(hidden_full, second_delta)
    whole_second = lax.all_gather(second_kernel, ("section", "chan"), axis=3, tiled=True)
    mine_second = turned(lax.dynamic_slice_in_dim(whole_second, member * local_ch, local_ch, 2))
    empty_sum = jnp.zeros((local_ch, rows_dev, grid_width), jnp.float32)
    shard_part = lax.all_gather(second_delta_rim, ("section", "chan"), axis=0, tiled=True)
    kernel_part = lax.slice_in_dim(mine_second, 0, shard_part.shape[0], axis=2)
    back_first = empty_sum + conv_rows(shard_part, kernel_part)
    gain_mine = film_gain[:, None, None]
    first_grad = back_first * silu_slope(first_mine * gain_mine)
    grad_film = noise_coef * jnp.sum(first_grad * first_mine, axis=(1, 2))
    first_delta = (first_grad * gain_mine).astype(jnp.bfloat16)
    grad_first = kernel_grad(stacked[:, 1:-1], first_delta)
    grad_parts = (grad_first, grad_second, grad_third, grad_film)
    den_out = den_value.astype(jnp.bfloat16)
    grad_first, grad_second, grad_third, grad_film = lax.psum(
        (grad_parts[0], grad_parts[1], grad_parts[2], grad_parts[3]), "rows"
    )
    return (den_out, grad_first, grad_second, grad_third, grad_film)


def solution(mesh):
    return jax.shard_map(
        shards,
        mesh=mesh,
        in_specs=(
            P(None, "rows", None),
            P(None, "rows", None),
            P(None, "rows", None),
            P(),
            P(None, None, None, "chan"),
            P(None, None, "chan", None),
            P(None, None, None, ("section", "chan")),
            P(None, None, None, ("section", "chan")),
            P(None, None, ("section", "chan"), None),
            P(("section", "chan")),
        ),
        out_specs=(
            P(None, "rows", None),
            P(None, None, None, ("section", "chan")),
            P(None, None, None, ("section", "chan")),
            P(None, None, ("section", "chan"), None),
            P(("section", "chan")),
        ),
        check_vma=False,
    )
```

profile of v0, /device:TPU:0, one launch (start us, length us, event | category | flops | bytes accessed | tf_op | source)
XLA Modules:
  0.0 844.1 jit_solution(11145103124998721474)
XLA Ops:
  18.9 30.4 %all-reduce = bf16[128]{0:T(256)(128)(2,1)S(1)} all-reduce(bf16[128]{0:T(256)(128)(2,1)S(1)} %dynamic-update-slice), channel_id=1, replica_groups=mesh['section'=2,'rows'=8,'chan'=8] {'section','chan'}, use_global_device_ids=true, to_apply=%add | all-reduce | flops 128 | bytes 512
  58.5 7.3 select_bitcast_fusion.1
  75.3 27.6 %all-reduce.6 = bf16[12,8,1024]{2,1,0:T(8,128)(2,1)S(1)} all-reduce(f32[12,8,1024]{2,1,0:T(8,128)S(1)} %slice_bitcast_fusion.3), channel_id=1, replica_groups=mesh['section'=2,'rows'=8,'chan'=8] {'chan'}, use_global_device_ids=true, to_apply=%region_1.2 | all-reduce | flops 98304 | bytes 589824 | tf_op jit(solution)/shard_map/psum | solution.py:115
  112.7 7.0 collective-permute-start.2
  119.8 18.4 %all_gather.16 = bf16[3,3,24,128]{2,3,1,0:T(8,128)(2,1)S(1)} all-gather(bf16[3,3,24,8]{2,3,1,0:T(8,128)(2,1)S(1)} %copy-done.8), channel_id=1, replica_groups=mesh['section'=2,'rows'=8,'chan'=8] {'section','chan'}, dimensions={3}, use_global_device_ids=true | all-gather | bytes 58752 | tf_op jit(solution)/shard_map/all_gather | solution.py:124
  150.9 8.9 %broadcast_select_fusion = f32[18,8,129,128]{3,1,2,0:T(8,128)S(1)} fusion(pred[8,129]{0,1:T(8,128)(4,1)S(1)} %copy-done.10, bf16[3,3,24,128]{2,3,1,0:T(8,128)(2,1)S(1)} %all_gather.16, bf16[24,20,1,7,2]{0,3,4,1,2:T(8,128)(2,1)S(1)} %slice.71, bf16[24,20,1,8,129]{0,3,4,1,2:T(8,128)(2,1)} %copy.92), kind=kOutput, calls=%fused_computation.56 | convolution fusion | flops 1032574464 | bytes 10571400 | tf_op jit(solution)/shard_map/conv_general_dilated | solution.py:48
  163.7 12.6 %fusion.30 = f32[16,8,129,8]{3,1,2,0:T(8,128)} fusion(bf16[3,3,128,8]{2,3,1,0:T(8,128)(2,1)S(1)} %copy-done.9, bf16[18,1,7,1,128]{4,2,3,0,1:T(8,128)(2,1)S(1)} %get-tuple-element.17, bf16[18,1,7,1,128]{4,2,3,0,1:T(8,128)(2,1)S(1)} %get-tuple-element.16, bf16[18,1,8,129,128]{4,2,3,0,1:T(8,128)(2,1)S(1)} %select_bitcast_fusion), kind=kOutput, calls=%fused_computation.39 | convolution fusion | flops 328495104 | bytes 5366784 | tf_op jit(solution)/shard_map/conv_general_dilated | solution.py:48
  185.0 7.3 collective-permute-start.4
  192.3 18.4 %all_gather.19 = bf16[3,3,128,128]{2,3,1,0:T(8,128)(2,1)} all-gather(bf16[3,3,128,8]{2,3,1,0:T(8,128)(2,1)S(1)} %copy-done.9), channel_id=1, replica_groups=mesh['section'=2,'rows'=8,'chan'=8] {'section','chan'}, dimensions={3}, use_global_device_ids=true | all-gather | bytes 313344 | tf_op jit(solution)/shard_map/all_gather | solution.py:149
  211.5 18.9 %copy.120 = f32[18,8,129,128]{2,1,3,0:T(8,128)} copy(f32[18,8,129,128]{3,1,2,0:T(8,128)} %copy-done.2) | data formatting | bytes 19021824 | tf_op jit(solution)/shard_map/conv_general_dilated | solution.py:48
  230.4 17.9 %reshape.184 = f32[18,1,1032,128]{2,3,0,1:T(8,128)} reshape(f32[18,8,129,128]{2,1,3,0:T(8,128)} %copy.120) | data formatting | bytes 19021824 | tf_op jit(solution)/shard_map/conv_general_dilated | solution.py:48
  255.9 11.2 %broadcast_select_fusion.3 = f32[16,8,129,12]{3,1,2,0:T(8,128)} fusion(pred[8,129]{0,1:T(8,128)(4,1)S(1)} %copy-done.10, bf16[3,3,8,12]{3,2,1,0:T(8,128)(2,1)S(1)} %copy-done.13, bf16[8,18,1,7,2]{0,3,4,1,2:T(8,128)(2,1)S(1)} %slice.77, bf16[8,18,1,8,129]{0,3,4,1,2:T(8,128)(2,1)} %copy.95), kind=kOutput, calls=%fused_computation.59 | convolution fusion | flops 29636352 | bytes 1096584 | tf_op jit(solution)/shard_map/conv_general_dilated | solution.py:48
  267.0 8.0 copy.96
  278.2 8.4 %select_convert_fusion.1 = bf16[128,1,18,1024]{3,0,2,1:T(8,128)(2,1)} fusion(f32[128]{0:T(128)S(1)} %multiply_add_fusion.3, pred[18]{0:T(512)(128)(4,1)S(1)} %compare_and_fusion, f32[18,1,1032,128]{2,3,0,1:T(8,128)} %reshape.184), kind=kLoop, calls=%fused_computation.14 | loop fusion | flops 16515072 | bytes 14156306 | tf_op jit(solution)/shard_map/convert_element_type | solution.py:129
  287.3 111.4 %all-reduce.5.cloned.1.call-done = f32[12,16,1024]{2,1,0:T(8,128)} async-done(((f32[12,16,1024]{2,1,0:T(8,128)}), f32[12,16,1024]{2,1,0:T(8,128)}) %all-reduce.5.cloned.1.call-update) | async-done | bytes 786448 | tf_op jit(solution)/shard_map/psum | solution.py:137
  410.0 9.3 %slice.88 = f32[18,1,1024,128]{2,3,0,1:T(8,128)} slice(f32[18,1,1032,128]{2,3,0,1:T(8,128)} %reshape.184), slice={[0:18], [0:1], [0:1024], [0:128]} | slice | bytes 18874368 | tf_op jit(solution)/shard_map/conv_general_dilated | solution.py:48
  429.1 11.0 %broadcast_select_fusion.2 = f32[16,8,129,8]{3,1,2,0:T(8,128)} fusion(pred[8,129]{0,1:T(8,128)(4,1)S(1)} %copy-done.10, bf16[3,3,8,12]{3,2,1,0:T(8,128)(2,1)S(1)} %copy-done.13, bf16[12,18,1,7,2]{0,3,4,1,2:T(8,128)(2,1)S(1)} %slice.82, bf16[12,18,1,8,129]{0,3,4,1,2:T(8,128)(2,1)} %copy.99), kind=kOutput, calls=%fused_computation.58 | convolution fusion | flops 30023040 | bytes 983016 | tf_op jit(solution)/shard_map/conv_general_dilated | solution.py:48
  440.1 7.5 copy.100
  458.8 13.2 %copy.108 = bf16[24,1,18,1024]{0,1,3,2:T(2,128)(2,1)} copy(bf16[24,1,18,1024]{3,2,0,1:T(8,128)(2,1)S(1)} %slice_bitcast_fusion) | data formatting | bytes 1769472 | tf_op jit(solution)/shard_map/broadcast_in_dim | solution.py:61
  472.1 21.3 %copy.110 = bf16[128,1,18,1024]{0,1,3,2:T(2,128)(2,1)} copy(bf16[128,1,18,1024]{3,0,2,1:T(8,128)(2,1)} %select_convert_fusion.1) | data formatting | bytes 9437184 | tf_op jit(solution)/shard_map/convert_element_type | solution.py:129
  493.4 15.4 %copy.112 = bf16[8,1,18,1024]{0,1,3,2:T(2,128)(2,1)} copy(bf16[8,1,18,1024]{3,0,2,1:T(8,128)(2,1)S(1)} %copy-done.6) | data formatting | bytes 589824 | tf_op jit(solution)/shard_map/broadcast_in_dim | solution.py:61
  508.8 9.0 %copy.113 = bf16[12,1,16,1024]{0,1,3,2:T(2,128)(2,1)} copy(bf16[12,1,16,1024]{3,2,0,1:T(8,128)(2,1)S(1)} %bitcast.183) | data formatting | bytes 786432 | tf_op jit(solution)/shard_map/broadcast_in_dim | solution.py:62
  518.6 52.5 %fusion.140 = f32[3,3,8,12]{3,2,1,0:T(8,128)S(1)} fusion(bf16[8,1,18,1024]{0,1,3,2:T(2,128)(2,1)} %copy.112, bf16[12,1,16,1024]{0,1,3,2:T(2,128)(2,1)} %copy.113), kind=kOutput, calls=%fused_computation.171 | convolution fusion | flops 28293120 | bytes 691584 | tf_op jit(solution)/shard_map/transpose | solution.py:68
  571.3 14.2 %copy.111 = bf16[8,1,16,1024]{0,1,3,2:T(2,128)(2,1)} copy(bf16[8,1,16,1024]{3,0,2,1:T(8,128)(2,1)S(1)} %fusion.84) | data formatting | bytes 524288 | tf_op jit(solution)/shard_map/convert_element_type | solution.py:144
  585.5 66.0 %fusion.139 = f32[3,3,128,8]{2,3,1,0:T(8,128)S(1)} fusion(bf16[128,1,18,1024]{0,1,3,2:T(2,128)(2,1)} %copy.110, bf16[8,1,16,1024]{0,1,3,2:T(2,128)(2,1)} %copy.111), kind=kOutput, calls=%fused_computation.170 | convolution fusion | flops 301793280 | bytes 5017600 | tf_op jit(solution)/shard_map/transpose | solution.py:68
  651.5 7.7 pad.12
  659.1 17.5 %reshape.183 = bf16[128,18,1,8,129]{4,3,0,1,2:T(8,128)(2,1)} reshape(bf16[128,18,1,1032]{3,0,1,2:T(8,128)(2,1)} %pad.12) | data formatting | bytes 9510912 | tf_op jit(solution)/shard_map/conv_general_dilated | solution.py:48
  676.6 13.1 %copy.103 = bf16[128,18,1,8,129]{0,3,4,1,2:T(8,128)(2,1)} copy(bf16[128,18,1,8,129]{4,3,0,1,2:T(8,128)(2,1)} %reshape.183) | data formatting | bytes 9510912 | tf_op jit(solution)/shard_map/conv_general_dilated | solution.py:48
  690.7 14.4 %broadcast_select_fusion.1 = f32[16,8,129,8]{3,1,2,0:T(8,128)} fusion(pred[8,129]{0,1:T(8,128)(4,1)S(1)} %copy-done.10, bf16[128,18,1,7,2]{0,3,4,1,2:T(8,128)(2,1)S(1)} %slice.86, bf16[128,18,1,8,129]{0,3,4,1,2:T(8,128)(2,1)} %copy.103, bf16[3,3,128,128]{2,3,1,0:T(8,128)(2,1)S(1)} %copy-done.7, s32[]{:T(128)S(6)} %select_n.34), kind=kOutput, calls=%fused_computation.57 | convolution fusion | flops 318968832 | bytes 5644300 | tf_op jit(solution)/shard_map/conv_general_dilated | solution.py:48
  712.9 14.2 %copy.109 = bf16[8,1,16,1024]{0,1,3,2:T(2,128)(2,1)} copy(bf16[8,1,16,1024]{3,0,2,1:T(8,128)(2,1)S(1)} %fusion.101) | data formatting | bytes 524288 | tf_op jit(solution)/shard_map/broadcast_in_dim | solution.py:62
  727.1 66.0 %fusion.138 = f32[3,3,24,8]{2,3,1,0:T(8,128)S(1)} fusion(bf16[24,1,18,1024]{0,1,3,2:T(2,128)(2,1)} %copy.108, bf16[8,1,16,1024]{0,1,3,2:T(2,128)(2,1)} %copy.109), kind=kOutput, calls=%fused_computation.169 | convolution fusion | flops 56586240 | bytes 1153792 | tf_op jit(solution)/shard_map/transpose | solution.py:68
  793.1 43.7 %all-reduce.1 = (f32[3,3,24,8]{2,3,1,0:T(8,128)}, f32[3,3,128,8]{2,3,1,0:T(8,128)}, f32[3,3,8,12]{3,2,1,0:T(8,128)}, f32[8]{0:T(128)}) all-reduce(f32[3,3,24,8]{2,3,1,0:T(8,128)S(1)} %fusion.138, f32[3,3,128,8]{2,3,1,0:T(8,128)S(1)} %fusion.139, ...), channel_id=1, replica_groups=mesh['section'=2,'rows'=8,'chan'=8] {'rows'}, use_global_device_ids=true, to_apply=%region_3.4 | all-reduce | flops 11816 | bytes 94528 | tf_op jit(solution)/shard_map/psum | solution.py:162
  (113 shorter events, 115.3 us)
Async XLA Ops:
  7.2 51.3 %copy-start = (bf16[3,3,12,16]{3,2,1,0:T(8,128)(2,1)S(1)}, bf16[3,3,12,16]{3,2,1,0:T(8,128)(2,1)}, u32[]{:S(2)}) copy-start(bf16[3,3,12,16]{3,2,1,0:T(8,128)(2,1)} %param.14) | copy-start | bytes 10372
  7.2 51.3 %copy-start.10 = (pred[8,129]{0,1:T(8,128)(4,1)S(1)}, pred[8,129]{0,1:T(8,128)(4,1)}, u32[]{:S(2)}) copy-start(pred[8,129]{0,1:T(8,128)(4,1)} %constant.100) | copy-start | bytes 3100
  7.2 391.5 %all-reduce.5.cloned.1.call-start = ((), (), s32[]{:S(2)}) async-start(), calls=%async_computation | async-start | bytes 1572864 | tf_op jit(solution)/shard_map/psum | solution.py:137
  8.5 44.0 %collective-permute-start = (bf16[12,2,1024]{2,1,0:T(2,128)(2,1)S(1)}, bf16[12,2,1024]{2,1,0:T(2,128)(2,1)S(1)}, u32[]{:S(2)}, u32[]{:S(2)}) collective-permute-start(bf16[12,2,1024]{2,1,0:T(2,128)(2,1)S(1)} %get-tuple-element.26), channel_id=1, source_target_pairs={{0,8},{8,16},{16,24},{24,32},{32,40},{40,48},{48,56},{1,9},{9,17},... | collective-permute-start | bytes 147464 | tf_op jit(solution)/shard_map/ppermute | solution.py:25
  13.5 39.0 %collective-permute-start.1 = (bf16[12,2,1024]{2,1,0:T(2,128)(2,1)S(1)}, bf16[12,2,1024]{2,1,0:T(2,128)(2,1)S(1)}, u32[]{:S(2)}, u32[]{:S(2)}) collective-permute-start(bf16[12,2,1024]{2,1,0:T(2,128)(2,1)S(1)} %get-tuple-element.27), channel_id=1, source_target_pairs={{8,0},{16,8},{24,16},{32,24},{40,32},{48,40},{56,48},{9,1},{17,9},... | collective-permute-start | bytes 147464 | tf_op jit(solution)/shard_map/ppermute | solution.py:26
  58.5 7.4 copy-start.12
  70.7 38.6 %copy-start.4 = (f32[12,16,1024]{2,1,0:T(8,128)S(1)}, f32[12,16,1024]{2,1,0:T(8,128)}, u32[]{:S(2)}) copy-start(f32[12,16,1024]{2,1,0:T(8,128)} %param.11) | copy-start | bytes 2359300
  70.7 49.0 %copy-start.8 = (bf16[3,3,24,8]{2,3,1,0:T(8,128)(2,1)S(1)}, bf16[3,3,24,8]{2,3,1,0:T(8,128)(2,1)}, u32[]{:S(2)}) copy-start(bf16[3,3,24,8]{2,3,1,0:T(8,128)(2,1)} %param.16) | copy-start | bytes 10372
  109.3 28.8 %copy-start.3 = (bf16[12,16,1024]{2,1,0:T(8,128)(2,1)}, bf16[12,16,1024]{2,1,0:T(8,128)(2,1)S(1)}, u32[]{:S(2)}) copy-start(bf16[12,16,1024]{2,1,0:T(8,128)(2,1)S(1)} %all_gather.15) | copy-start | bytes 1179652
  111.4 26.7 %collective-permute-start.3 = (bf16[12,2,1024]{2,1,0:T(2,128)(2,1)S(1)}, bf16[12,2,1024]{2,1,0:T(2,128)(2,1)S(1)}, u32[]{:S(2)}, u32[]{:S(2)}) collective-permute-start(bf16[12,2,1024]{2,1,0:T(2,128)(2,1)S(1)} %get-tuple-element.25), channel_id=1, source_target_pairs={{8,0},{16,8},{24,16},{32,24},{40,32},{48,40},{56,48},{9,1},{17,9},... | collective-permute-start | bytes 147464 | tf_op jit(solution)/shard_map/ppermute | solution.py:26
  112.7 25.4 %collective-permute-start.2 = (bf16[12,2,1024]{2,1,0:T(2,128)(2,1)S(1)}, bf16[12,2,1024]{2,1,0:T(2,128)(2,1)S(1)}, u32[]{:S(2)}, u32[]{:S(2)}) collective-permute-start(bf16[12,2,1024]{2,1,0:T(2,128)(2,1)S(1)} %get-tuple-element.24), channel_id=1, source_target_pairs={{0,8},{8,16},{16,24},{24,32},{32,40},{40,48},{48,56},{1,9},{9,17},... | collective-permute-start | bytes 147464 | tf_op jit(solution)/shard_map/ppermute | solution.py:25
  159.7 3.9 copy-start.2
  159.8 3.9 copy-start.9
  183.7 64.6 %collective-permute-start.5 = (bf16[8,1,1024]{2,0,1:T(8,128)(2,1)S(1)}, bf16[8,1,1024]{2,0,1:T(8,128)(2,1)S(1)}, u32[]{:S(2)}, u32[]{:S(2)}) collective-permute-start(bf16[8,1,1024]{2,0,1:T(8,128)(2,1)S(1)} %get-tuple-element.33), channel_id=1, source_target_pairs={{8,0},{16,8},{24,16},{32,24},{40,32},{48,40},{56,48},{9,1},{17,9},... | collective-permute-start | bytes 49160 | tf_op jit(solution)/shard_map/ppermute | solution.py:26
  185.0 63.3 %collective-permute-start.4 = (bf16[8,1,1024]{2,0,1:T(8,128)(2,1)S(1)}, bf16[8,1,1024]{2,0,1:T(8,128)(2,1)S(1)}, u32[]{:S(2)}, u32[]{:S(2)}) collective-permute-start(bf16[8,1,1024]{2,0,1:T(8,128)(2,1)S(1)} %get-tuple-element.32), channel_id=1, source_target_pairs={{0,8},{8,16},{16,24},{24,32},{32,40},{40,48},{48,56},{1,9},{9,17},... | collective-permute-start | bytes 49160 | tf_op jit(solution)/shard_map/ppermute | solution.py:25
  248.3 7.5 copy-start.13
  278.1 373.3 %all-gather.2.cloned.1.call-start = ((), (), s32[]{:S(2)}) async-start(), calls=%async_computation.1 | async-start | bytes 5013504 | tf_op jit(solution)/shard_map/all_gather | solution.py:152
  402.2 17.1 %collective-permute-start.7 = (bf16[12,1,1024]{2,1,0:T(2,128)(2,1)S(1)}, bf16[12,1,1024]{2,1,0:T(2,128)(2,1)S(1)}, u32[]{:S(2)}, u32[]{:S(2)}) collective-permute-start(bf16[12,1,1024]{2,1,0:T(2,128)(2,1)S(1)} %get-tuple-element.23), channel_id=1, source_target_pairs={{8,0},{16,8},{24,16},{32,24},{40,32},{48,40},{56,48},{9,1},{17,9},... | collective-permute-start | bytes 73736 | tf_op jit(solution)/shard_map/ppermute | solution.py:26
  403.5 15.8 %collective-permute-start.6 = (bf16[12,1,1024]{2,1,0:T(2,128)(2,1)S(1)}, bf16[12,1,1024]{2,1,0:T(2,128)(2,1)S(1)}, u32[]{:S(2)}, u32[]{:S(2)}) collective-permute-start(bf16[12,1,1024]{2,1,0:T(2,128)(2,1)S(1)} %get-tuple-element.22), channel_id=1, source_target_pairs={{0,8},{8,16},{16,24},{24,32},{32,40},{40,48},{48,56},{1,9},{9,17},... | collective-permute-start | bytes 73736 | tf_op jit(solution)/shard_map/ppermute | solution.py:25
  449.4 68.4 %collective-permute-start.9 = (bf16[8,1,1024]{2,0,1:T(8,128)(2,1)S(1)}, bf16[8,1,1024]{2,0,1:T(8,128)(2,1)S(1)}, u32[]{:S(2)}, u32[]{:S(2)}) collective-permute-start(bf16[8,1,1024]{2,0,1:T(8,128)(2,1)S(1)} %get-tuple-element.31), channel_id=1, source_target_pairs={{8,0},{16,8},{24,16},{32,24},{40,32},{48,40},{56,48},{9,1},{17,9},... | collective-permute-start | bytes 49160 | tf_op jit(solution)/shard_map/ppermute | solution.py:26
  450.7 67.1 %collective-permute-start.8 = (bf16[8,1,1024]{2,0,1:T(8,128)(2,1)S(1)}, bf16[8,1,1024]{2,0,1:T(8,128)(2,1)S(1)}, u32[]{:S(2)}, u32[]{:S(2)}) collective-permute-start(bf16[8,1,1024]{2,0,1:T(8,128)(2,1)S(1)} %get-tuple-element.30), channel_id=1, source_target_pairs={{0,8},{8,16},{16,24},{24,32},{32,40},{40,48},{48,56},{1,9},{9,17},... | collective-permute-start | bytes 49160 | tf_op jit(solution)/shard_map/ppermute | solution.py:25
  472.1 21.3 %copy-start.6 = (bf16[8,1,18,1024]{3,0,2,1:T(8,128)(2,1)S(1)}, bf16[8,1,18,1024]{3,0,2,1:T(8,128)(2,1)}, u32[]{:S(2)}) copy-start(bf16[8,1,18,1024]{3,0,2,1:T(8,128)(2,1)} %get-tuple-element.28) | copy-start | bytes 884740
  676.6 14.1 %copy-start.7 = (bf16[3,3,128,128]{2,3,1,0:T(8,128)(2,1)S(1)}, bf16[3,3,128,128]{2,3,1,0:T(8,128)(2,1)}, u32[]{:S(2)}) copy-start(bf16[3,3,128,128]{2,3,1,0:T(8,128)(2,1)} %all_gather.19) | copy-start | bytes 884740
  705.0 7.3 copy-start.5
  705.0 7.3 copy-start.11
  727.1 109.7 %copy-start.1 = (bf16[3,3,12,16]{3,2,1,0:T(8,128)(2,1)S(1)}, bf16[3,3,12,16]{3,2,1,0:T(8,128)(2,1)}, u32[]{:S(2)}) copy-start(bf16[3,3,12,16]{3,2,1,0:T(8,128)(2,1)} %param.14) | copy-start | bytes 10372
Sparse Core Ops, SparseCore 0:
  278.3 120.3 all-reduce.4
  518.7 40.0 all-gather.1
where the time goes:
time: 855 us; the launch traced here: 844 us
  matrix products  255 us (30%)
  local copies, waits for them, and re-layouts  251 us (29%)
  blocking collectives  145 us (17%)
  waiting for transfers between devices  111 us (13%)
  starting transfers between devices  38 us (4%)
  other arithmetic  25.3 us (3%)
  between operations  19.2 us (2%)
    transpose x3, matrix products, kernel_grad(): return jnp.transpose(result_conv, (2, 3, 0, 1))  184 us
    conv_general_dilated x28, local copies, waits for them, and re-layouts, conv_rows(): lax.conv_general_dilated(grid_field[None], kernel, (1, 1), ((0, 0), (1, 1...  147 us
    psum x1, waiting for transfers between devices, shards(): out_full = lax.psum(out_part, ('section', 'chan'))  111 us
    conv_general_dilated x7, matrix products, conv_rows(): lax.conv_general_dilated(grid_field[None], kernel, (1, 1), ((0, 0), (1, 1...  70.3 us
    psum x1, blocking collectives, shards(): lax.psum((grad_parts[0], grad_parts[1], grad_parts[2], grad_parts[3]), 'r...  43.7 us
    ppermute x5, starting transfers between devices, padded(): before = lax.ppermute(last, axis, up)  31.5 us
    unnamed x1, blocking collectives  30.4 us
    broadcast_in_dim x3, local copies, waits for them, and re-layouts, kernel_grad(): grid_field[:, None]  29 us
  transfers between devices with their start and end apart: 12, of which 1 were waited for; matrix products, arithmetic and copies ran while one was open for 30% of the time, Pallas kernels for 0%

commit v1 on v0

v1 whole, which is shorter than its diff:
```python
import math

import numpy as np
import jax
import jax.numpy as jnp
from jax import lax
from jax.experimental import pallas as pl
from jax.experimental.pallas import tpu as pltpu
from jax.sharding import PartitionSpec as P

COUT = 12
NSIG = 32
NH = 128
NW = 1024
TW = 64
RIM = 8
PLANES = 5
SUB = 16
WIN = PLANES * SUB
TAPS = 9
FILM_LANE = 120
MIB = 1024 * 1024
GROUP = ("section", "chan")
f32 = jnp.float32
bf16 = jnp.bfloat16


def coef_table():
    i = np.arange(NSIG, dtype=np.float64)
    high, low = 4.0 ** (1 / 7), 0.25 ** (1 / 7)
    level = (high + i / (NSIG - 1) * (low - high)) ** 7
    total = level**2 + 0.25
    out_coef = 0.5 * level / np.sqrt(total)
    weight = total / (0.5 * level) ** 2
    table = np.zeros((NSIG, 8), np.float32)
    table[:, 0] = level
    table[:, 1] = 0.25 / total
    table[:, 2] = out_coef
    table[:, 3] = 1 / np.sqrt(total)
    table[:, 4] = np.log(8 * level) / 4
    table[:, 5] = 2 * weight * out_coef / math.sqrt(COUT * NH * NW)
    return table


def place_constants():
    sel_first = np.zeros((TAPS, 24, 256), np.float32)
    sel_low = np.zeros((TAPS, COUT, 128), np.float32)
    for tap in range(TAPS):
        for c in range(COUT):
            sel_first[tap, c, tap * COUT + c] = 1
            sel_first[tap, COUT + c, 128 + tap * COUT + c] = 1
            sel_low[tap, c, tap * COUT + c] = 1
    order = np.zeros((WIN, 128), np.float32)
    back = np.zeros((WIN, 128), np.float32)
    for t in range(PLANES):
        for s in range(SUB):
            col = PLANES * s + t
            order[t * SUB + s, col] = 1
            if RIM <= col < RIM + TW:
                back[t * SUB + s, col - RIM] = 1
                back[t * SUB + s, TW + col - RIM] = 1
    spread = np.zeros((128, 384), np.float32)
    repeat = np.zeros((128, 10 * 128), np.float32)
    for c in range(COUT):
        for g in range(TAPS):
            spread[24 + c, g * COUT + c] = 1
            for first in (0, 48, 80):
                spread[first + c, 128 + g * COUT + c] = 1
                spread[first + COUT + c, 256 + g * COUT + c] = 1
            for tap in range(TAPS):
                repeat[tap * COUT + c, tap * 128 + g * COUT + c] = 1
            repeat[(8 - g) * COUT + c, 9 * 128 + g * COUT + c] = 1
    return sel_first, sel_low, order, back, spread, repeat


def dot(a, b, ca=1, cb=0):
    return lax.dot_general(a, b, (((ca,), (cb,)), ((), ())), preferred_element_type=f32)


def sigmoid(v):
    return 1.0 / (1.0 + jnp.exp(-v))


def member():
    return lax.axis_index("section") * lax.axis_size("chan") + lax.axis_index("chan")


def pack_kernel(cond, target, noise, w1, w2, w3, r1, r2, film, sel_first, sel_low,
                own, last, leading, packed, scr, sems):
    start = member() * TW - RIM
    base = jnp.clip((start + 128) // 128 * 128 - 128, 0, NW - 256)
    base = pl.multiple_of(base, 128)
    copies = []
    for k, src in enumerate((target, noise, cond)):
        copy = pltpu.make_async_copy(src.at[:, :, pl.ds(base, 256)], scr.at[k], sems.at[k])
        copy.start()
        copies.append(copy)
    half = lax.axis_index("section") == 0
    eye = (lax.broadcasted_iota(jnp.int32, (8, 8), 0)
           == lax.broadcasted_iota(jnp.int32, (8, 8), 1)).astype(f32)
    blocks = []
    for a in range(3):
        for b in range(3):
            blocks.append(dot(eye, w2[a, b].astype(f32), 1, 1))
    first = jnp.zeros((8, 256), f32)
    third = jnp.zeros((8, 128), f32)
    reg_a = jnp.zeros((16, 128), f32)
    reg_b = jnp.zeros((16, 128), f32)
    for a in range(3):
        for b in range(3):
            tap = 3 * a + b
            first += dot(w1[a, b].astype(f32), sel_first[tap], 0, 0)
            third += dot(w3[a, b].astype(f32), sel_low[tap])
            reg_a += dot(r1[a, b].astype(f32), sel_low[tap], 0, 0)
            reg_b += dot(r2[a, b].astype(f32), sel_low[tap])
    lane = lax.broadcasted_iota(jnp.int32, (8, 128), 1)
    film_col = jnp.sum(eye * film[...].astype(f32), axis=1, keepdims=True)
    third = jnp.where(lane == FILM_LANE, film_col, third)
    blocks += [first[:, :128], first[:, 128:], third,
               jnp.where(half, reg_a[:8], reg_a[8:]), jnp.where(half, reg_b[:8], reg_b[8:])]
    for p in range(7):
        pair = jnp.concatenate(blocks[2 * p:2 * p + 2], axis=0).astype(bf16)
        for q in range(16):
            packed[q, p * 16:(p + 1) * 16, :] = pair
    offset = start - base
    shift = lax.rem(512 - offset, 256)
    for k, copy in enumerate(copies):
        copy.wait()
        rows = scr[k].reshape(COUT * 16, 256)
        moved = pltpu.roll(rows, shift, 1)[:, :128]
        col = start + lax.broadcasted_iota(jnp.int32, moved.shape, 1)
        moved = jnp.where((col >= 0) & (col < NW), moved, 0.0).reshape(COUT, 16, 128)
        own[k * COUT:(k + 1) * COUT] = moved
        last[k * COUT:(k + 1) * COUT] = moved[:, 8:]
        leading[k * COUT:(k + 1) * COUT] = moved[:, :8]


def put(ref, at, n, value):
    ref[pl.ds(at, n), 1:PLANES + 1] = value.astype(bf16)
    ref[pl.ds(at, n), 0] = pltpu.roll(value[:, PLANES - 1], 1, 1).astype(bf16)
    ref[pl.ds(at, n), PLANES + 1] = pltpu.roll(value[:, 0], SUB - 1, 1).astype(bf16)


def stack_taps(ref, at, n):
    parts = []
    for a in range(3):
        for b in range(3):
            parts.append(ref[pl.ds(at + a - 1, n), b:b + PLANES].reshape(n * WIN, 128))
    return jnp.concatenate(parts, axis=1)


def pick_taps(ref, at, n):
    lane = lax.broadcasted_iota(jnp.int32, (SUB, 128), 1)
    total = None
    for a in range(3):
        for b in range(3):
            low = (3 * a + b) * COUT
            mask = jnp.where((lane >= low) & (lane < low + COUT), 1.0, 0.0).astype(bf16)
            part = ref[pl.ds(at + a - 1, n), b:b + PLANES] * mask[None, None]
            total = part if total is None else total + part
    return total


def prep_kernel(own, before, after, order, spread, cond_taps, target9, noise9, scr, cond9, sems):
    copies = [
        pltpu.make_async_copy(before, scr.at[0:36, 0:8, :], sems.at[0]),
        pltpu.make_async_copy(own, scr.at[0:36, 8:24, :], sems.at[1]),
        pltpu.make_async_copy(after, scr.at[0:36, 24:32, :], sems.at[2]),
    ]
    for copy in copies:
        copy.start()
    scr[36:48] = jnp.zeros((12, 32, 128), f32)
    for copy in copies:
        copy.wait()
    flat = scr.reshape(48 * 32, 128)

    def row(i):
        x = flat[pl.ds(i, 48, stride=32), :]
        high = x.astype(bf16)
        rest = x[:32] - high[:32].astype(f32)
        mid = rest.astype(bf16)
        low = (rest - mid.astype(f32)).astype(bf16)
        rows = jnp.concatenate([high, mid, low, jnp.zeros((16, 128), bf16)], axis=0)
        cells = dot(order[...], rows, 1, 1).astype(bf16)
        wide = dot(cells, spread[...]).reshape(1, PLANES, SUB, 384)
        put(cond9, i, 1, wide[..., :128])
        return wide

    for i in range(1, 31):
        wide = row(i)
        if 3 <= i < 29:
            target9[i - 3:i - 2] = wide[..., 128:256]
            noise9[i - 3:i - 2] = wide[..., 256:]

    @pl.loop(0, 7)
    def _(k):
        at = 2 + 4 * k
        cond_taps[pl.ds(at - 2, 4)] = pick_taps(cond9, at, 4)


def step_kernel(index, table, cond_taps, target9, noise9, gathered, repeat, back, out,
                w2, w2t, w1, w3, w3f, w3r, r1, r2,
                hid, inp, one, two, dlt, sdl, taps_in, taps_d, resid, noisy, act, slope,
                den, grad1, film_sum, den_rows):
    level = index[0]
    sigma, skip, out_coef = table[level, 0], table[level, 1], table[level, 2]
    in_coef, noise_coef, delta_coef = table[level, 3], table[level, 4], table[level, 5]
    first_row = lax.axis_index("rows") * 16 - RIM
    first_col = member() * TW - RIM

    def block(k):
        pair = gathered[:, (k // 2) * 16:(k // 2 + 1) * 16, :].astype(f32)
        low = (k % 2) * 8
        return pair[:, low:low + 8].reshape(128, 128).astype(bf16)

    for tap in range(TAPS):
        part = block(tap)
        w2[:, tap * 128:(tap + 1) * 128] = part
        w2t[(8 - tap) * 128:(9 - tap) * 128, :] = part
    w1[:, :128] = block(9)
    w1[:, 128:] = block(10)
    w3[...] = block(11)
    r1[...] = block(12)
    wide = dot(w3[...], repeat[...]).astype(bf16)
    for tap in range(TAPS):
        w3r[tap * 128:(tap + 1) * 128, :] = wide[:, tap * 128:(tap + 1) * 128]
    w3f[...] = wide[:, 9 * 128:]
    wide = dot(block(13), repeat[:, :9 * 128]).astype(bf16)
    for tap in range(TAPS):
        r2[tap * 128:(tap + 1) * 128, :] = wide[:, tap * 128:(tap + 1) * 128]
    lane = lax.broadcasted_iota(jnp.int32, (16, 128), 1)
    pick_film = jnp.where(lane == FILM_LANE, 1.0, 0.0).astype(bf16)
    gain = 1.0 + noise_coef * dot(pick_film, w3[...], 1, 1)[0:1]

    def grid_mask(at, n):
        shape = (n, PLANES, SUB, 128)
        row = lax.broadcasted_iota(jnp.int32, shape, 0) + (at + first_row)
        col = (lax.broadcasted_iota(jnp.int32, shape, 2) * PLANES
               + lax.broadcasted_iota(jnp.int32, shape, 1) + first_col)
        return (row >= 0) & (row < NH) & (col >= 0) & (col < NW)

    def tile_mask(n):
        shape = (n, PLANES, SUB, 128)
        col = (lax.broadcasted_iota(jnp.int32, shape, 2) * PLANES
               + lax.broadcasted_iota(jnp.int32, shape, 1))
        return (col >= RIM) & (col < RIM + TW)

    def cells(value, n):
        return value.reshape(n, PLANES, SUB, 128)

    def flat(value):
        return value.reshape(-1, 128)

    def sweep(first, count, n, body):
        @pl.loop(0, count // n)
        def _(k):
            body(first + k * n, n)

    def reg_one(at, n):
        v = dot(flat(cond_taps[pl.ds(at - 2, n)]), r1[...], 1, 1)
        v = cells(v * sigmoid(v), n)
        put(hid, at, n, jnp.where(grid_mask(at, n), v, 0.0))

    sweep(2, 28, 7, reg_one)

    def reg_two(at, n):
        mean = cells(dot(stack_taps(hid, at, n), r2[...]), n).astype(bf16).astype(f32)
        rest = target9[pl.ds(at - 3, n)] - mean
        noised = rest + sigma * noise9[pl.ds(at - 3, n)]
        resid[pl.ds(at - 3, n)] = rest
        noisy[pl.ds(at - 3, n)] = noised
        put(inp, at, n, jnp.where(grid_mask(at, n), in_coef * noised, 0.0))

    sweep(3, 26, 13, reg_two)

    def conv_one(at, n):
        picked = pick_taps(inp, at, n)
        taps_in[pl.ds(at - 4, n)] = picked
        both = jnp.concatenate([flat(picked), flat(cond_taps[pl.ds(at - 2, n)])], axis=1)
        v = dot(both, w1[...], 1, 1)
        act[pl.ds(at - 4, n)] = cells(v, n)
        v = v * gain
        v = cells(v * sigmoid(v), n)
        put(one, at, n, jnp.where(grid_mask(at, n), v, 0.0))

    sweep(4, 24, 6, conv_one)

    def conv_two(at, n):
        v = dot(stack_taps(one, at, n), w2[...], 1, 1)
        s = sigmoid(v)
        slope[pl.ds(at - 5, n)] = cells(s * (1.0 + v * (1.0 - s)), n)
        put(two, at, n, jnp.where(grid_mask(at, n), cells(v * s, n), 0.0))

    sweep(5, 22, 11, conv_two)

    def conv_three(at, n):
        v = cells(dot(stack_taps(two, at, n), w3r[...]), n)
        value = skip * noisy[pl.ds(at - 3, n)] + out_coef * v
        den[pl.ds(at - 6, n)] = value.astype(bf16)
        delta = delta_coef * (value - resid[pl.ds(at - 3, n)])
        put(dlt, at, n, jnp.where(grid_mask(at, n), delta, 0.0))

    sweep(6, 20, 10, conv_three)

    def delta_two(at, n):
        picked = pick_taps(dlt, at, n)
        taps_d[pl.ds(at - 7, n)] = picked
        v = cells(dot(flat(picked), w3f[...], 1, 1), n) * slope[pl.ds(at - 5, n)]
        put(sdl, at, n, jnp.where(grid_mask(at, n), v, 0.0))

    sweep(7, 18, 6, delta_two)

    film_sum[...] = jnp.zeros((8, 128), f32)

    def delta_one(at, n):
        v = dot(stack_taps(sdl, at, n), w2t[...])
        a = flat(act[pl.ds(at - 4, n)])
        u = a * gain
        s = sigmoid(u)
        g = cells(v * (s * (1.0 + u * (1.0 - s))), n)
        g = flat(jnp.where(tile_mask(n), g, 0.0))
        film_sum[...] += jnp.sum((g * a).reshape(-1, 8, 128), axis=0)
        grad1[pl.ds(at - 8, n)] = cells(g * gain, n).astype(bf16)

    sweep(8, 16, 8, delta_one)

    inside = jnp.where(tile_mask(1), 1.0, 0.0).astype(bf16)
    own = slice(RIM, RIM + 16)
    d2 = flat(sdl[own, 1:PLANES + 1] * inside)
    g2 = dot(d2, stack_taps(one, RIM, 16), 0, 0)
    g1 = dot(flat(grad1[...]),
             jnp.concatenate([flat(taps_in[4:20]), flat(cond_taps[6:22])], axis=1), 0, 0)
    g3 = dot(flat(two[own, 1:PLANES + 1] * inside), flat(taps_d[1:17]), 0, 0)
    film = noise_coef * jnp.sum(film_sum[...], axis=0, keepdims=True)
    film = jnp.transpose(jnp.broadcast_to(film, (8, 128)))[:, 0:1]
    g3 = jnp.where(lax.broadcasted_iota(jnp.int32, (128, 128), 1) == FILM_LANE, film, g3)
    parts = [g2[:, k * 128:(k + 1) * 128] for k in range(9)] + [g1[:, :128], g1[:, 128:], g3]
    for p in range(6):
        pair = [part.reshape(16, 8, 128) for part in parts[2 * p:2 * p + 2]]
        out[:, p * 16:(p + 1) * 16, :] = jnp.concatenate(pair, axis=1).astype(bf16)

    fields = (lax.broadcasted_iota(jnp.int32, (16, 128), 0)
              == lax.broadcasted_iota(jnp.int32, (16, 128), 1)).astype(f32).astype(bf16)
    for i in range(16):
        turned = dot(fields, den[i + 2].reshape(WIN, 128), 1, 1).astype(bf16)
        den_rows[i * 16:(i + 1) * 16, :] = dot(turned, back[...])
    for c in range(6):
        left = den_rows[pl.ds(c, 16, stride=16), :]
        right = den_rows[pl.ds(c + 6, 16, stride=16), :]
        tile = jnp.where(lane < TW, left, right).astype(bf16)
        out[:, 96 + c * 16:96 + (c + 1) * 16, :] = jnp.broadcast_to(tile[None], (16, 16, 128))


def fold_kernel(parts, out):
    for p in range(6):
        total = jnp.sum(parts[:, p * 16:(p + 1) * 16, :].astype(f32), axis=0).astype(bf16)
        for q in range(8):
            out[q, p * 16:(p + 1) * 16, :] = total


def field_kernel(parts, out):
    for k in range(8):
        for c in range(6):
            a = parts[2 * k, 96 + c * 16:96 + (c + 1) * 16, :].astype(f32)
            b = parts[2 * k + 1, 96 + c * 16:96 + (c + 1) * 16, :].astype(f32)
            cols = slice(k * 128, (k + 1) * 128)
            out[c, :, cols] = jnp.concatenate([a[:, :TW], b[:, :TW]], axis=1).astype(bf16)
            out[c + 6, :, cols] = jnp.concatenate([a[:, TW:], b[:, TW:]], axis=1).astype(bf16)


def finish_kernel(parts, g1, g2, g3, film):
    def block(k):
        pair = jnp.sum(parts[:, (k // 2) * 16:(k // 2 + 1) * 16, :].astype(f32), axis=0)
        return pair[(k % 2) * 8:(k % 2) * 8 + 8]

    low, high, third = jnp.transpose(block(9)), jnp.transpose(block(10)), block(11)
    for a in range(3):
        for b in range(3):
            tap = 3 * a + b
            lanes = slice(tap * COUT, (tap + 1) * COUT)
            g2[a, b] = jnp.transpose(block(tap))
            g1[a, b, :COUT] = low[lanes]
            g1[a, b, COUT:] = high[lanes]
            g3[a, b] = third[:, (8 - tap) * COUT:(9 - tap) * COUT]
    film[...] = jnp.transpose(third)[FILM_LANE:FILM_LANE + 1]


VMEM = pl.BlockSpec(memory_space=pltpu.VMEM)
SMEM = pl.BlockSpec(memory_space=pltpu.SMEM)
ANY = pl.BlockSpec(memory_space=pl.ANY)


def kernel_call(body, ins, outs, scratch=(), limit=16, cost=None):
    return pl.pallas_call(
        body,
        in_specs=list(ins),
        out_specs=[VMEM] * len(outs),
        out_shape=[jax.ShapeDtypeStruct(shape, dtype) for shape, dtype in outs],
        scratch_shapes=list(scratch),
        compiler_params=pltpu.CompilerParams(vmem_limit_bytes=limit * MIB),
        cost_estimate=cost,
    )


def planes(rows, dtype, count=PLANES):
    return pltpu.VMEM((rows, count, SUB, 128), dtype)


def shards(condition, target, noise_draw, sigma_index, reg_first, reg_second, first_kernel,
           second_kernel, third_kernel, film_scale):
    sel_first, sel_low, order, back, spread, repeat = place_constants()
    own, last, leading, packed = kernel_call(
        pack_kernel, [ANY] * 3 + [VMEM] * 8,
        [((36, 16, 128), f32), ((36, 8, 128), f32), ((36, 8, 128), f32), ((16, 112, 128), bf16)],
        [pltpu.VMEM((3, COUT, 16, 256), f32), pltpu.SemaphoreType.DMA((3,))],
    )(condition, target, noise_draw, first_kernel, second_kernel, third_kernel, reg_first,
      reg_second, film_scale.reshape(1, 8), jnp.asarray(sel_first), jnp.asarray(sel_low))
    up = [(i, i + 1) for i in range(lax.axis_size("rows") - 1)]
    before = lax.ppermute(last, "rows", up)
    after = lax.ppermute(leading, "rows", [(j, i) for i, j in up])
    gathered = lax.all_to_all(packed, GROUP, 0, 0, tiled=True)
    cond_taps, target9, noise9 = kernel_call(
        prep_kernel, [ANY] * 3 + [VMEM] * 2,
        [((28, PLANES, SUB, 128), bf16), ((26, PLANES, SUB, 128), f32),
         ((26, PLANES, SUB, 128), f32)],
        [pltpu.VMEM((48, 32, 128), f32), planes(32, bf16, 7), pltpu.SemaphoreType.DMA((3,))],
        cost=pl.CostEstimate(flops=1 << 28, bytes_accessed=8 * MIB, transcendentals=0),
    )(own, before, after, jnp.asarray(order, bf16), jnp.asarray(spread, bf16))
    wide = [planes(32, bf16, 7) for _ in range(6)]
    out, = kernel_call(
        step_kernel, [SMEM] * 2 + [VMEM] * 6, [((16, 192, 128), bf16)],
        [pltpu.VMEM((128, 1152), bf16), pltpu.VMEM((1152, 128), bf16),
         pltpu.VMEM((128, 256), bf16), pltpu.VMEM((128, 128), bf16),
         pltpu.VMEM((128, 128), bf16), pltpu.VMEM((1152, 128), bf16),
         pltpu.VMEM((128, 128), bf16), pltpu.VMEM((1152, 128), bf16)]
        + wide
        + [planes(24, bf16), planes(18, bf16), planes(26, f32), planes(26, f32),
           planes(24, f32), planes(22, f32), planes(20, bf16), planes(16, bf16),
           pltpu.VMEM((8, 128), f32), pltpu.VMEM((256, 128), f32)],
        limit=48,
    )(sigma_index, jnp.asarray(coef_table()), cond_taps, target9, noise9, gathered,
      jnp.asarray(repeat, bf16), jnp.asarray(back, bf16))
    parts = lax.all_to_all(out, GROUP, 0, 0, tiled=True)
    folded, = kernel_call(fold_kernel, [VMEM], [((8, 96, 128), bf16)])(parts)
    denoised, = kernel_call(
        field_kernel, [VMEM], [((COUT, 16, NW), bf16)],
        cost=pl.CostEstimate(flops=1 << 26, bytes_accessed=2 * MIB, transcendentals=0),
    )(parts)
    sums = lax.all_to_all(folded, "rows", 0, 0, tiled=True)
    g1, g2, g3, film = kernel_call(
        finish_kernel, [VMEM],
        [((3, 3, 24, 8), f32), ((3, 3, 128, 8), f32), ((3, 3, 8, 12), f32), ((1, 8), f32)],
    )(sums)
    return denoised, g1, g2, g3, film.reshape(8)


def solution(mesh):
    return jax.shard_map(
        shards,
        mesh=mesh,
        in_specs=(
            P(None, "rows", None),
            P(None, "rows", None),
            P(None, "rows", None),
            P(),
            P(None, None, None, "chan"),
            P(None, None, "chan", None),
            P(None, None, None, GROUP),
            P(None, None, None, GROUP),
            P(None, None, GROUP, None),
            P(GROUP),
        ),
        out_specs=(
            P(None, "rows", None),
            P(None, None, None, GROUP),
            P(None, None, None, GROUP),
            P(None, None, GROUP, None),
            P(GROUP),
        ),
        check_vma=False,
    )
```

time: 855 us -> 92.8 us (0.11); the launches traced: 844 us -> 91.8 us
  matrix products: 255 us -> 0 us
  local copies, waits for them, and re-layouts: 251 us -> 14 us
  blocking collectives: 145 us -> 18.3 us
  waiting for transfers between devices: 111 us -> 16.4 us
  other arithmetic: 25.3 us -> 0 us
  Pallas kernels: 0 us -> 22.6 us
  starting transfers between devices: 38 us -> 19.1 us
  between operations: 19.2 us -> 1.4 us
    transpose x3 -> x0, matrix products: 184 us -> none  [kernel_grad(): return jnp.transpose(result_conv, (2, 3, 0, 1))]
    conv_general_dilated x28 -> x0, local copies, waits for them, and re-layouts: 147 us -> none  [conv_rows(): lax.conv_general_dilated(grid_field[None], kernel, (1, 1), ((0, 0), (1, 1...]
    psum x1 -> x0, waiting for transfers between devices: 111 us -> none  [shards(): out_full = lax.psum(out_part, ('section', 'chan'))]
    psum x2 -> x0, blocking collectives: 71.3 us -> none  [the longest x1 43.7 us: shards(): lax.psum((grad_parts[0], grad_parts[1], grad_parts[2], grad_parts[3]), 'r...]
    conv_general_dilated x7 -> x0, matrix products: 70.3 us -> none  [conv_rows(): lax.conv_general_dilated(grid_field[None], kernel, (1, 1), ((0, 0), (1, 1...]
    broadcast_in_dim x10 -> x0, local copies, waits for them, and re-layouts: 63.1 us -> none  [the longest x3 29 us: kernel_grad(): grid_field[:, None]]
    all_gather x3 -> x0, blocking collectives: 43.1 us -> none  [the longest x1 18.4 us: shards(): lax.all_gather(second_kernel, ('section', 'chan'), axis=3, tiled=True)]
    convert_element_type x4 -> x0, local copies, waits for them, and re-layouts: 35.6 us -> none  [the longest x2 21.4 us: shards(): grid_rows(jax.nn.silu(first_all * gain_all), slab_start - 1, total_rows)]
  transfers between devices with their start and end apart: 12 -> 4, of which waited for: 1 -> 3; matrix products, arithmetic and copies ran while one was open for 30% -> 0% of each run, Pallas kernels for 0% -> 7%
where the time goes in v1:
time: 92.8 us; the launch traced here: 91.8 us
  Pallas kernels  22.6 us (24%)
  starting transfers between devices  19.1 us (21%)
  blocking collectives  18.3 us (20%)
  waiting for transfers between devices  16.4 us (18%)
  local copies, waits for them, and re-layouts  14 us (15%)
  between operations  1.4 us (2%)
    all_to_all x1, blocking collectives, shards(): parts = lax.all_to_all(out, GROUP, 0, 0, tiled=True)  18.3 us
    unnamed x36, local copies, waits for them, and re-layouts  14 us
    pallas_call x1, Pallas kernels, shards(): kernel_call(step_kernel, [SMEM] * 2 + [VMEM] * 6, [((16, 192, 128), bf16)...  13.3 us
    all_to_all x1, waiting for transfers between devices, shards(): sums = lax.all_to_all(folded, 'rows', 0, 0, tiled=True)  7.53 us
    all_to_all x1, starting transfers between devices, shards(): sums = lax.all_to_all(folded, 'rows', 0, 0, tiled=True)  6.63 us
    all_to_all x1, starting transfers between devices, shards(): gathered = lax.all_to_all(packed, GROUP, 0, 0, tiled=True)  6.56 us
    ppermute x1, waiting for transfers between devices, shards(): after = lax.ppermute(leading, 'rows', [(j, i) for i, j in up])  6.34 us
    pallas_call x1, Pallas kernels, shards(): kernel_call(prep_kernel, [ANY] * 3 + [VMEM] * 2, [((28, PLANES, SUB, 128)...  5.3 us
  transfers between devices with their start and end apart: 4, of which 3 were waited for; matrix products, arithmetic and copies ran while one was open for 0% of the time, Pallas kernels for 7%

profile of v1, /device:TPU:0, one launch (start us, length us, event | category | flops | bytes accessed | tf_op | source)
XLA Modules:
  0.0 91.8 jit_solution(8925787365411743989)
XLA Ops:
  0.6 0.8 copy.22.w1
  1.4 0.9 %copy.23.w2 = bf16[3,3,128,8]{3,2,1,0:T(8,128)(2,1)S(1)} copy(bf16[3,3,128,8]{2,3,1,0:T(8,128)(2,1)} %param.24) | data formatting | bytes 36864 | tf_op args[7]
  2.4 0.0 copy-start
  2.4 1.1 %copy-done = f32[12,16,1024]{2,1,0:T(8,128)S(1)} copy-done((f32[12,16,1024]{2,1,0:T(8,128)S(1)}, f32[12,16,1024]{2,1,0:T(8,128)}, u32[]{:S(2)}) %copy-start) | copy-done | bytes 786456
  3.5 1.1 %copy-done.1 = f32[12,16,1024]{2,1,0:T(8,128)S(1)} copy-done((f32[12,16,1024]{2,1,0:T(8,128)S(1)}, f32[12,16,1024]{2,1,0:T(8,128)}, u32[]{:S(2)}) %copy-start.1) | copy-done | bytes 786456
  4.7 1.1 %copy-done.2 = f32[12,16,1024]{2,1,0:T(8,128)S(1)} copy-done((f32[12,16,1024]{2,1,0:T(8,128)S(1)}, f32[12,16,1024]{2,1,0:T(8,128)}, u32[]{:S(2)}) %copy-start.2) | copy-done | bytes 786456
  5.8 0.9 %copy-done.4 = f32[9,24,256]{2,1,0:T(8,128)S(1)} copy-done((f32[9,24,256]{2,1,0:T(8,128)S(1)}, f32[9,24,256]{2,1,0:T(8,128)}, u32[]{:S(2)}) %copy-start.4) | copy-done | bytes 221208
  6.7 0.9 copy-done.5
  7.6 0.8 copy-done.6
  8.4 0.8 copy-done.7
  9.2 0.7 copy-done.9
  9.9 0.7 copy-done.11
  10.5 1.5 %shard_map.200 = (f32[36,16,128]{2,1,0:T(8,128)S(1)}, f32[36,8,128]{2,1,0:T(8,128)S(1)}, f32[36,8,128]{2,1,0:T(8,128)S(1)}, bf16[16,112,128]{2,1,0:T(8,128)(2,1)}) custom-call(f32[12,16,1024]{2,1,0:T(8,128)S(1)} %copy-done, f32[12,16,1024]{2,1,0:T(8,128)S(1)} %copy-done.1, f32[12,16,1024]{2,1,0:T(8,128)S(1)} %copy-done.2, ...), custom_call_target="tpu_custom_call" | custom-call | tf_op jit(solution)/shard_map/pallas_call | solution.py:412
  12.0 0.0 copy-start.12
  12.0 0.7 copy-done.12
  12.7 6.6 %all-to-all-start = ((bf16[16,112,128]{2,1,0:T(8,128)(2,1)}), bf16[16,112,128]{2,1,0:T(8,128)(2,1)S(1)}, u32[]{:S(2)}, u32[]{:S(2)}) async-start(bf16[16,112,128]{2,1,0:T(8,128)(2,1)} %get-tuple-element.22), calls=%async_computation | async-start | bytes 917504 | tf_op jit(solution)/shard_map/all_to_all | solution.py:421
  19.3 4.6 %collective-permute-start = (f32[36,8,128]{2,1,0:T(8,128)S(1)}, f32[36,8,128]{2,1,0:T(8,128)S(1)}, u32[]{:S(2)}, u32[]{:S(2)}) collective-permute-start(f32[36,8,128]{2,1,0:T(8,128)S(1)} %get-tuple-element.17), channel_id=1, source_target_pairs={{0,8},{8,16},{16,24},{24,32},{32,40},{40,48},{48,56},{1,9},{9,17},... | collective-permute-start | bytes 442376 | tf_op jit(solution)/shard_map/ppermute | solution.py:419
  23.9 1.3 %collective-permute-start.1 = (f32[36,8,128]{2,1,0:T(8,128)S(1)}, f32[36,8,128]{2,1,0:T(8,128)S(1)}, u32[]{:S(2)}, u32[]{:S(2)}) collective-permute-start(f32[36,8,128]{2,1,0:T(8,128)S(1)} %get-tuple-element.18), channel_id=1, source_target_pairs={{8,0},{16,8},{24,16},{32,24},{40,32},{48,40},{56,48},{9,1},{17,9},... | collective-permute-start | bytes 442376 | tf_op jit(solution)/shard_map/ppermute | solution.py:420
  25.9 2.5 %collective-permute-done.before = f32[36,8,128]{2,1,0:T(8,128)S(1)} collective-permute-done((f32[36,8,128]{2,1,0:T(8,128)S(1)}, f32[36,8,128]{2,1,0:T(8,128)S(1)}, u32[]{:S(2)}, u32[]{:S(2)}) %collective-permute-start) | collective-permute-done | bytes 147488 | tf_op jit(solution)/shard_map/ppermute | solution.py:419
  28.4 6.3 %collective-permute-done.1.after = f32[36,8,128]{2,1,0:T(8,128)S(1)} collective-permute-done((f32[36,8,128]{2,1,0:T(8,128)S(1)}, f32[36,8,128]{2,1,0:T(8,128)S(1)}, u32[]{:S(2)}, u32[]{:S(2)}) %collective-permute-start.1) | collective-permute-done | bytes 147488 | tf_op jit(solution)/shard_map/ppermute | solution.py:420
  34.7 1.0 %copy-done.13 = f32[36,16,128]{2,1,0:T(8,128)S(1)} copy-done((f32[36,16,128]{2,1,0:T(8,128)S(1)}, f32[36,16,128]{2,1,0:T(8,128)}, u32[]{:S(2)}) %copy-start.13) | copy-done | bytes 294936
  35.7 0.9 copy-done.14
  36.6 5.3 %shard_map.201 = (bf16[28,5,16,128]{3,2,1,0:T(8,128)(2,1)S(1)}, f32[26,5,16,128]{3,2,1,0:T(8,128)S(1)}, f32[26,5,16,128]{3,2,1,0:T(8,128)S(1)}) custom-call(f32[36,16,128]{2,1,0:T(8,128)S(1)} %copy-done.13, f32[36,8,128]{2,1,0:T(8,128)S(1)} %collective-permute-done.before, f32[36,8,128]{2,1,0:T(8,128)S(1)} %collective-permute-done.1.after, ...), custom_call_target="tpu_custom_call" | custom-call | flops 268435456 | bytes 8388608 | tf_op jit(solution)/shard_map/pallas_call | solution.py:422
  41.9 13.3 %shard_map.202 = bf16[16,192,128]{2,1,0:T(8,128)(2,1)S(1)} custom-call(s32[1]{0:T(128)S(6)} %copy.26.index, f32[32,8]{1,0:T(8,128)S(1)} %copy-done.10, bf16[28,5,16,128]{3,2,1,0:T(8,128)(2,1)S(1)} %get-tuple-element.19.cond_taps, f32[26,5,16,128]{3,2,1,0:T(8,128)S(1)} %get-tuple-element.20.target9, f32[26,5,16,128]{3,2,1,0:T(8,128)S(1)} %get-tuple-element.21.noise9, ...), custom_call_target="tpu_custom_call" | custom-call | tf_op jit(solution)/shard_map/pallas_call | solution.py:430
  55.2 18.3 %all_to_all.15.parts = bf16[16,192,128]{2,1,0:T(8,128)(2,1)S(1)} all-to-all(bf16[16,192,128]{2,1,0:T(8,128)(2,1)S(1)} %shard_map.202), channel_id=1, replica_groups=mesh['section'=2,'rows'=8,'chan'=8] {'section','chan'}, dimensions={0} | all-to-all | bytes 1572864 | tf_op jit(solution)/shard_map/all_to_all | solution.py:443
  73.6 0.7 shard_map.204
  74.3 6.6 %all-to-all-start.2 = ((bf16[8,96,128]{2,1,0:T(8,128)(2,1)}), bf16[8,96,128]{2,1,0:T(8,128)(2,1)S(1)}, u32[]{:S(2)}, u32[]{:S(2)}) async-start(bf16[8,96,128]{2,1,0:T(8,128)(2,1)} %shard_map.204), calls=%async_computation.2 | async-start | bytes 393216 | tf_op jit(solution)/shard_map/all_to_all | solution.py:449
  81.0 0.9 %shard_map.203 = bf16[12,16,1024]{2,1,0:T(8,128)(2,1)} custom-call(bf16[16,192,128]{2,1,0:T(8,128)(2,1)S(1)} %all_to_all.15.parts), custom_call_target="tpu_custom_call" | custom-call | flops 67108864 | bytes 2097152 | tf_op jit(solution)/shard_map/pallas_call | solution.py:445
  81.9 7.5 %all-to-all-done.2.parts = bf16[8,96,128]{2,1,0:T(8,128)(2,1)S(1)} async-done(((bf16[8,96,128]{2,1,0:T(8,128)(2,1)}), bf16[8,96,128]{2,1,0:T(8,128)(2,1)S(1)}, u32[]{:S(2)}, u32[]{:S(2)}) %all-to-all-start.2) | async-done | bytes 196640 | tf_op jit(solution)/shard_map/all_to_all | solution.py:449
  89.4 0.9 shard_map.205
  90.3 0.7 copy.24
  91.0 0.8 copy.25
  (19 shorter events, 0.0 us)
Async XLA Ops:
  2.4 1.1 %copy-start = (f32[12,16,1024]{2,1,0:T(8,128)S(1)}, f32[12,16,1024]{2,1,0:T(8,128)}, u32[]{:S(2)}) copy-start(f32[12,16,1024]{2,1,0:T(8,128)} %cond.1) | copy-start | bytes 2359300
  3.5 1.1 %copy-start.1 = (f32[12,16,1024]{2,1,0:T(8,128)S(1)}, f32[12,16,1024]{2,1,0:T(8,128)}, u32[]{:S(2)}) copy-start(f32[12,16,1024]{2,1,0:T(8,128)} %target.1) | copy-start | bytes 2359300
  4.7 1.1 %copy-start.2 = (f32[12,16,1024]{2,1,0:T(8,128)S(1)}, f32[12,16,1024]{2,1,0:T(8,128)}, u32[]{:S(2)}) copy-start(f32[12,16,1024]{2,1,0:T(8,128)} %noise.1) | copy-start | bytes 2359300
  5.8 0.9 %copy-start.4 = (f32[9,24,256]{2,1,0:T(8,128)S(1)}, f32[9,24,256]{2,1,0:T(8,128)}, u32[]{:S(2)}) copy-start(f32[9,24,256]{2,1,0:T(8,128)} %constant.14.clone.sel_first) | copy-start | bytes 663556
  6.7 0.9 copy-start.5
  7.6 0.8 copy-start.6
  8.4 0.8 copy-start.7
  9.2 0.7 copy-start.9
  9.9 0.7 copy-start.11
  10.5 24.2 %copy-start.15 = (bf16[80,128]{1,0:T(8,128)(2,1)S(1)}, bf16[80,128]{1,0:T(8,128)(2,1)}, u32[]{:S(2)}) copy-start(bf16[80,128]{1,0:T(8,128)(2,1)} %constant.16.clone.order) | copy-start | bytes 61444
  12.0 0.7 copy-start.12
  12.7 29.2 %copy-start.3 = (bf16[128,1280]{1,0:T(8,128)(2,1)S(1)}, bf16[128,1280]{1,0:T(8,128)(2,1)}, u32[]{:S(2)}) copy-start(bf16[128,1280]{1,0:T(8,128)(2,1)} %constant.19.clone.repeat) | copy-start | bytes 983044
  12.7 29.2 %copy-start.8 = (bf16[80,128]{1,0:T(8,128)(2,1)S(1)}, bf16[80,128]{1,0:T(8,128)(2,1)}, u32[]{:S(2)}) copy-start(bf16[80,128]{1,0:T(8,128)(2,1)} %constant.20.clone.back) | copy-start | bytes 61444
  12.7 29.2 %copy-start.10 = (f32[32,8]{1,0:T(8,128)S(1)}, f32[32,8]{1,0:T(8,128)}, u32[]{:S(2)}) copy-start(f32[32,8]{1,0:T(8,128)} %constant.18.clone.table) | copy-start | bytes 3076
  12.7 29.2 %all-to-all-start = ((bf16[16,112,128]{2,1,0:T(8,128)(2,1)}), bf16[16,112,128]{2,1,0:T(8,128)(2,1)S(1)}, u32[]{:S(2)}, u32[]{:S(2)}) async-start(bf16[16,112,128]{2,1,0:T(8,128)(2,1)} %get-tuple-element.22), calls=%async_computation | async-start | bytes 917504 | tf_op jit(solution)/shard_map/all_to_all | solution.py:421
  19.3 9.1 %collective-permute-start = (f32[36,8,128]{2,1,0:T(8,128)S(1)}, f32[36,8,128]{2,1,0:T(8,128)S(1)}, u32[]{:S(2)}, u32[]{:S(2)}) collective-permute-start(f32[36,8,128]{2,1,0:T(8,128)S(1)} %get-tuple-element.17), channel_id=1, source_target_pairs={{0,8},{8,16},{16,24},{24,32},{32,40},{40,48},{48,56},{1,9},{9,17},... | collective-permute-start | bytes 442376 | tf_op jit(solution)/shard_map/ppermute | solution.py:419
  23.9 10.8 %collective-permute-start.1 = (f32[36,8,128]{2,1,0:T(8,128)S(1)}, f32[36,8,128]{2,1,0:T(8,128)S(1)}, u32[]{:S(2)}, u32[]{:S(2)}) collective-permute-start(f32[36,8,128]{2,1,0:T(8,128)S(1)} %get-tuple-element.18), channel_id=1, source_target_pairs={{8,0},{16,8},{24,16},{32,24},{40,32},{48,40},{56,48},{9,1},{17,9},... | collective-permute-start | bytes 442376 | tf_op jit(solution)/shard_map/ppermute | solution.py:420
  34.7 1.0 %copy-start.13 = (f32[36,16,128]{2,1,0:T(8,128)S(1)}, f32[36,16,128]{2,1,0:T(8,128)}, u32[]{:S(2)}) copy-start(f32[36,16,128]{2,1,0:T(8,128)} %copy-done.12) | copy-start | bytes 884740
  35.7 0.9 copy-start.14
  74.3 15.1 %all-to-all-start.2 = ((bf16[8,96,128]{2,1,0:T(8,128)(2,1)}), bf16[8,96,128]{2,1,0:T(8,128)(2,1)S(1)}, u32[]{:S(2)}, u32[]{:S(2)}) async-start(bf16[8,96,128]{2,1,0:T(8,128)(2,1)} %shard_map.204), calls=%async_computation.2 | async-start | bytes 393216 | tf_op jit(solution)/shard_map/all_to_all | solution.py:449

commit v2 on v1

--- a/solution.py
+++ b/solution.py
@@ -43,13 +43,6 @@
 
 
 def place_constants():
-    sel_first = np.zeros((TAPS, 24, 256), np.float32)
-    sel_low = np.zeros((TAPS, COUT, 128), np.float32)
-    for tap in range(TAPS):
-        for c in range(COUT):
-            sel_first[tap, c, tap * COUT + c] = 1
-            sel_first[tap, COUT + c, 128 + tap * COUT + c] = 1
-            sel_low[tap, c, tap * COUT + c] = 1
     order = np.zeros((WIN, 128), np.float32)
     back = np.zeros((WIN, 128), np.float32)
     for t in range(PLANES):
@@ -70,7 +63,7 @@
             for tap in range(TAPS):
                 repeat[tap * COUT + c, tap * 128 + g * COUT + c] = 1
             repeat[(8 - g) * COUT + c, 9 * 128 + g * COUT + c] = 1
-    return sel_first, sel_low, order, back, spread, repeat
+    return order, back, spread, repeat
 
 
 def dot(a, b, ca=1, cb=0):
@@ -85,54 +78,80 @@
     return lax.axis_index("section") * lax.axis_size("chan") + lax.axis_index("chan")
 
 
-def pack_kernel(cond, target, noise, w1, w2, w3, r1, r2, film, sel_first, sel_low,
-                own, last, leading, packed, scr, sems):
+def window_place():
     start = member() * TW - RIM
     base = jnp.clip((start + 128) // 128 * 128 - 128, 0, NW - 256)
-    base = pl.multiple_of(base, 128)
-    copies = []
-    for k, src in enumerate((target, noise, cond)):
-        copy = pltpu.make_async_copy(src.at[:, :, pl.ds(base, 256)], scr.at[k], sems.at[k])
-        copy.start()
-        copies.append(copy)
+    return start, pl.multiple_of(base, 128)
+
+
+def window_copy(src, dst, sem):
+    copy = pltpu.make_async_copy(src.at[:, :, pl.ds(window_place()[1], 256)], dst, sem)
+    copy.start()
+    return copy
+
+
+def window(wide):
+    start, base = window_place()
+    rows = pltpu.roll(wide.reshape(COUT * 16, 256), lax.rem(512 - (start - base), 256), 1)
+    rows = rows[:, :128]
+    col = start + lax.broadcasted_iota(jnp.int32, rows.shape, 1)
+    return jnp.where((col >= 0) & (col < NW), rows, 0.0).reshape(COUT, 16, 128)
+
+
+def pack_kernel(cond, target, noise, w1_any, w2_any, w3_any, r1_any, r2_any, film_any,
+                last, leading, packed, scr, w1, w2, w3, r1, r2, film, sems):
+    small = []
+    for k, (src, dst) in enumerate(((w2_any, w2), (w1_any, w1), (w3_any, w3), (r1_any, r1),
+                                    (r2_any, r2), (film_any, film))):
+        small.append(pltpu.make_async_copy(src, dst, sems.at[k]))
+        small[-1].start()
+    copies = [window_copy(src, scr.at[k], sems.at[6 + k])
+              for k, src in enumerate((target, noise, cond))]
     half = lax.axis_index("section") == 0
     eye = (lax.broadcasted_iota(jnp.int32, (8, 8), 0)
            == lax.broadcasted_iota(jnp.int32, (8, 8), 1)).astype(f32)
+    for k, copy in enumerate(copies):
+        copy.wait()
+        moved = window(scr[k])
+        last[k * COUT:(k + 1) * COUT] = moved[:, 8:]
+        leading[k * COUT:(k + 1) * COUT] = moved[:, :8]
+    for copy in small:
+        copy.wait()
+
+    def place(n, at):
+        lane = lax.broadcasted_iota(jnp.int32, (n, 128), 1)
+        row = lax.broadcasted_iota(jnp.int32, (n, 128), 0)
+        return jnp.where((lane - row == at) & (row < COUT), 1.0, 0.0)
+
+    first_in = jnp.zeros((8, 128), f32)
+    first_cond = jnp.zeros((8, 128), f32)
+    third = jnp.zeros((8, 128), f32)
+    reg_a = jnp.zeros((16, 128), f32)
+    reg_b = jnp.zeros((16, 128), f32)
     blocks = []
     for a in range(3):
         for b in range(3):
-            blocks.append(dot(eye, w2[a, b].astype(f32), 1, 1))
-    first = jnp.zeros((8, 256), f32)
-    third = jnp.zeros((8, 128), f32)
-    reg_a = jnp.zeros((16, 128), f32)
-    reg_b = jnp.zeros((16, 128), f32)
-    for a in range(3):
-        for b in range(3):
             tap = 3 * a + b
-            first += dot(w1[a, b].astype(f32), sel_first[tap], 0, 0)
-            third += dot(w3[a, b].astype(f32), sel_low[tap])
-            reg_a += dot(r1[a, b].astype(f32), sel_low[tap], 0, 0)
-            reg_b += dot(r2[a, b].astype(f32), sel_low[tap])
+            low = place(COUT, tap * COUT)
+            lane = lax.broadcasted_iota(jnp.int32, (24, 128), 1)
+            row = lax.broadcasted_iota(jnp.int32, (24, 128), 0)
+            low_in = jnp.where((lane - row == tap * COUT) & (row < COUT), 1.0, 0.0)
+            low_cond = jnp.where((lane - row == (tap - 1) * COUT) & (row >= COUT), 1.0, 0.0)
+            blocks.append(w2[a, b].astype(f32))
+            first_in += dot(w1[a, b].astype(f32), low_in)
+            first_cond += dot(w1[a, b].astype(f32), low_cond)
+            third += dot(w3[a, b].astype(f32), low)
+            reg_a += dot(r1[a, b].astype(f32), low, 0, 0)
+            reg_b += dot(r2[a, b].astype(f32), low)
     lane = lax.broadcasted_iota(jnp.int32, (8, 128), 1)
     film_col = jnp.sum(eye * film[...].astype(f32), axis=1, keepdims=True)
     third = jnp.where(lane == FILM_LANE, film_col, third)
-    blocks += [first[:, :128], first[:, 128:], third,
+    blocks += [first_in, first_cond, third,
                jnp.where(half, reg_a[:8], reg_a[8:]), jnp.where(half, reg_b[:8], reg_b[8:])]
     for p in range(7):
         pair = jnp.concatenate(blocks[2 * p:2 * p + 2], axis=0).astype(bf16)
         for q in range(16):
             packed[q, p * 16:(p + 1) * 16, :] = pair
-    offset = start - base
-    shift = lax.rem(512 - offset, 256)
-    for k, copy in enumerate(copies):
-        copy.wait()
-        rows = scr[k].reshape(COUT * 16, 256)
-        moved = pltpu.roll(rows, shift, 1)[:, :128]
-        col = start + lax.broadcasted_iota(jnp.int32, moved.shape, 1)
-        moved = jnp.where((col >= 0) & (col < NW), moved, 0.0).reshape(COUT, 16, 128)
-        own[k * COUT:(k + 1) * COUT] = moved
-        last[k * COUT:(k + 1) * COUT] = moved[:, 8:]
-        leading[k * COUT:(k + 1) * COUT] = moved[:, :8]
 
 
 def put(ref, at, n, value):
@@ -161,16 +180,23 @@
     return total
 
 
-def prep_kernel(own, before, after, order, spread, cond_taps, target9, noise9, scr, cond9, sems):
-    copies = [
-        pltpu.make_async_copy(before, scr.at[0:36, 0:8, :], sems.at[0]),
-        pltpu.make_async_copy(own, scr.at[0:36, 8:24, :], sems.at[1]),
-        pltpu.make_async_copy(after, scr.at[0:36, 24:32, :], sems.at[2]),
+def prep_kernel(cond, target, noise, before, after, order_any, spread_any,
+                cond_taps, target9, noise9, scr, wide, cond9, order, spread, sems):
+    copies = [window_copy(src, wide.at[k], sems.at[k])
+              for k, src in enumerate((target, noise, cond))]
+    others = [
+        pltpu.make_async_copy(before, scr.at[0:36, 0:8, :], sems.at[3]),
+        pltpu.make_async_copy(after, scr.at[0:36, 24:32, :], sems.at[4]),
+        pltpu.make_async_copy(order_any, order, sems.at[5]),
+        pltpu.make_async_copy(spread_any, spread, sems.at[6]),
     ]
-    for copy in copies:
+    for copy in others:
         copy.start()
     scr[36:48] = jnp.zeros((12, 32, 128), f32)
-    for copy in copies:
+    for k, copy in enumerate(copies):
+        copy.wait()
+        scr[k * COUT:(k + 1) * COUT, 8:24] = window(wide[k])
+    for copy in others:
         copy.wait()
     flat = scr.reshape(48 * 32, 128)
 
@@ -198,10 +224,16 @@
         cond_taps[pl.ds(at - 2, 4)] = pick_taps(cond9, at, 4)
 
 
-def step_kernel(index, table, cond_taps, target9, noise9, gathered, repeat, back, out,
-                w2, w2t, w1, w3, w3f, w3r, r1, r2,
+def step_kernel(index, table, cond_any, target_any, noise_any, gathered_any, repeat_any, back_any,
+                out, cond_taps, target9, noise9, gathered, repeat, back, sems, w2, w2t, w1, w3, w3f, w3r, r1, r2,
                 hid, inp, one, two, dlt, sdl, taps_in, taps_d, resid, noisy, act, slope,
                 den, grad1, film_sum, den_rows):
+    copies = []
+    for k, (src, dst) in enumerate(((gathered_any, gathered), (repeat_any, repeat),
+                                    (cond_any, cond_taps), (target_any, target9),
+                                    (noise_any, noise9), (back_any, back))):
+        copies.append(pltpu.make_async_copy(src, dst, sems.at[k]))
+        copies[-1].start()
     level = index[0]
     sigma, skip, out_coef = table[level, 0], table[level, 1], table[level, 2]
     in_coef, noise_coef, delta_coef = table[level, 3], table[level, 4], table[level, 5]
@@ -213,6 +245,7 @@
         low = (k % 2) * 8
         return pair[:, low:low + 8].reshape(128, 128).astype(bf16)
 
+    copies[0].wait()
     for tap in range(TAPS):
         part = block(tap)
         w2[:, tap * 128:(tap + 1) * 128] = part
@@ -221,6 +254,7 @@
     w1[:, 128:] = block(10)
     w3[...] = block(11)
     r1[...] = block(12)
+    copies[1].wait()
     wide = dot(w3[...], repeat[...]).astype(bf16)
     for tap in range(TAPS):
         w3r[tap * 128:(tap + 1) * 128, :] = wide[:, tap * 128:(tap + 1) * 128]
@@ -261,6 +295,7 @@
         v = cells(v * sigmoid(v), n)
         put(hid, at, n, jnp.where(grid_mask(at, n), v, 0.0))
 
+    copies[2].wait()
     sweep(2, 28, 7, reg_one)
 
     def reg_two(at, n):
@@ -271,6 +306,8 @@
         noisy[pl.ds(at - 3, n)] = noised
         put(inp, at, n, jnp.where(grid_mask(at, n), in_coef * noised, 0.0))
 
+    for copy in copies[3:]:
+        copy.wait()
     sweep(3, 26, 13, reg_two)
 
     def conv_one(at, n):
@@ -373,14 +410,14 @@
         pair = jnp.sum(parts[:, (k // 2) * 16:(k // 2 + 1) * 16, :].astype(f32), axis=0)
         return pair[(k % 2) * 8:(k % 2) * 8 + 8]
 
-    low, high, third = jnp.transpose(block(9)), jnp.transpose(block(10)), block(11)
+    low, high, third = block(9), block(10), block(11)
     for a in range(3):
         for b in range(3):
             tap = 3 * a + b
             lanes = slice(tap * COUT, (tap + 1) * COUT)
-            g2[a, b] = jnp.transpose(block(tap))
-            g1[a, b, :COUT] = low[lanes]
-            g1[a, b, COUT:] = high[lanes]
+            g2[a, b] = block(tap)
+            g1[a, b, :, :COUT] = low[:, lanes]
+            g1[a, b, :, COUT:] = high[:, lanes]
             g3[a, b] = third[:, (8 - tap) * COUT:(9 - tap) * COUT]
     film[...] = jnp.transpose(third)[FILM_LANE:FILM_LANE + 1]
 
@@ -408,28 +445,38 @@
 
 def shards(condition, target, noise_draw, sigma_index, reg_first, reg_second, first_kernel,
            second_kernel, third_kernel, film_scale):
-    sel_first, sel_low, order, back, spread, repeat = place_constants()
-    own, last, leading, packed = kernel_call(
-        pack_kernel, [ANY] * 3 + [VMEM] * 8,
-        [((36, 16, 128), f32), ((36, 8, 128), f32), ((36, 8, 128), f32), ((16, 112, 128), bf16)],
-        [pltpu.VMEM((3, COUT, 16, 256), f32), pltpu.SemaphoreType.DMA((3,))],
-    )(condition, target, noise_draw, first_kernel, second_kernel, third_kernel, reg_first,
-      reg_second, film_scale.reshape(1, 8), jnp.asarray(sel_first), jnp.asarray(sel_low))
+    order, back, spread, repeat = place_constants()
+    last, leading, packed = kernel_call(
+        pack_kernel, [ANY] * 9,
+        [((36, 8, 128), f32), ((36, 8, 128), f32), ((16, 112, 128), bf16)],
+        [pltpu.VMEM((3, COUT, 16, 256), f32), pltpu.VMEM((3, 3, 8, 24), bf16),
+         pltpu.VMEM((3, 3, 8, 128), bf16), pltpu.VMEM((3, 3, 8, 12), bf16),
+         pltpu.VMEM((3, 3, 12, 16), bf16), pltpu.VMEM((3, 3, 16, 12), bf16),
+         pltpu.VMEM((1, 8), bf16), pltpu.SemaphoreType.DMA((9,))],
+        limit=60,
+    )(condition, target, noise_draw, jnp.swapaxes(first_kernel, 2, 3),
+      jnp.swapaxes(second_kernel, 2, 3), third_kernel, reg_first, reg_second,
+      film_scale.reshape(1, 8))
     up = [(i, i + 1) for i in range(lax.axis_size("rows") - 1)]
     before = lax.ppermute(last, "rows", up)
     after = lax.ppermute(leading, "rows", [(j, i) for i, j in up])
     gathered = lax.all_to_all(packed, GROUP, 0, 0, tiled=True)
     cond_taps, target9, noise9 = kernel_call(
-        prep_kernel, [ANY] * 3 + [VMEM] * 2,
+        prep_kernel, [ANY] * 7,
         [((28, PLANES, SUB, 128), bf16), ((26, PLANES, SUB, 128), f32),
          ((26, PLANES, SUB, 128), f32)],
-        [pltpu.VMEM((48, 32, 128), f32), planes(32, bf16, 7), pltpu.SemaphoreType.DMA((3,))],
-        cost=pl.CostEstimate(flops=1 << 28, bytes_accessed=8 * MIB, transcendentals=0),
-    )(own, before, after, jnp.asarray(order, bf16), jnp.asarray(spread, bf16))
+        [pltpu.VMEM((48, 32, 128), f32), pltpu.VMEM((3, COUT, 16, 256), f32),
+         planes(32, bf16, 7), pltpu.VMEM((WIN, 128), bf16), pltpu.VMEM((128, 384), bf16),
+         pltpu.SemaphoreType.DMA((7,))],
+        limit=60,
+        cost=pl.CostEstimate(flops=1 << 32, bytes_accessed=8 * MIB, transcendentals=0),
+    )(condition, target, noise_draw, before, after, jnp.asarray(order, bf16), jnp.asarray(spread, bf16))
     wide = [planes(32, bf16, 7) for _ in range(6)]
     out, = kernel_call(
-        step_kernel, [SMEM] * 2 + [VMEM] * 6, [((16, 192, 128), bf16)],
-        [pltpu.VMEM((128, 1152), bf16), pltpu.VMEM((1152, 128), bf16),
+        step_kernel, [SMEM] * 2 + [ANY] * 6, [((16, 192, 128), bf16)],
+        [planes(28, bf16), planes(26, f32), planes(26, f32), pltpu.VMEM((16, 112, 128), bf16),
+         pltpu.VMEM((128, 1280), bf16), pltpu.VMEM((WIN, 128), bf16),
+         pltpu.SemaphoreType.DMA((6,)), pltpu.VMEM((128, 1152), bf16), pltpu.VMEM((1152, 128), bf16),
          pltpu.VMEM((128, 256), bf16), pltpu.VMEM((128, 128), bf16),
          pltpu.VMEM((128, 128), bf16), pltpu.VMEM((1152, 128), bf16),
          pltpu.VMEM((128, 128), bf16), pltpu.VMEM((1152, 128), bf16)]
@@ -437,7 +484,7 @@
         + [planes(24, bf16), planes(18, bf16), planes(26, f32), planes(26, f32),
            planes(24, f32), planes(22, f32), planes(20, bf16), planes(16, bf16),
            pltpu.VMEM((8, 128), f32), pltpu.VMEM((256, 128), f32)],
-        limit=48,
+        limit=60,
     )(sigma_index, jnp.asarray(coef_table()), cond_taps, target9, noise9, gathered,
       jnp.asarray(repeat, bf16), jnp.asarray(back, bf16))
     parts = lax.all_to_all(out, GROUP, 0, 0, tiled=True)
@@ -449,9 +496,9 @@
     sums = lax.all_to_all(folded, "rows", 0, 0, tiled=True)
     g1, g2, g3, film = kernel_call(
         finish_kernel, [VMEM],
-        [((3, 3, 24, 8), f32), ((3, 3, 128, 8), f32), ((3, 3, 8, 12), f32), ((1, 8), f32)],
+        [((3, 3, 8, 24), f32), ((3, 3, 8, 128), f32), ((3, 3, 8, 12), f32), ((1, 8), f32)],
     )(sums)
-    return denoised, g1, g2, g3, film.reshape(8)
+    return denoised, jnp.swapaxes(g1, 2, 3), jnp.swapaxes(g2, 2, 3), g3, film.reshape(8)
 
 
 def solution(mesh):

time: 92.8 us -> 79.8 us (0.86)
  local copies, waits for them, and re-layouts: 14 us -> 1.45 us
  waiting for transfers between devices: 16.4 us -> 9.01 us
  Pallas kernels: 22.6 us -> 28.4 us
  blocking collectives: 18.3 us -> 19.5 us
    unnamed x36 -> x6, local copies, waits for them, and re-layouts: 14 us -> 1.45 us
    pallas_call x4, Pallas kernels: 21 us -> 26.7 us  [the longest x1 15.5 us: shards(): kernel_call(step_kernel, [SMEM] * 2 + [ANY] * 6, [((16, 192, 128), bf16)]...]
    ppermute x1, waiting for transfers between devices: 6.34 us -> 1.48 us  [shards(): after = lax.ppermute(leading, 'rows', [(j, i) for i, j in up])]
    ppermute x1, waiting for transfers between devices: 2.48 us -> 0.01 us  [shards(): before = lax.ppermute(last, 'rows', up)]
    all_to_all x1, blocking collectives: 18.3 us -> 19.5 us  [shards(): parts = lax.all_to_all(out, GROUP, 0, 0, tiled=True)]
    all_to_all x1, starting transfers between devices: 6.56 us -> 5.46 us  [shards(): gathered = lax.all_to_all(packed, GROUP, 0, 0, tiled=True)]
    all_to_all x1, starting transfers between devices: 6.63 us -> 7.68 us  [shards(): sums = lax.all_to_all(folded, 'rows', 0, 0, tiled=True)]
  transfers between devices with their start and end apart: 4 -> 4, of which waited for: 3 -> 2; matrix products, arithmetic and copies ran while one was open for 0% -> 0% of each run, Pallas kernels for 7% -> 11%
where the time goes in v2:
time: 79.8 us; the launch traced here: 79.2 us
  Pallas kernels  28.4 us (36%)
  starting transfers between devices  19.5 us (24%)
  blocking collectives  19.5 us (24%)
  waiting for transfers between devices  9.01 us (11%)
  local copies, waits for them, and re-layouts  1.45 us (2%)
  between operations  1.37 us (2%)
    all_to_all x1, blocking collectives, shards(): parts = lax.all_to_all(out, GROUP, 0, 0, tiled=True)  19.5 us
    pallas_call x1, Pallas kernels, shards(): kernel_call(step_kernel, [SMEM] * 2 + [ANY] * 6, [((16, 192, 128), bf16)]...  15.5 us
    pallas_call x1, Pallas kernels, shards(): kernel_call(prep_kernel, [ANY] * 7, [((28, PLANES, SUB, 128), bf16), ((26...  7.96 us
    all_to_all x1, starting transfers between devices, shards(): sums = lax.all_to_all(folded, 'rows', 0, 0, tiled=True)  7.68 us
    all_to_all x1, waiting for transfers between devices, shards(): sums = lax.all_to_all(folded, 'rows', 0, 0, tiled=True)  7.53 us
    all_to_all x1, starting transfers between devices, shards(): gathered = lax.all_to_all(packed, GROUP, 0, 0, tiled=True)  5.46 us
    ppermute x1, starting transfers between devices, shards(): before = lax.ppermute(last, 'rows', up)  5.02 us
    pallas_call x1, Pallas kernels, shards(): kernel_call(pack_kernel, [ANY] * 9, [((36, 8, 128), f32), ((36, 8, 128),...  2.52 us
  transfers between devices with their start and end apart: 4, of which 2 were waited for; matrix products, arithmetic and copies ran while one was open for 0% of the time, Pallas kernels for 11%

profile of v2, /device:TPU:0, one launch (start us, length us, event | category | flops | bytes accessed | tf_op | source)
XLA Modules:
  0.0 79.2 jit_solution(11950984195206546547)
XLA Ops:
  0.6 2.5 %shard_map.182 = (f32[36,8,128]{2,1,0:T(8,128)}, f32[36,8,128]{2,1,0:T(8,128)}, bf16[16,112,128]{2,1,0:T(8,128)(2,1)}) custom-call(f32[12,16,1024]{2,1,0:T(8,128)} %cond.3, f32[12,16,1024]{2,1,0:T(8,128)} %target.3, f32[12,16,1024]{2,1,0:T(8,128)} %noise.3, bf16[3,3,8,24]{3,2,1,0:T(8,128)(2,1)} %bitcast.6, bf16[3,3,8,128]{3,2,1,0:T(8,128)(2,1)} %bitcast.7, ...), custom_call_target="tpu_custom_call" | custom-call | tf_op jit(solution)/shard_map/pallas_call | solution.py:449
  3.2 5.0 %collective-permute-start = (f32[36,8,128]{2,1,0:T(8,128)}, f32[36,8,128]{2,1,0:T(8,128)S(1)}, u32[]{:S(2)}, u32[]{:S(2)}) collective-permute-start(f32[36,8,128]{2,1,0:T(8,128)} %get-tuple-element.15), channel_id=1, source_target_pairs={{0,8},{8,16},{16,24},{24,32},{32,40},{40,48},{48,56},{1,9},{9,17},... | collective-permute-start | bytes 442376 | tf_op jit(solution)/shard_map/ppermute | solution.py:461
  8.2 1.3 %collective-permute-start.1 = (f32[36,8,128]{2,1,0:T(8,128)}, f32[36,8,128]{2,1,0:T(8,128)S(1)}, u32[]{:S(2)}, u32[]{:S(2)}) collective-permute-start(f32[36,8,128]{2,1,0:T(8,128)} %get-tuple-element.16), channel_id=1, source_target_pairs={{8,0},{16,8},{24,16},{32,24},{40,32},{48,40},{56,48},{9,1},{17,9},... | collective-permute-start | bytes 442376 | tf_op jit(solution)/shard_map/ppermute | solution.py:462
  9.5 5.5 %all-to-all-start = ((bf16[16,112,128]{2,1,0:T(8,128)(2,1)}), bf16[16,112,128]{2,1,0:T(8,128)(2,1)S(1)}, u32[]{:S(2)}, u32[]{:S(2)}) async-start(bf16[16,112,128]{2,1,0:T(8,128)(2,1)} %get-tuple-element.20), calls=%async_computation | async-start | bytes 917504 | tf_op jit(solution)/shard_map/all_to_all | solution.py:463
  15.6 0.0 collective-permute-done.before
  15.6 0.0 copy-start.1
  15.6 1.5 %collective-permute-done.1.after = f32[36,8,128]{2,1,0:T(8,128)S(1)} collective-permute-done((f32[36,8,128]{2,1,0:T(8,128)}, f32[36,8,128]{2,1,0:T(8,128)S(1)}, u32[]{:S(2)}, u32[]{:S(2)}) %collective-permute-start.1) | collective-permute-done | bytes 147488 | tf_op jit(solution)/shard_map/ppermute | solution.py:462
  17.1 0.0 copy-done.1
  17.1 0.0 copy-start.2
  17.1 0.7 copy-done.2
  17.8 8.0 %shard_map.183 = (bf16[28,5,16,128]{3,2,1,0:T(8,128)(2,1)}, f32[26,5,16,128]{3,2,1,0:T(8,128)}, f32[26,5,16,128]{3,2,1,0:T(8,128)}) custom-call(f32[12,16,1024]{2,1,0:T(8,128)} %cond.3, f32[12,16,1024]{2,1,0:T(8,128)} %target.3, f32[12,16,1024]{2,1,0:T(8,128)} %noise.3, f32[36,8,128]{2,1,0:T(8,128)} %copy-done.1, f32[36,8,128]{2,1,0:T(8,128)} %copy-done.2, ...), custom_call_target="tpu_custom_call" | custom-call | flops 4294967296 | bytes 8388608 | tf_op jit(solution)/shard_map/pallas_call | solution.py:464
  25.7 0.0 all-to-all-done.gathered_any
  25.8 0.0 copy-start
  25.8 0.8 copy-done
  26.5 15.5 %shard_map.184 = bf16[16,192,128]{2,1,0:T(8,128)(2,1)} custom-call(s32[1]{0:T(128)S(6)} %copy.20.index, f32[32,8]{1,0:T(8,128)} %constant.12.clone.table, bf16[28,5,16,128]{3,2,1,0:T(8,128)(2,1)} %get-tuple-element.17.cond_any, f32[26,5,16,128]{3,2,1,0:T(8,128)} %get-tuple-element.18.target_any, f32[26,5,16,128]{3,2,1,0:T(8,128)} %get-tuple-element.19.noise_any, ...), custom_call_target="tpu_custom_call" | custom-call | tf_op jit(solution)/shard_map/pallas_call | solution.py:475
  42.0 19.5 %all_to_all.15.parts = bf16[16,192,128]{2,1,0:T(8,128)(2,1)S(1)} all-to-all(bf16[16,192,128]{2,1,0:T(8,128)(2,1)} %shard_map.184), channel_id=1, replica_groups=mesh['section'=2,'rows'=8,'chan'=8] {'section','chan'}, dimensions={0} | all-to-all | bytes 1572864 | tf_op jit(solution)/shard_map/all_to_all | solution.py:490
  61.6 0.7 shard_map.186
  62.3 7.7 %all-to-all-start.2 = ((bf16[8,96,128]{2,1,0:T(8,128)(2,1)}), bf16[8,96,128]{2,1,0:T(8,128)(2,1)S(1)}, u32[]{:S(2)}, u32[]{:S(2)}) async-start(bf16[8,96,128]{2,1,0:T(8,128)(2,1)} %shard_map.186), calls=%async_computation.2 | async-start | bytes 393216 | tf_op jit(solution)/shard_map/all_to_all | solution.py:496
  70.0 0.9 %shard_map.185 = bf16[12,16,1024]{2,1,0:T(8,128)(2,1)} custom-call(bf16[16,192,128]{2,1,0:T(8,128)(2,1)S(1)} %all_to_all.15.parts), custom_call_target="tpu_custom_call" | custom-call | flops 67108864 | bytes 2097152 | tf_op jit(solution)/shard_map/pallas_call | solution.py:492
  71.0 7.5 %all-to-all-done.2.parts = bf16[8,96,128]{2,1,0:T(8,128)(2,1)S(1)} async-done(((bf16[8,96,128]{2,1,0:T(8,128)(2,1)}), bf16[8,96,128]{2,1,0:T(8,128)(2,1)S(1)}, u32[]{:S(2)}, u32[]{:S(2)}) %all-to-all-start.2) | async-done | bytes 196640 | tf_op jit(solution)/shard_map/all_to_all | solution.py:496
  78.5 0.7 shard_map.187
Async XLA Ops:
  3.2 12.4 %collective-permute-start = (f32[36,8,128]{2,1,0:T(8,128)}, f32[36,8,128]{2,1,0:T(8,128)S(1)}, u32[]{:S(2)}, u32[]{:S(2)}) collective-permute-start(f32[36,8,128]{2,1,0:T(8,128)} %get-tuple-element.15), channel_id=1, source_target_pairs={{0,8},{8,16},{16,24},{24,32},{32,40},{40,48},{48,56},{1,9},{9,17},... | collective-permute-start | bytes 442376 | tf_op jit(solution)/shard_map/ppermute | solution.py:461
  8.2 8.9 %collective-permute-start.1 = (f32[36,8,128]{2,1,0:T(8,128)}, f32[36,8,128]{2,1,0:T(8,128)S(1)}, u32[]{:S(2)}, u32[]{:S(2)}) collective-permute-start(f32[36,8,128]{2,1,0:T(8,128)} %get-tuple-element.16), channel_id=1, source_target_pairs={{8,0},{16,8},{24,16},{32,24},{40,32},{48,40},{56,48},{9,1},{17,9},... | collective-permute-start | bytes 442376 | tf_op jit(solution)/shard_map/ppermute | solution.py:462
  9.5 16.3 %all-to-all-start = ((bf16[16,112,128]{2,1,0:T(8,128)(2,1)}), bf16[16,112,128]{2,1,0:T(8,128)(2,1)S(1)}, u32[]{:S(2)}, u32[]{:S(2)}) async-start(bf16[16,112,128]{2,1,0:T(8,128)(2,1)} %get-tuple-element.20), calls=%async_computation | async-start | bytes 917504 | tf_op jit(solution)/shard_map/all_to_all | solution.py:463
  15.6 1.5 %copy-start.1 = (f32[36,8,128]{2,1,0:T(8,128)}, f32[36,8,128]{2,1,0:T(8,128)S(1)}, u32[]{:S(2)}) copy-start(f32[36,8,128]{2,1,0:T(8,128)S(1)} %collective-permute-done.before) | copy-start | bytes 442372
  17.1 0.7 copy-start.2
  25.8 0.8 %copy-start = (bf16[16,112,128]{2,1,0:T(8,128)(2,1)}, bf16[16,112,128]{2,1,0:T(8,128)(2,1)S(1)}, u32[]{:S(2)}) copy-start(bf16[16,112,128]{2,1,0:T(8,128)(2,1)S(1)} %all-to-all-done.gathered_any) | copy-start | bytes 1376260
  62.3 16.1 %all-to-all-start.2 = ((bf16[8,96,128]{2,1,0:T(8,128)(2,1)}), bf16[8,96,128]{2,1,0:T(8,128)(2,1)S(1)}, u32[]{:S(2)}, u32[]{:S(2)}) async-start(bf16[8,96,128]{2,1,0:T(8,128)(2,1)} %shard_map.186), calls=%async_computation.2 | async-start | bytes 393216 | tf_op jit(solution)/shard_map/all_to_all | solution.py:496

commit v3 on v2

--- a/solution.py
+++ b/solution.py
@@ -44,7 +44,7 @@
 
 def place_constants():
     order = np.zeros((WIN, 128), np.float32)
-    back = np.zeros((WIN, 128), np.float32)
+    back = np.zeros((128, 128), np.float32)
     for t in range(PLANES):
         for s in range(SUB):
             col = PLANES * s + t
@@ -71,7 +71,7 @@
 
 
 def sigmoid(v):
-    return 1.0 / (1.0 + jnp.exp(-v))
+    return 0.5 * jnp.tanh(0.5 * v) + 0.5
 
 
 def member():
@@ -160,14 +160,6 @@
     ref[pl.ds(at, n), PLANES + 1] = pltpu.roll(value[:, 0], SUB - 1, 1).astype(bf16)
 
 
-def stack_taps(ref, at, n):
-    parts = []
-    for a in range(3):
-        for b in range(3):
-            parts.append(ref[pl.ds(at + a - 1, n), b:b + PLANES].reshape(n * WIN, 128))
-    return jnp.concatenate(parts, axis=1)
-
-
 def pick_taps(ref, at, n):
     lane = lax.broadcasted_iota(jnp.int32, (SUB, 128), 1)
     total = None
@@ -215,19 +207,53 @@
     for i in range(1, 31):
         wide = row(i)
         if 3 <= i < 29:
-            target9[i - 3:i - 2] = wide[..., 128:256]
-            noise9[i - 3:i - 2] = wide[..., 256:]
+            target9[(i - 3) // 2, (i - 3) % 2] = wide[0, ..., 128:256]
+            noise9[(i - 3) // 2, (i - 3) % 2] = wide[0, ..., 256:]
 
     @pl.loop(0, 7)
     def _(k):
         at = 2 + 4 * k
-        cond_taps[pl.ds(at - 2, 4)] = pick_taps(cond9, at, 4)
+        cond_taps[pl.ds(2 * k, 2)] = pick_taps(cond9, at, 4).reshape(2, 2, PLANES, SUB, 128)
+
+
+def some(ref, row, k, n, base=0):
+    return ref.at[pl.ds((row - base) // 2 + n * k, n), (row - base) % 2]
+
+
+def put_pair(ref, row, k, n, value):
+    dst = some(ref, row, k, n)
+    dst[:, 1:PLANES + 1] = value.astype(bf16)
+    dst[:, 0] = pltpu.roll(value[:, PLANES - 1], 1, 1).astype(bf16)
+    dst[:, PLANES + 1] = pltpu.roll(value[:, 0], SUB - 1, 1).astype(bf16)
+
+
+def stack_rows(ref, row, k, n):
+    parts = []
+    for u in range(4):
+        src = some(ref, row + u - 1, k, n)
+        for b in range(3):
+            parts.append(src[:, b:b + PLANES].reshape(n * WIN, 128))
+    return jnp.concatenate(parts, axis=1)
+
+
+def pick_pair(ref, row, k, n):
+    lane = lax.broadcasted_iota(jnp.int32, (SUB, 128), 1)
+    total = None
+    for a in range(3):
+        src = some(ref, row + a - 1, k, n)
+        for b in range(3):
+            low = (3 * a + b) * COUT
+            mask = jnp.where((lane >= low) & (lane < low + COUT), 1.0, 0.0).astype(bf16)
+            part = src[:, b:b + PLANES] * mask[None, None]
+            total = part if total is None else total + part
+    return total
 
 
 def step_kernel(index, table, cond_any, target_any, noise_any, gathered_any, repeat_any, back_any,
-                out, cond_taps, target9, noise9, gathered, repeat, back, sems, w2, w2t, w1, w3, w3f, w3r, r1, r2,
+                out, cond_taps, target9, noise9, gathered, repeat, back, sems,
+                w2, w2t, w1, w3, w3f, w3r, r1, r2,
                 hid, inp, one, two, dlt, sdl, taps_in, taps_d, resid, noisy, act, slope,
-                den, grad1, film_sum, den_rows):
+                den, grad1, film_sum, den_rows, inside):
     copies = []
     for k, (src, dst) in enumerate(((gathered_any, gathered), (repeat_any, repeat),
                                     (cond_any, cond_taps), (target_any, target9),
@@ -239,135 +265,186 @@
     in_coef, noise_coef, delta_coef = table[level, 3], table[level, 4], table[level, 5]
     first_row = lax.axis_index("rows") * 16 - RIM
     first_col = member() * TW - RIM
+    for ref in (w2, w2t, w3r, r2):
+        ref[...] = jnp.zeros(ref.shape, bf16)
+    for ref in (r1, w3f):
+        ref[...] = jnp.zeros(ref.shape, bf16)
+    den[:, :, PLANES:] = jnp.zeros((10, 2, 8 - PLANES, SUB, 128), bf16)
+    shape = (PLANES, SUB, 128)
+    col = (lax.broadcasted_iota(jnp.int32, shape, 1) * PLANES
+           + lax.broadcasted_iota(jnp.int32, shape, 0))
+    inside[...] = jnp.where((col + first_col >= 0) & (col + first_col < NW), 1.0, 0.0)
+    tile = jnp.where((col >= RIM) & (col < RIM + TW), 1.0, 0.0)
 
     def block(k):
         pair = gathered[:, (k // 2) * 16:(k // 2 + 1) * 16, :].astype(f32)
         low = (k % 2) * 8
         return pair[:, low:low + 8].reshape(128, 128).astype(bf16)
 
+    def spot(tap, v):
+        a, b = tap // 3, tap % 3
+        at = (3 * (a + v) + b) * 128
+        return slice(at, at + 128)
+
+    halves = (slice(0, 128), slice(128, 256))
     copies[0].wait()
+    for v in range(2):
+        r1[halves[v], halves[v]] = block(12)
+    w3[...] = block(11)
+    copies[1].wait()
+    wide = dot(block(13), repeat[:, :9 * 128]).astype(bf16)
+    for tap in range(TAPS):
+        for v in range(2):
+            r2[spot(tap, v), halves[v]] = wide[:, tap * 128:(tap + 1) * 128]
+    w1[:, :128] = block(9)
+    w1[:, 128:] = block(10)
     for tap in range(TAPS):
         part = block(tap)
-        w2[:, tap * 128:(tap + 1) * 128] = part
-        w2t[(8 - tap) * 128:(9 - tap) * 128, :] = part
-    w1[:, :128] = block(9)
-    w1[:, 128:] = block(10)
-    w3[...] = block(11)
-    r1[...] = block(12)
-    copies[1].wait()
+        for v in range(2):
+            w2[halves[v], spot(tap, v)] = part
+            w2t[spot(8 - tap, v), halves[v]] = part
     wide = dot(w3[...], repeat[...]).astype(bf16)
     for tap in range(TAPS):
-        w3r[tap * 128:(tap + 1) * 128, :] = wide[:, tap * 128:(tap + 1) * 128]
-    w3f[...] = wide[:, 9 * 128:]
-    wide = dot(block(13), repeat[:, :9 * 128]).astype(bf16)
-    for tap in range(TAPS):
-        r2[tap * 128:(tap + 1) * 128, :] = wide[:, tap * 128:(tap + 1) * 128]
+        for v in range(2):
+            w3r[spot(tap, v), halves[v]] = wide[:, tap * 128:(tap + 1) * 128]
+    for v in range(2):
+        w3f[halves[v], halves[v]] = wide[:, 9 * 128:]
     lane = lax.broadcasted_iota(jnp.int32, (16, 128), 1)
     pick_film = jnp.where(lane == FILM_LANE, 1.0, 0.0).astype(bf16)
     gain = 1.0 + noise_coef * dot(pick_film, w3[...], 1, 1)[0:1]
 
-    def grid_mask(at, n):
-        shape = (n, PLANES, SUB, 128)
-        row = lax.broadcasted_iota(jnp.int32, shape, 0) + (at + first_row)
-        col = (lax.broadcasted_iota(jnp.int32, shape, 2) * PLANES
-               + lax.broadcasted_iota(jnp.int32, shape, 1) + first_col)
-        return (row >= 0) & (row < NH) & (col >= 0) & (col < NW)
-
-    def tile_mask(n):
-        shape = (n, PLANES, SUB, 128)
-        col = (lax.broadcasted_iota(jnp.int32, shape, 2) * PLANES
-               + lax.broadcasted_iota(jnp.int32, shape, 1))
-        return (col >= RIM) & (col < RIM + TW)
-
-    def cells(value, n):
-        return value.reshape(n, PLANES, SUB, 128)
+    def cells(value):
+        return value.reshape(-1, PLANES, SUB, 128)
 
     def flat(value):
         return value.reshape(-1, 128)
 
-    def sweep(first, count, n, body):
+    def sweep(count, n, body):
         @pl.loop(0, count // n)
         def _(k):
-            body(first + k * n, n)
-
-    def reg_one(at, n):
-        v = dot(flat(cond_taps[pl.ds(at - 2, n)]), r1[...], 1, 1)
-        v = cells(v * sigmoid(v), n)
-        put(hid, at, n, jnp.where(grid_mask(at, n), v, 0.0))
+            body(k, n)
+
+    def clear(ref):
+        @pl.when(first_row < 0)
+        def _():
+            ref[0:4] = jnp.zeros((4, 2, PLANES + 2, SUB, 128), bf16)
+
+        @pl.when(first_row + 32 > NH)
+        def _():
+            ref[12:16] = jnp.zeros((4, 2, PLANES + 2, SUB, 128), bf16)
+
+    def reg_one(k, n):
+        both = jnp.concatenate([flat(some(cond_taps, 2 + v, k, n, 2)[...]) for v in range(2)], 1)
+        value = dot(both, r1[...], 1, 1)
+        for v in range(2):
+            x = value[:, halves[v]]
+            put_pair(hid, 2 + v, k, n, cells(x * sigmoid(x)) * inside[...])
 
     copies[2].wait()
-    sweep(2, 28, 7, reg_one)
-
-    def reg_two(at, n):
-        mean = cells(dot(stack_taps(hid, at, n), r2[...]), n).astype(bf16).astype(f32)
-        rest = target9[pl.ds(at - 3, n)] - mean
-        noised = rest + sigma * noise9[pl.ds(at - 3, n)]
-        resid[pl.ds(at - 3, n)] = rest
-        noisy[pl.ds(at - 3, n)] = noised
-        put(inp, at, n, jnp.where(grid_mask(at, n), in_coef * noised, 0.0))
+    sweep(14, 7, reg_one)
+    clear(hid)
+
+    def reg_two(k, n):
+        value = dot(stack_rows(hid, 3, k, n), r2[...])
+        for v in range(2):
+            row = 3 + v
+            mean = cells(value[:, halves[v]]).astype(bf16).astype(f32)
+            rest = some(target9, row, k, n, 3)[...] - mean
+            noised = rest + sigma * some(noise9, row, k, n, 3)[...]
+            some(resid, row, k, n, 3)[...] = rest
+            some(noisy, row, k, n, 3)[...] = noised
+            put_pair(inp, row, k, n, in_coef * noised * inside[...])
 
     for copy in copies[3:]:
         copy.wait()
-    sweep(3, 26, 13, reg_two)
-
-    def conv_one(at, n):
-        picked = pick_taps(inp, at, n)
-        taps_in[pl.ds(at - 4, n)] = picked
-        both = jnp.concatenate([flat(picked), flat(cond_taps[pl.ds(at - 2, n)])], axis=1)
-        v = dot(both, w1[...], 1, 1)
-        act[pl.ds(at - 4, n)] = cells(v, n)
-        v = v * gain
-        v = cells(v * sigmoid(v), n)
-        put(one, at, n, jnp.where(grid_mask(at, n), v, 0.0))
-
-    sweep(4, 24, 6, conv_one)
-
-    def conv_two(at, n):
-        v = dot(stack_taps(one, at, n), w2[...], 1, 1)
-        s = sigmoid(v)
-        slope[pl.ds(at - 5, n)] = cells(s * (1.0 + v * (1.0 - s)), n)
-        put(two, at, n, jnp.where(grid_mask(at, n), cells(v * s, n), 0.0))
-
-    sweep(5, 22, 11, conv_two)
-
-    def conv_three(at, n):
-        v = cells(dot(stack_taps(two, at, n), w3r[...]), n)
-        value = skip * noisy[pl.ds(at - 3, n)] + out_coef * v
-        den[pl.ds(at - 6, n)] = value.astype(bf16)
-        delta = delta_coef * (value - resid[pl.ds(at - 3, n)])
-        put(dlt, at, n, jnp.where(grid_mask(at, n), delta, 0.0))
-
-    sweep(6, 20, 10, conv_three)
-
-    def delta_two(at, n):
-        picked = pick_taps(dlt, at, n)
-        taps_d[pl.ds(at - 7, n)] = picked
-        v = cells(dot(flat(picked), w3f[...], 1, 1), n) * slope[pl.ds(at - 5, n)]
-        put(sdl, at, n, jnp.where(grid_mask(at, n), v, 0.0))
-
-    sweep(7, 18, 6, delta_two)
-
+    sweep(13, 13, reg_two)
+    clear(inp)
+
+    def conv_one(k, n):
+        for v in range(2):
+            row = 4 + v
+            picked = pick_pair(inp, row, k, n)
+            some(taps_in, row, k, n, 4)[...] = picked
+            both = jnp.concatenate([flat(picked), flat(some(cond_taps, row, k, n, 2)[...])], 1)
+            value = dot(both, w1[...], 1, 1)
+            some(act, row, k, n, 4)[...] = cells(value)
+            u = value * gain
+            put_pair(one, row, k, n, cells(u * sigmoid(u)) * inside[...])
+
+    sweep(12, 6, conv_one)
+    clear(one)
+
+    def conv_two(k, n):
+        value = dot(stack_rows(one, 5, k, n), w2[...], 1, 1)
+        for v in range(2):
+            x = value[:, halves[v]]
+            s = sigmoid(x)
+            some(slope, 5 + v, k, n, 5)[...] = cells(s * (1.0 + x * (1.0 - s)))
+            put_pair(two, 5 + v, k, n, cells(x * s) * inside[...])
+
+    sweep(11, 11, conv_two)
+    clear(two)
+
+    def conv_three(k, n):
+        value = dot(stack_rows(two, 6, k, n), w3r[...])
+        for v in range(2):
+            row = 6 + v
+            full = skip * some(noisy, row, k, n, 3)[...] + out_coef * cells(value[:, halves[v]])
+            some(den, row, k, n, 6)[:, :PLANES] = full.astype(bf16)
+            delta = delta_coef * (full - some(resid, row, k, n, 3)[...])
+            put_pair(dlt, row, k, n, delta * inside[...])
+
+    sweep(10, 10, conv_three)
+    clear(dlt)
+
+    def delta_two(k, n):
+        parts = []
+        for v in range(2):
+            picked = pick_pair(dlt, 7 + v, k, n)
+            some(taps_d, 7 + v, k, n, 7)[...] = picked
+            parts.append(flat(picked))
+        value = dot(jnp.concatenate(parts, axis=1), w3f[...], 1, 1)
+        for v in range(2):
+            x = cells(value[:, halves[v]]) * some(slope, 7 + v, k, n, 5)[...]
+            put_pair(sdl, 7 + v, k, n, x * inside[...])
+
+    sweep(9, 9, delta_two)
+    clear(sdl)
     film_sum[...] = jnp.zeros((8, 128), f32)
 
-    def delta_one(at, n):
-        v = dot(stack_taps(sdl, at, n), w2t[...])
-        a = flat(act[pl.ds(at - 4, n)])
-        u = a * gain
-        s = sigmoid(u)
-        g = cells(v * (s * (1.0 + u * (1.0 - s))), n)
-        g = flat(jnp.where(tile_mask(n), g, 0.0))
-        film_sum[...] += jnp.sum((g * a).reshape(-1, 8, 128), axis=0)
-        grad1[pl.ds(at - 8, n)] = cells(g * gain, n).astype(bf16)
-
-    sweep(8, 16, 8, delta_one)
-
-    inside = jnp.where(tile_mask(1), 1.0, 0.0).astype(bf16)
-    own = slice(RIM, RIM + 16)
-    d2 = flat(sdl[own, 1:PLANES + 1] * inside)
-    g2 = dot(d2, stack_taps(one, RIM, 16), 0, 0)
-    g1 = dot(flat(grad1[...]),
-             jnp.concatenate([flat(taps_in[4:20]), flat(cond_taps[6:22])], axis=1), 0, 0)
-    g3 = dot(flat(two[own, 1:PLANES + 1] * inside), flat(taps_d[1:17]), 0, 0)
+    def delta_one(k, n):
+        value = dot(stack_rows(sdl, 8, k, n), w2t[...])
+        for v in range(2):
+            a = flat(some(act, 8 + v, k, n, 4)[...])
+            u = a * gain
+            s = sigmoid(u)
+            g = flat(cells(value[:, halves[v]] * (s * (1.0 + u * (1.0 - s)))) * tile)
+            film_sum[...] += jnp.sum((g * a).reshape(-1, 8, 128), axis=0)
+            some(grad1, 8 + v, k, n, 8)[...] = cells(g * gain).astype(bf16)
+
+    sweep(8, 8, delta_one)
+
+    tile_low = tile.astype(bf16)
+
+    def both_rows(read):
+        return jnp.concatenate([read(8), read(9)], axis=0)
+
+    def own_cells(ref):
+        return lambda row: flat(some(ref, row, 0, 8)[:, 1:PLANES + 1] * tile_low)
+
+    def own_field(ref, base):
+        return lambda row: flat(some(ref, row, 0, 8, base)[...])
+
+    def taps_of(row):
+        return jnp.concatenate([flat(some(one, row + a - 1, 0, 8)[:, b:b + PLANES])
+                                for a in range(3) for b in range(3)], axis=1)
+
+    def first_taps(row):
+        return jnp.concatenate([own_field(taps_in, 4)(row), own_field(cond_taps, 2)(row)], axis=1)
+
+    g2 = dot(both_rows(own_cells(sdl)), both_rows(taps_of), 0, 0)
+    g1 = dot(both_rows(own_field(grad1, 8)), both_rows(first_taps), 0, 0)
+    g3 = dot(both_rows(own_cells(two)), both_rows(own_field(taps_d, 7)), 0, 0)
     film = noise_coef * jnp.sum(film_sum[...], axis=0, keepdims=True)
     film = jnp.transpose(jnp.broadcast_to(film, (8, 128)))[:, 0:1]
     g3 = jnp.where(lax.broadcasted_iota(jnp.int32, (128, 128), 1) == FILM_LANE, film, g3)
@@ -378,14 +455,14 @@
 
     fields = (lax.broadcasted_iota(jnp.int32, (16, 128), 0)
               == lax.broadcasted_iota(jnp.int32, (16, 128), 1)).astype(f32).astype(bf16)
-    for i in range(16):
-        turned = dot(fields, den[i + 2].reshape(WIN, 128), 1, 1).astype(bf16)
-        den_rows[i * 16:(i + 1) * 16, :] = dot(turned, back[...])
+    turned = dot(fields, den[1:9].reshape(16 * 128, 128), 1, 1).astype(bf16)
+    turned = jnp.concatenate([turned[:, i * 128:(i + 1) * 128] for i in range(16)], axis=0)
+    den_rows[...] = dot(turned, back[...])
     for c in range(6):
         left = den_rows[pl.ds(c, 16, stride=16), :]
         right = den_rows[pl.ds(c + 6, 16, stride=16), :]
-        tile = jnp.where(lane < TW, left, right).astype(bf16)
-        out[:, 96 + c * 16:96 + (c + 1) * 16, :] = jnp.broadcast_to(tile[None], (16, 16, 128))
+        piece = jnp.where(lane < TW, left, right).astype(bf16)
+        out[:, 96 + c * 16:96 + (c + 1) * 16, :] = jnp.broadcast_to(piece[None], (16, 16, 128))
 
 
 def fold_kernel(parts, out):
@@ -441,6 +518,10 @@
 
 def planes(rows, dtype, count=PLANES):
     return pltpu.VMEM((rows, count, SUB, 128), dtype)
+
+
+def pairs(rows, dtype, count=PLANES):
+    return pltpu.VMEM((rows // 2, 2, count, SUB, 128), dtype)
 
 
 def shards(condition, target, noise_draw, sigma_index, reg_first, reg_second, first_kernel,
@@ -463,27 +544,29 @@
     gathered = lax.all_to_all(packed, GROUP, 0, 0, tiled=True)
     cond_taps, target9, noise9 = kernel_call(
         prep_kernel, [ANY] * 7,
-        [((28, PLANES, SUB, 128), bf16), ((26, PLANES, SUB, 128), f32),
-         ((26, PLANES, SUB, 128), f32)],
+        [((14, 2, PLANES, SUB, 128), bf16), ((13, 2, PLANES, SUB, 128), f32),
+         ((13, 2, PLANES, SUB, 128), f32)],
         [pltpu.VMEM((48, 32, 128), f32), pltpu.VMEM((3, COUT, 16, 256), f32),
          planes(32, bf16, 7), pltpu.VMEM((WIN, 128), bf16), pltpu.VMEM((128, 384), bf16),
          pltpu.SemaphoreType.DMA((7,))],
         limit=60,
         cost=pl.CostEstimate(flops=1 << 32, bytes_accessed=8 * MIB, transcendentals=0),
     )(condition, target, noise_draw, before, after, jnp.asarray(order, bf16), jnp.asarray(spread, bf16))
-    wide = [planes(32, bf16, 7) for _ in range(6)]
+    wide = [pairs(32, bf16, PLANES + 2) for _ in range(6)]
     out, = kernel_call(
         step_kernel, [SMEM] * 2 + [ANY] * 6, [((16, 192, 128), bf16)],
-        [planes(28, bf16), planes(26, f32), planes(26, f32), pltpu.VMEM((16, 112, 128), bf16),
-         pltpu.VMEM((128, 1280), bf16), pltpu.VMEM((WIN, 128), bf16),
-         pltpu.SemaphoreType.DMA((6,)), pltpu.VMEM((128, 1152), bf16), pltpu.VMEM((1152, 128), bf16),
-         pltpu.VMEM((128, 256), bf16), pltpu.VMEM((128, 128), bf16),
-         pltpu.VMEM((128, 128), bf16), pltpu.VMEM((1152, 128), bf16),
-         pltpu.VMEM((128, 128), bf16), pltpu.VMEM((1152, 128), bf16)]
+        [pairs(28, bf16), pairs(26, f32), pairs(26, f32), pltpu.VMEM((16, 112, 128), bf16),
+         pltpu.VMEM((128, 1280), bf16), pltpu.VMEM((128, 128), bf16),
+         pltpu.SemaphoreType.DMA((6,)), pltpu.VMEM((256, 1536), bf16),
+         pltpu.VMEM((1536, 256), bf16), pltpu.VMEM((128, 256), bf16),
+         pltpu.VMEM((128, 128), bf16), pltpu.VMEM((256, 256), bf16),
+         pltpu.VMEM((1536, 256), bf16), pltpu.VMEM((256, 256), bf16),
+         pltpu.VMEM((1536, 256), bf16)]
         + wide
-        + [planes(24, bf16), planes(18, bf16), planes(26, f32), planes(26, f32),
-           planes(24, f32), planes(22, f32), planes(20, bf16), planes(16, bf16),
-           pltpu.VMEM((8, 128), f32), pltpu.VMEM((256, 128), f32)],
+        + [pairs(24, bf16), pairs(18, bf16), pairs(26, f32), pairs(26, f32),
+           pairs(24, f32), pairs(22, f32), pairs(20, bf16, 8), pairs(16, bf16),
+           pltpu.VMEM((8, 128), f32), pltpu.VMEM((256, 128), f32),
+           pltpu.VMEM((PLANES, SUB, 128), f32)],
         limit=60,
     )(sigma_index, jnp.asarray(coef_table()), cond_taps, target9, noise9, gathered,
       jnp.asarray(repeat, bf16), jnp.asarray(back, bf16))

time: 79.8 us -> 76.1 us (0.954)
  Pallas kernels: 28.4 us -> 24.8 us
    pallas_call x1, Pallas kernels: 15.5 us -> 11.9 us  [shards(): kernel_call(step_kernel, [SMEM] * 2 + [ANY] * 6, [((16, 192, 128), bf16)]...]
  transfers between devices with their start and end apart: 4 -> 4, of which waited for: 2 -> 2; matrix products, arithmetic and copies ran while one was open for 0% -> 0% of each run, Pallas kernels for 11% -> 12%
where the time goes in v3:
time: 76.1 us; the launch traced here: 75.5 us
  Pallas kernels  24.8 us (33%)
  blocking collectives  19.5 us (26%)
  starting transfers between devices  19.4 us (25%)
  waiting for transfers between devices  9.01 us (12%)
  local copies, waits for them, and re-layouts  1.45 us (2%)
  between operations  1.37 us (2%)
    all_to_all x1, blocking collectives, shards(): parts = lax.all_to_all(out, GROUP, 0, 0, tiled=True)  19.5 us
    pallas_call x1, Pallas kernels, shards(): kernel_call(step_kernel, [SMEM] * 2 + [ANY] * 6, [((16, 192, 128), bf16)]...  11.9 us
    pallas_call x1, Pallas kernels, shards(): kernel_call(prep_kernel, [ANY] * 7, [((14, 2, PLANES, SUB, 128), bf16), (...  7.96 us
    all_to_all x1, starting transfers between devices, shards(): sums = lax.all_to_all(folded, 'rows', 0, 0, tiled=True)  7.61 us
    all_to_all x1, waiting for transfers between devices, shards(): sums = lax.all_to_all(folded, 'rows', 0, 0, tiled=True)  7.53 us
    all_to_all x1, starting transfers between devices, shards(): gathered = lax.all_to_all(packed, GROUP, 0, 0, tiled=True)  5.46 us
    ppermute x1, starting transfers between devices, shards(): before = lax.ppermute(last, 'rows', up)  5.02 us
    pallas_call x1, Pallas kernels, shards(): kernel_call(pack_kernel, [ANY] * 9, [((36, 8, 128), f32), ((36, 8, 128),...  2.52 us
  transfers between devices with their start and end apart: 4, of which 2 were waited for; matrix products, arithmetic and copies ran while one was open for 0% of the time, Pallas kernels for 12%

profile of v3, /device:TPU:0, one launch (start us, length us, event | category | flops | bytes accessed | tf_op | source)
XLA Modules:
  0.0 75.5 jit_solution(14163462414363554945)
XLA Ops:
  0.6 2.5 %shard_map.182 = (f32[36,8,128]{2,1,0:T(8,128)}, f32[36,8,128]{2,1,0:T(8,128)}, bf16[16,112,128]{2,1,0:T(8,128)(2,1)}) custom-call(f32[12,16,1024]{2,1,0:T(8,128)} %cond.3, f32[12,16,1024]{2,1,0:T(8,128)} %target.3, f32[12,16,1024]{2,1,0:T(8,128)} %noise.3, bf16[3,3,8,24]{3,2,1,0:T(8,128)(2,1)} %bitcast.6, bf16[3,3,8,128]{3,2,1,0:T(8,128)(2,1)} %bitcast.7, ...), custom_call_target="tpu_custom_call" | custom-call | tf_op jit(solution)/shard_map/pallas_call | solution.py:530
  3.2 5.0 %collective-permute-start = (f32[36,8,128]{2,1,0:T(8,128)}, f32[36,8,128]{2,1,0:T(8,128)S(1)}, u32[]{:S(2)}, u32[]{:S(2)}) collective-permute-start(f32[36,8,128]{2,1,0:T(8,128)} %get-tuple-element.15), channel_id=1, source_target_pairs={{0,8},{8,16},{16,24},{24,32},{32,40},{40,48},{48,56},{1,9},{9,17},... | collective-permute-start | bytes 442376 | tf_op jit(solution)/shard_map/ppermute | solution.py:542
  8.2 1.3 %collective-permute-start.1 = (f32[36,8,128]{2,1,0:T(8,128)}, f32[36,8,128]{2,1,0:T(8,128)S(1)}, u32[]{:S(2)}, u32[]{:S(2)}) collective-permute-start(f32[36,8,128]{2,1,0:T(8,128)} %get-tuple-element.16), channel_id=1, source_target_pairs={{8,0},{16,8},{24,16},{32,24},{40,32},{48,40},{56,48},{9,1},{17,9},... | collective-permute-start | bytes 442376 | tf_op jit(solution)/shard_map/ppermute | solution.py:543
  9.5 5.5 %all-to-all-start = ((bf16[16,112,128]{2,1,0:T(8,128)(2,1)}), bf16[16,112,128]{2,1,0:T(8,128)(2,1)S(1)}, u32[]{:S(2)}, u32[]{:S(2)}) async-start(bf16[16,112,128]{2,1,0:T(8,128)(2,1)} %get-tuple-element.20), calls=%async_computation | async-start | bytes 917504 | tf_op jit(solution)/shard_map/all_to_all | solution.py:544
  15.6 0.0 collective-permute-done.before
  15.6 0.0 copy-start.1
  15.6 1.5 %collective-permute-done.1.after = f32[36,8,128]{2,1,0:T(8,128)S(1)} collective-permute-done((f32[36,8,128]{2,1,0:T(8,128)}, f32[36,8,128]{2,1,0:T(8,128)S(1)}, u32[]{:S(2)}, u32[]{:S(2)}) %collective-permute-start.1) | collective-permute-done | bytes 147488 | tf_op jit(solution)/shard_map/ppermute | solution.py:543
  17.1 0.0 copy-done.1
  17.1 0.0 copy-start.2
  17.1 0.7 copy-done.2
  17.8 8.0 %shard_map.183 = (bf16[14,2,5,16,128]{4,3,2,1,0:T(8,128)(2,1)}, f32[13,2,5,16,128]{4,3,2,1,0:T(8,128)}, f32[13,2,5,16,128]{4,3,2,1,0:T(8,128)}) custom-call(f32[12,16,1024]{2,1,0:T(8,128)} %cond.3, f32[12,16,1024]{2,1,0:T(8,128)} %target.3, f32[12,16,1024]{2,1,0:T(8,128)} %noise.3, f32[36,8,128]{2,1,0:T(8,128)} %copy-done.1, f32[36,8,128]{2,1,0:T(8,128)} %copy-done.2, ...), custom_call_target="tpu_custom_call" | custom-call | flops 4294967296 | bytes 8388608 | tf_op jit(solution)/shard_map/pallas_call | solution.py:545
  25.7 0.0 all-to-all-done.gathered_any
  25.8 0.0 copy-start
  25.8 0.8 %copy-done = bf16[16,112,128]{2,1,0:T(8,128)(2,1)} copy-done((bf16[16,112,128]{2,1,0:T(8,128)(2,1)}, bf16[16,112,128]{2,1,0:T(8,128)(2,1)S(1)}, u32[]{:S(2)}) %copy-start) | copy-done | bytes 458776
  26.5 11.9 %shard_map.184 = bf16[16,192,128]{2,1,0:T(8,128)(2,1)} custom-call(s32[1]{0:T(128)S(6)} %copy.20.index, f32[32,8]{1,0:T(8,128)} %constant.12.clone.table, bf16[14,2,5,16,128]{4,3,2,1,0:T(8,128)(2,1)} %get-tuple-element.17.cond_any, f32[13,2,5,16,128]{4,3,2,1,0:T(8,128)} %get-tuple-element.18.target_any, f32[13,2,5,16,128]{4,3,2,1,0:T(8,128)} %get-tuple-element.19.noise_any, ...), custom_call_target="tpu_custom_call" | custom-call | tf_op jit(solution)/shard_map/pallas_call | solution.py:556
  38.4 19.5 %all_to_all.15.parts = bf16[16,192,128]{2,1,0:T(8,128)(2,1)S(1)} all-to-all(bf16[16,192,128]{2,1,0:T(8,128)(2,1)} %shard_map.184), channel_id=1, replica_groups=mesh['section'=2,'rows'=8,'chan'=8] {'section','chan'}, dimensions={0} | all-to-all | bytes 1572864 | tf_op jit(solution)/shard_map/all_to_all | solution.py:573
  58.0 0.7 shard_map.186
  58.7 7.6 %all-to-all-start.2 = ((bf16[8,96,128]{2,1,0:T(8,128)(2,1)}), bf16[8,96,128]{2,1,0:T(8,128)(2,1)S(1)}, u32[]{:S(2)}, u32[]{:S(2)}) async-start(bf16[8,96,128]{2,1,0:T(8,128)(2,1)} %shard_map.186), calls=%async_computation.2 | async-start | bytes 393216 | tf_op jit(solution)/shard_map/all_to_all | solution.py:579
  66.3 0.9 %shard_map.185 = bf16[12,16,1024]{2,1,0:T(8,128)(2,1)} custom-call(bf16[16,192,128]{2,1,0:T(8,128)(2,1)S(1)} %all_to_all.15.parts), custom_call_target="tpu_custom_call" | custom-call | flops 67108864 | bytes 2097152 | tf_op jit(solution)/shard_map/pallas_call | solution.py:575
  67.3 7.5 %all-to-all-done.2.parts = bf16[8,96,128]{2,1,0:T(8,128)(2,1)S(1)} async-done(((bf16[8,96,128]{2,1,0:T(8,128)(2,1)}), bf16[8,96,128]{2,1,0:T(8,128)(2,1)S(1)}, u32[]{:S(2)}, u32[]{:S(2)}) %all-to-all-start.2) | async-done | bytes 196640 | tf_op jit(solution)/shard_map/all_to_all | solution.py:579
  74.8 0.7 shard_map.187
Async XLA Ops:
  3.2 12.4 %collective-permute-start = (f32[36,8,128]{2,1,0:T(8,128)}, f32[36,8,128]{2,1,0:T(8,128)S(1)}, u32[]{:S(2)}, u32[]{:S(2)}) collective-permute-start(f32[36,8,128]{2,1,0:T(8,128)} %get-tuple-element.15), channel_id=1, source_target_pairs={{0,8},{8,16},{16,24},{24,32},{32,40},{40,48},{48,56},{1,9},{9,17},... | collective-permute-start | bytes 442376 | tf_op jit(solution)/shard_map/ppermute | solution.py:542
  8.2 8.9 %collective-permute-start.1 = (f32[36,8,128]{2,1,0:T(8,128)}, f32[36,8,128]{2,1,0:T(8,128)S(1)}, u32[]{:S(2)}, u32[]{:S(2)}) collective-permute-start(f32[36,8,128]{2,1,0:T(8,128)} %get-tuple-element.16), channel_id=1, source_target_pairs={{8,0},{16,8},{24,16},{32,24},{40,32},{48,40},{56,48},{9,1},{17,9},... | collective-permute-start | bytes 442376 | tf_op jit(solution)/shard_map/ppermute | solution.py:543
  9.5 16.3 %all-to-all-start = ((bf16[16,112,128]{2,1,0:T(8,128)(2,1)}), bf16[16,112,128]{2,1,0:T(8,128)(2,1)S(1)}, u32[]{:S(2)}, u32[]{:S(2)}) async-start(bf16[16,112,128]{2,1,0:T(8,128)(2,1)} %get-tuple-element.20), calls=%async_computation | async-start | bytes 917504 | tf_op jit(solution)/shard_map/all_to_all | solution.py:544
  15.6 1.5 %copy-start.1 = (f32[36,8,128]{2,1,0:T(8,128)}, f32[36,8,128]{2,1,0:T(8,128)S(1)}, u32[]{:S(2)}) copy-start(f32[36,8,128]{2,1,0:T(8,128)S(1)} %collective-permute-done.before) | copy-start | bytes 442372
  17.1 0.7 copy-start.2
  25.8 0.8 %copy-start = (bf16[16,112,128]{2,1,0:T(8,128)(2,1)}, bf16[16,112,128]{2,1,0:T(8,128)(2,1)S(1)}, u32[]{:S(2)}) copy-start(bf16[16,112,128]{2,1,0:T(8,128)(2,1)S(1)} %all-to-all-done.gathered_any) | copy-start | bytes 1376260
  58.7 16.1 %all-to-all-start.2 = ((bf16[8,96,128]{2,1,0:T(8,128)(2,1)}), bf16[8,96,128]{2,1,0:T(8,128)(2,1)S(1)}, u32[]{:S(2)}, u32[]{:S(2)}) async-start(bf16[8,96,128]{2,1,0:T(8,128)(2,1)} %shard_map.186), calls=%async_computation.2 | async-start | bytes 393216 | tf_op jit(solution)/shard_map/all_to_all | solution.py:579

commit v4 on v3

--- a/solution.py
+++ b/solution.py
@@ -173,7 +173,7 @@
 
 
 def prep_kernel(cond, target, noise, before, after, order_any, spread_any,
-                cond_taps, target9, noise9, scr, wide, cond9, order, spread, sems):
+                cond_taps, fields, scr, wide, cond9, cells, order, spread, sems):
     copies = [window_copy(src, wide.at[k], sems.at[k])
               for k, src in enumerate((target, noise, cond))]
     others = [
@@ -192,23 +192,21 @@
         copy.wait()
     flat = scr.reshape(48 * 32, 128)
 
-    def row(i):
+    for i in range(1, 31):
         x = flat[pl.ds(i, 48, stride=32), :]
         high = x.astype(bf16)
         rest = x[:32] - high[:32].astype(f32)
         mid = rest.astype(bf16)
         low = (rest - mid.astype(f32)).astype(bf16)
         rows = jnp.concatenate([high, mid, low, jnp.zeros((16, 128), bf16)], axis=0)
-        cells = dot(order[...], rows, 1, 1).astype(bf16)
-        wide = dot(cells, spread[...]).reshape(1, PLANES, SUB, 384)
-        put(cond9, i, 1, wide[..., :128])
-        return wide
-
-    for i in range(1, 31):
-        wide = row(i)
+        turned = dot(order[...], rows, 1, 1).astype(bf16)
+        cells[(i - 1) * WIN:i * WIN] = turned
         if 3 <= i < 29:
-            target9[(i - 3) // 2, (i - 3) % 2] = wide[0, ..., 128:256]
-            noise9[(i - 3) // 2, (i - 3) % 2] = wide[0, ..., 256:]
+            fields[(i - 3) // 2, (i - 3) % 2] = turned.reshape(PLANES, SUB, 128)
+    count = 6
+    for i in range(1, 31, count):
+        wide = dot(cells[(i - 1) * WIN:(i - 1 + count) * WIN], spread[...])
+        put(cond9, i, count, wide.reshape(count, PLANES, SUB, 128))
 
     @pl.loop(0, 7)
     def _(k):
@@ -217,7 +215,7 @@
 
 
 def some(ref, row, k, n, base=0):
-    return ref.at[pl.ds((row - base) // 2 + n * k, n), (row - base) % 2]
+    return ref.at[pl.ds((row - base) // 2 + k, n), (row - base) % 2]
 
 
 def put_pair(ref, row, k, n, value):
@@ -249,20 +247,18 @@
     return total
 
 
-def step_kernel(index, table, cond_any, target_any, noise_any, gathered_any, repeat_any, back_any,
-                out, cond_taps, target9, noise9, gathered, repeat, back, sems,
+def step_kernel(index_any, table_any, cond_any, field_any, gathered_any, repeat_any, back_any,
+                spread_any, out, index, table, cond_taps, fields, gathered, repeat, back, spread, sems,
                 w2, w2t, w1, w3, w3f, w3r, r1, r2,
                 hid, inp, one, two, dlt, sdl, taps_in, taps_d, resid, noisy, act, slope,
                 den, grad1, film_sum, den_rows, inside):
     copies = []
     for k, (src, dst) in enumerate(((gathered_any, gathered), (repeat_any, repeat),
-                                    (cond_any, cond_taps), (target_any, target9),
-                                    (noise_any, noise9), (back_any, back))):
+                                    (cond_any, cond_taps), (spread_any, spread),
+                                    (field_any, fields), (index_any, index),
+                                    (table_any, table), (back_any, back))):
         copies.append(pltpu.make_async_copy(src, dst, sems.at[k]))
         copies[-1].start()
-    level = index[0]
-    sigma, skip, out_coef = table[level, 0], table[level, 1], table[level, 2]
-    in_coef, noise_coef, delta_coef = table[level, 3], table[level, 4], table[level, 5]
     first_row = lax.axis_index("rows") * 16 - RIM
     first_col = member() * TW - RIM
     for ref in (w2, w2t, w3r, r2):
@@ -309,9 +305,6 @@
             w3r[spot(tap, v), halves[v]] = wide[:, tap * 128:(tap + 1) * 128]
     for v in range(2):
         w3f[halves[v], halves[v]] = wide[:, 9 * 128:]
-    lane = lax.broadcasted_iota(jnp.int32, (16, 128), 1)
-    pick_film = jnp.where(lane == FILM_LANE, 1.0, 0.0).astype(bf16)
-    gain = 1.0 + noise_coef * dot(pick_film, w3[...], 1, 1)[0:1]
 
     def cells(value):
         return value.reshape(-1, PLANES, SUB, 128)
@@ -322,7 +315,10 @@
     def sweep(count, n, body):
         @pl.loop(0, count // n)
         def _(k):
-            body(k, n)
+            body(k * n, n)
+
+        if count % n:
+            body(count // n * n, count % n)
 
     def clear(ref):
         @pl.when(first_row < 0)
@@ -349,14 +345,21 @@
         for v in range(2):
             row = 3 + v
             mean = cells(value[:, halves[v]]).astype(bf16).astype(f32)
-            rest = some(target9, row, k, n, 3)[...] - mean
-            noised = rest + sigma * some(noise9, row, k, n, 3)[...]
+            both = dot(flat(some(fields, row, k, n, 3)[...]), spread[...])
+            rest = cells(both[:, halves[0]]) - mean
+            noised = rest + sigma * cells(both[:, halves[1]])
             some(resid, row, k, n, 3)[...] = rest
             some(noisy, row, k, n, 3)[...] = noised
             put_pair(inp, row, k, n, in_coef * noised * inside[...])
 
     for copy in copies[3:]:
         copy.wait()
+    level = index[0]
+    sigma, skip, out_coef = table[level, 0], table[level, 1], table[level, 2]
+    in_coef, noise_coef, delta_coef = table[level, 3], table[level, 4], table[level, 5]
+    lane = lax.broadcasted_iota(jnp.int32, (16, 128), 1)
+    pick_film = jnp.where(lane == FILM_LANE, 1.0, 0.0).astype(bf16)
+    gain = 1.0 + noise_coef * dot(pick_film, w3[...], 1, 1)[0:1]
     sweep(13, 13, reg_two)
     clear(inp)
 
@@ -394,7 +397,7 @@
             delta = delta_coef * (full - some(resid, row, k, n, 3)[...])
             put_pair(dlt, row, k, n, delta * inside[...])
 
-    sweep(10, 10, conv_three)
+    sweep(10, 5, conv_three)
     clear(dlt)
 
     def delta_two(k, n):
@@ -500,7 +503,6 @@
 
 
 VMEM = pl.BlockSpec(memory_space=pltpu.VMEM)
-SMEM = pl.BlockSpec(memory_space=pltpu.SMEM)
 ANY = pl.BlockSpec(memory_space=pl.ANY)
 
 
@@ -542,22 +544,22 @@
     before = lax.ppermute(last, "rows", up)
     after = lax.ppermute(leading, "rows", [(j, i) for i, j in up])
     gathered = lax.all_to_all(packed, GROUP, 0, 0, tiled=True)
-    cond_taps, target9, noise9 = kernel_call(
+    cond_taps, fields = kernel_call(
         prep_kernel, [ANY] * 7,
-        [((14, 2, PLANES, SUB, 128), bf16), ((13, 2, PLANES, SUB, 128), f32),
-         ((13, 2, PLANES, SUB, 128), f32)],
+        [((14, 2, PLANES, SUB, 128), bf16), ((13, 2, PLANES, SUB, 128), bf16)],
         [pltpu.VMEM((48, 32, 128), f32), pltpu.VMEM((3, COUT, 16, 256), f32),
-         planes(32, bf16, 7), pltpu.VMEM((WIN, 128), bf16), pltpu.VMEM((128, 384), bf16),
+         planes(32, bf16, 7), pltpu.VMEM((30 * WIN, 128), bf16), pltpu.VMEM((WIN, 128), bf16), pltpu.VMEM((128, 128), bf16),
          pltpu.SemaphoreType.DMA((7,))],
         limit=60,
         cost=pl.CostEstimate(flops=1 << 32, bytes_accessed=8 * MIB, transcendentals=0),
-    )(condition, target, noise_draw, before, after, jnp.asarray(order, bf16), jnp.asarray(spread, bf16))
+    )(condition, target, noise_draw, before, after, jnp.asarray(order, bf16), jnp.asarray(spread[:, :128], bf16))
     wide = [pairs(32, bf16, PLANES + 2) for _ in range(6)]
     out, = kernel_call(
-        step_kernel, [SMEM] * 2 + [ANY] * 6, [((16, 192, 128), bf16)],
-        [pairs(28, bf16), pairs(26, f32), pairs(26, f32), pltpu.VMEM((16, 112, 128), bf16),
-         pltpu.VMEM((128, 1280), bf16), pltpu.VMEM((128, 128), bf16),
-         pltpu.SemaphoreType.DMA((6,)), pltpu.VMEM((256, 1536), bf16),
+        step_kernel, [ANY] * 8, [((16, 192, 128), bf16)],
+        [pltpu.SMEM((1,), jnp.int32), pltpu.SMEM((NSIG, 8), f32), pairs(28, bf16),
+         pairs(26, bf16), pltpu.VMEM((16, 112, 128), bf16), pltpu.VMEM((128, 1280), bf16),
+         pltpu.VMEM((128, 128), bf16), pltpu.VMEM((128, 256), bf16),
+         pltpu.SemaphoreType.DMA((8,)), pltpu.VMEM((256, 1536), bf16),
          pltpu.VMEM((1536, 256), bf16), pltpu.VMEM((128, 256), bf16),
          pltpu.VMEM((128, 128), bf16), pltpu.VMEM((256, 256), bf16),
          pltpu.VMEM((1536, 256), bf16), pltpu.VMEM((256, 256), bf16),
@@ -568,8 +570,8 @@
            pltpu.VMEM((8, 128), f32), pltpu.VMEM((256, 128), f32),
            pltpu.VMEM((PLANES, SUB, 128), f32)],
         limit=60,
-    )(sigma_index, jnp.asarray(coef_table()), cond_taps, target9, noise9, gathered,
-      jnp.asarray(repeat, bf16), jnp.asarray(back, bf16))
+    )(sigma_index, jnp.asarray(coef_table()), cond_taps, fields, gathered,
+      jnp.asarray(repeat, bf16), jnp.asarray(back, bf16), jnp.asarray(spread[:, 128:], bf16))
     parts = lax.all_to_all(out, GROUP, 0, 0, tiled=True)
     folded, = kernel_call(fold_kernel, [VMEM], [((8, 96, 128), bf16)])(parts)
     denoised, = kernel_call(

time: 76.1 us -> 72.4 us (0.951)
  Pallas kernels: 24.8 us -> 19.1 us
  waiting for transfers between devices: 9.01 us -> 12.4 us
  blocking collectives: 19.5 us -> 17.3 us
  starting transfers between devices: 19.4 us -> 20.3 us
    pallas_call x1, Pallas kernels: 7.96 us -> 3.93 us  [shards(): kernel_call(prep_kernel, [ANY] * 7, [((14, 2, PLANES, SUB, 128), bf16), (...]
    all_to_all x1, waiting for transfers between devices: 0.01 us -> 3.41 us  [shards(): gathered = lax.all_to_all(packed, GROUP, 0, 0, tiled=True)]
    all_to_all x1, blocking collectives: 19.5 us -> 17.3 us  [shards(): parts = lax.all_to_all(out, GROUP, 0, 0, tiled=True)]
    pallas_call x1, Pallas kernels: 11.9 us -> 10.2 us  [shards(): kernel_call(step_kernel, [ANY] * 8, [((16, 192, 128), bf16)], [pltpu.SMEM...]
    all_to_all x1, starting transfers between devices: 7.61 us -> 8.57 us  [shards(): sums = lax.all_to_all(folded, 'rows', 0, 0, tiled=True)]
  transfers between devices with their start and end apart: 4 -> 4, of which waited for: 2 -> 3; matrix products, arithmetic and copies ran while one was open for 0% -> 0% of each run, Pallas kernels for 12% -> 7%
where the time goes in v4:
time: 72.4 us; the launch traced here: 71.9 us
  starting transfers between devices  20.3 us (28%)
  Pallas kernels  19.1 us (26%)
  blocking collectives  17.3 us (24%)
  waiting for transfers between devices  12.4 us (17%)
  local copies, waits for them, and re-layouts  1.43 us (2%)
  between operations  1.35 us (2%)
    all_to_all x1, blocking collectives, shards(): parts = lax.all_to_all(out, GROUP, 0, 0, tiled=True)  17.3 us
    pallas_call x1, Pallas kernels, shards(): kernel_call(step_kernel, [ANY] * 8, [((16, 192, 128), bf16)], [pltpu.SMEM...  10.2 us
    all_to_all x1, starting transfers between devices, shards(): sums = lax.all_to_all(folded, 'rows', 0, 0, tiled=True)  8.57 us
    all_to_all x1, waiting for transfers between devices, shards(): sums = lax.all_to_all(folded, 'rows', 0, 0, tiled=True)  7.53 us
    all_to_all x1, starting transfers between devices, shards(): gathered = lax.all_to_all(packed, GROUP, 0, 0, tiled=True)  5.46 us
    ppermute x1, starting transfers between devices, shards(): before = lax.ppermute(last, 'rows', up)  5.02 us
    pallas_call x1, Pallas kernels, shards(): kernel_call(prep_kernel, [ANY] * 7, [((14, 2, PLANES, SUB, 128), bf16), (...  3.93 us
    all_to_all x1, waiting for transfers between devices, shards(): gathered = lax.all_to_all(packed, GROUP, 0, 0, tiled=True)  3.41 us
  transfers between devices with their start and end apart: 4, of which 3 were waited for; matrix products, arithmetic and copies ran while one was open for 0% of the time, Pallas kernels for 7%

profile of v4, /device:TPU:0, one launch (start us, length us, event | category | flops | bytes accessed | tf_op | source)
XLA Modules:
  0.0 71.9 jit_solution(15051793665246117519)
XLA Ops:
  0.6 2.5 %shard_map.191 = (f32[36,8,128]{2,1,0:T(8,128)}, f32[36,8,128]{2,1,0:T(8,128)}, bf16[16,112,128]{2,1,0:T(8,128)(2,1)}) custom-call(f32[12,16,1024]{2,1,0:T(8,128)} %cond.3, f32[12,16,1024]{2,1,0:T(8,128)} %target.3, f32[12,16,1024]{2,1,0:T(8,128)} %noise.3, bf16[3,3,8,24]{3,2,1,0:T(8,128)(2,1)} %bitcast.6, bf16[3,3,8,128]{3,2,1,0:T(8,128)(2,1)} %bitcast.7, ...), custom_call_target="tpu_custom_call" | custom-call | tf_op jit(solution)/shard_map/pallas_call | solution.py:532
  3.2 5.0 %collective-permute-start = (f32[36,8,128]{2,1,0:T(8,128)}, f32[36,8,128]{2,1,0:T(8,128)S(1)}, u32[]{:S(2)}, u32[]{:S(2)}) collective-permute-start(f32[36,8,128]{2,1,0:T(8,128)} %get-tuple-element.14), channel_id=1, source_target_pairs={{0,8},{8,16},{16,24},{24,32},{32,40},{40,48},{48,56},{1,9},{9,17},... | collective-permute-start | bytes 442376 | tf_op jit(solution)/shard_map/ppermute | solution.py:544
  8.2 1.3 %collective-permute-start.1 = (f32[36,8,128]{2,1,0:T(8,128)}, f32[36,8,128]{2,1,0:T(8,128)S(1)}, u32[]{:S(2)}, u32[]{:S(2)}) collective-permute-start(f32[36,8,128]{2,1,0:T(8,128)} %get-tuple-element.15), channel_id=1, source_target_pairs={{8,0},{16,8},{24,16},{32,24},{40,32},{48,40},{56,48},{9,1},{17,9},... | collective-permute-start | bytes 442376 | tf_op jit(solution)/shard_map/ppermute | solution.py:545
  9.5 5.5 %all-to-all-start = ((bf16[16,112,128]{2,1,0:T(8,128)(2,1)}), bf16[16,112,128]{2,1,0:T(8,128)(2,1)S(1)}, u32[]{:S(2)}, u32[]{:S(2)}) async-start(bf16[16,112,128]{2,1,0:T(8,128)(2,1)} %get-tuple-element.18), calls=%async_computation | async-start | bytes 917504 | tf_op jit(solution)/shard_map/all_to_all | solution.py:546
  15.6 0.0 collective-permute-done.before
  15.6 0.0 copy-start.1
  15.6 1.5 %collective-permute-done.1.after = f32[36,8,128]{2,1,0:T(8,128)S(1)} collective-permute-done((f32[36,8,128]{2,1,0:T(8,128)}, f32[36,8,128]{2,1,0:T(8,128)S(1)}, u32[]{:S(2)}, u32[]{:S(2)}) %collective-permute-start.1) | collective-permute-done | bytes 147488 | tf_op jit(solution)/shard_map/ppermute | solution.py:545
  17.1 0.0 copy-done.1
  17.1 0.0 copy-start.2
  17.1 0.7 copy-done.2
  17.8 3.9 %shard_map.192 = (bf16[14,2,5,16,128]{4,3,2,1,0:T(8,128)(2,1)}, bf16[13,2,5,16,128]{4,3,2,1,0:T(8,128)(2,1)}) custom-call(f32[12,16,1024]{2,1,0:T(8,128)} %cond.3, f32[12,16,1024]{2,1,0:T(8,128)} %target.3, f32[12,16,1024]{2,1,0:T(8,128)} %noise.3, f32[36,8,128]{2,1,0:T(8,128)} %copy-done.1, f32[36,8,128]{2,1,0:T(8,128)} %copy-done.2, ...), custom_call_target="tpu_custom_call" | custom-call | flops 4294967296 | bytes 8388608 | tf_op jit(solution)/shard_map/pallas_call | solution.py:547
  21.7 3.4 %all-to-all-done.gathered_any = bf16[16,112,128]{2,1,0:T(8,128)(2,1)S(1)} async-done(((bf16[16,112,128]{2,1,0:T(8,128)(2,1)}), bf16[16,112,128]{2,1,0:T(8,128)(2,1)S(1)}, u32[]{:S(2)}, u32[]{:S(2)}) %all-to-all-start) | async-done | bytes 458784 | tf_op jit(solution)/shard_map/all_to_all | solution.py:546
  25.1 0.0 copy-start
  25.1 0.8 %copy-done = bf16[16,112,128]{2,1,0:T(8,128)(2,1)} copy-done((bf16[16,112,128]{2,1,0:T(8,128)(2,1)}, bf16[16,112,128]{2,1,0:T(8,128)(2,1)S(1)}, u32[]{:S(2)}) %copy-start) | copy-done | bytes 458776
  25.9 10.2 %shard_map.193 = bf16[16,192,128]{2,1,0:T(8,128)(2,1)} custom-call(s32[1]{0:T(128)S(6)} %copy.21.index_any, f32[32,8]{1,0:T(8,128)} %constant.14.clone.table_any, bf16[14,2,5,16,128]{4,3,2,1,0:T(8,128)(2,1)} %get-tuple-element.16.cond_any, bf16[13,2,5,16,128]{4,3,2,1,0:T(8,128)(2,1)} %get-tuple-element.17.field_any, bf16[16,112,128]{2,1,0:T(8,128)(2,1)} %copy-done, ...), custom_call_target="tpu_custom_call" | custom-call | tf_op jit(solution)/shard_map/pallas_call | solution.py:557
  36.1 17.3 %all_to_all.15.parts = bf16[16,192,128]{2,1,0:T(8,128)(2,1)S(1)} all-to-all(bf16[16,192,128]{2,1,0:T(8,128)(2,1)} %shard_map.193), channel_id=1, replica_groups=mesh['section'=2,'rows'=8,'chan'=8] {'section','chan'}, dimensions={0} | all-to-all | bytes 1572864 | tf_op jit(solution)/shard_map/all_to_all | solution.py:575
  53.3 0.7 %shard_map.195 = bf16[8,96,128]{2,1,0:T(8,128)(2,1)} custom-call(bf16[16,192,128]{2,1,0:T(8,128)(2,1)S(1)} %all_to_all.15.parts), custom_call_target="tpu_custom_call" | custom-call | tf_op jit(solution)/shard_map/pallas_call | solution.py:576
  54.1 8.6 %all-to-all-start.2 = ((bf16[8,96,128]{2,1,0:T(8,128)(2,1)}), bf16[8,96,128]{2,1,0:T(8,128)(2,1)S(1)}, u32[]{:S(2)}, u32[]{:S(2)}) async-start(bf16[8,96,128]{2,1,0:T(8,128)(2,1)} %shard_map.195), calls=%async_computation.2 | async-start | bytes 393216 | tf_op jit(solution)/shard_map/all_to_all | solution.py:581
  62.7 0.9 %shard_map.194 = bf16[12,16,1024]{2,1,0:T(8,128)(2,1)} custom-call(bf16[16,192,128]{2,1,0:T(8,128)(2,1)S(1)} %all_to_all.15.parts), custom_call_target="tpu_custom_call" | custom-call | flops 67108864 | bytes 2097152 | tf_op jit(solution)/shard_map/pallas_call | solution.py:577
  63.6 7.5 %all-to-all-done.2.parts = bf16[8,96,128]{2,1,0:T(8,128)(2,1)S(1)} async-done(((bf16[8,96,128]{2,1,0:T(8,128)(2,1)}), bf16[8,96,128]{2,1,0:T(8,128)(2,1)S(1)}, u32[]{:S(2)}, u32[]{:S(2)}) %all-to-all-start.2) | async-done | bytes 196640 | tf_op jit(solution)/shard_map/all_to_all | solution.py:581
  71.1 0.7 %shard_map.196 = (f32[3,3,8,24]{3,2,1,0:T(8,128)}, f32[3,3,8,128]{3,2,1,0:T(8,128)}, f32[3,3,8,12]{3,2,1,0:T(8,128)}, f32[1,8]{1,0:T(1,128)}) custom-call(bf16[8,96,128]{2,1,0:T(8,128)(2,1)S(1)} %all-to-all-done.2.parts), custom_call_target="tpu_custom_call" | custom-call | tf_op jit(solution)/shard_map/pallas_call | solution.py:582
Async XLA Ops:
  3.2 12.4 %collective-permute-start = (f32[36,8,128]{2,1,0:T(8,128)}, f32[36,8,128]{2,1,0:T(8,128)S(1)}, u32[]{:S(2)}, u32[]{:S(2)}) collective-permute-start(f32[36,8,128]{2,1,0:T(8,128)} %get-tuple-element.14), channel_id=1, source_target_pairs={{0,8},{8,16},{16,24},{24,32},{32,40},{40,48},{48,56},{1,9},{9,17},... | collective-permute-start | bytes 442376 | tf_op jit(solution)/shard_map/ppermute | solution.py:544
  8.2 8.9 %collective-permute-start.1 = (f32[36,8,128]{2,1,0:T(8,128)}, f32[36,8,128]{2,1,0:T(8,128)S(1)}, u32[]{:S(2)}, u32[]{:S(2)}) collective-permute-start(f32[36,8,128]{2,1,0:T(8,128)} %get-tuple-element.15), channel_id=1, source_target_pairs={{8,0},{16,8},{24,16},{32,24},{40,32},{48,40},{56,48},{9,1},{17,9},... | collective-permute-start | bytes 442376 | tf_op jit(solution)/shard_map/ppermute | solution.py:545
  9.5 15.6 %all-to-all-start = ((bf16[16,112,128]{2,1,0:T(8,128)(2,1)}), bf16[16,112,128]{2,1,0:T(8,128)(2,1)S(1)}, u32[]{:S(2)}, u32[]{:S(2)}) async-start(bf16[16,112,128]{2,1,0:T(8,128)(2,1)} %get-tuple-element.18), calls=%async_computation | async-start | bytes 917504 | tf_op jit(solution)/shard_map/all_to_all | solution.py:546
  15.6 1.5 %copy-start.1 = (f32[36,8,128]{2,1,0:T(8,128)}, f32[36,8,128]{2,1,0:T(8,128)S(1)}, u32[]{:S(2)}) copy-start(f32[36,8,128]{2,1,0:T(8,128)S(1)} %collective-permute-done.before) | copy-start | bytes 442372
  17.1 0.7 copy-start.2
  25.1 0.8 %copy-start = (bf16[16,112,128]{2,1,0:T(8,128)(2,1)}, bf16[16,112,128]{2,1,0:T(8,128)(2,1)S(1)}, u32[]{:S(2)}) copy-start(bf16[16,112,128]{2,1,0:T(8,128)(2,1)S(1)} %all-to-all-done.gathered_any) | copy-start | bytes 1376260
  54.1 17.0 %all-to-all-start.2 = ((bf16[8,96,128]{2,1,0:T(8,128)(2,1)}), bf16[8,96,128]{2,1,0:T(8,128)(2,1)S(1)}, u32[]{:S(2)}, u32[]{:S(2)}) async-start(bf16[8,96,128]{2,1,0:T(8,128)(2,1)} %shard_map.195), calls=%async_computation.2 | async-start | bytes 393216 | tf_op jit(solution)/shard_map/all_to_all | solution.py:581

commit v5 on v4

--- a/solution.py
+++ b/solution.py
@@ -98,8 +98,25 @@
     return jnp.where((col >= 0) & (col < NW), rows, 0.0).reshape(COUT, 16, 128)
 
 
-def pack_kernel(cond, target, noise, w1_any, w2_any, w3_any, r1_any, r2_any, film_any,
-                last, leading, packed, scr, w1, w2, w3, r1, r2, film, sems):
+def scalar_copies(index_any, table_any, index, table, sem_a, sem_b):
+    copies = [pltpu.make_async_copy(index_any, index, sem_a),
+              pltpu.make_async_copy(table_any, table, sem_b)]
+    for copy in copies:
+        copy.start()
+    return copies
+
+
+def send(ref, field, low):
+    high = field.astype(bf16)
+    ref[:COUT] = high
+    ref[COUT:2 * COUT] = (field - high.astype(f32)).astype(bf16)
+    ref[2 * COUT:] = low.astype(bf16)
+
+
+def pack_kernel(index_any, table_any, cond, target, noise, w1_any, w2_any, w3_any, r1_any,
+                r2_any, film_any, last, leading, packed,
+                index, table, scr, w1, w2, w3, r1, r2, film, sems):
+    scalars = scalar_copies(index_any, table_any, index, table, sems.at[9], sems.at[10])
     small = []
     for k, (src, dst) in enumerate(((w2_any, w2), (w1_any, w1), (w3_any, w3), (r1_any, r1),
                                     (r2_any, r2), (film_any, film))):
@@ -110,11 +127,14 @@
     half = lax.axis_index("section") == 0
     eye = (lax.broadcasted_iota(jnp.int32, (8, 8), 0)
            == lax.broadcasted_iota(jnp.int32, (8, 8), 1)).astype(f32)
-    for k, copy in enumerate(copies):
+    for copy in copies + scalars:
         copy.wait()
-        moved = window(scr[k])
-        last[k * COUT:(k + 1) * COUT] = moved[:, 8:]
-        leading[k * COUT:(k + 1) * COUT] = moved[:, :8]
+    draw = window(scr[1])
+    noised = window(scr[0]) + table[index[0], 0] * draw
+    low = window(scr[2])
+    row = lax.broadcasted_iota(jnp.int32, (COUT, 8, 128), 1)
+    send(last, jnp.where(row < 2, pltpu.roll(draw[:, 8:], 2, 1), noised[:, 8:]), low[:, 8:])
+    send(leading, jnp.where(row >= 6, pltpu.roll(draw[:, :8], 6, 1), noised[:, :8]), low[:, :8])
     for copy in small:
         copy.wait()
 
@@ -172,22 +192,29 @@
     return total
 
 
-def prep_kernel(cond, target, noise, before, after, order_any, spread_any,
-                cond_taps, fields, scr, wide, cond9, cells, order, spread, sems):
+def prep_kernel(index_any, table_any, cond, target, noise, before, after, order_any, spread_any,
+                cond_taps, fields, index, table, scr, wide, cond9, cells, order, spread, sems):
     copies = [window_copy(src, wide.at[k], sems.at[k])
               for k, src in enumerate((target, noise, cond))]
     others = [
-        pltpu.make_async_copy(before, scr.at[0:36, 0:8, :], sems.at[3]),
-        pltpu.make_async_copy(after, scr.at[0:36, 24:32, :], sems.at[4]),
-        pltpu.make_async_copy(order_any, order, sems.at[5]),
-        pltpu.make_async_copy(spread_any, spread, sems.at[6]),
+        pltpu.make_async_copy(order_any, order, sems.at[3]),
+        pltpu.make_async_copy(spread_any, spread, sems.at[4]),
     ]
     for copy in others:
         copy.start()
+    scalars = scalar_copies(index_any, table_any, index, table, sems.at[5], sems.at[6])
     scr[36:48] = jnp.zeros((12, 32, 128), f32)
-    for k, copy in enumerate(copies):
+    for src, rows, shift in ((before, slice(0, 8), 6), (after, slice(24, 32), 2)):
+        field = src[:COUT].astype(f32) + src[COUT:2 * COUT].astype(f32)
+        scr[0:12, rows] = field
+        scr[12:24, rows] = pltpu.roll(field, shift, 1)
+        scr[24:36, rows] = src[2 * COUT:].astype(f32)
+    for copy in copies + scalars:
         copy.wait()
-        scr[k * COUT:(k + 1) * COUT, 8:24] = window(wide[k])
+    draw = window(wide[1])
+    scr[0:12, 8:24] = window(wide[0]) + table[index[0], 0] * draw
+    scr[12:24, 8:24] = draw
+    scr[24:36, 8:24] = window(wide[2])
     for copy in others:
         copy.wait()
     flat = scr.reshape(48 * 32, 128)
@@ -247,18 +274,14 @@
     return total
 
 
-def step_kernel(index_any, table_any, cond_any, field_any, gathered_any, repeat_any, back_any,
-                spread_any, out, index, table, cond_taps, fields, gathered, repeat, back, spread, sems,
+def step_kernel(index_any, table_any, field_any, cond_taps, gathered, repeat, back, spread, out,
+                index, table, fields, sems,
                 w2, w2t, w1, w3, w3f, w3r, r1, r2,
-                hid, inp, one, two, dlt, sdl, taps_in, taps_d, resid, noisy, act, slope,
+                hid, inp, one, two, dlt, sdl, taps_in, taps_d, draw, noisy, act, slope,
                 den, grad1, film_sum, den_rows, inside):
-    copies = []
-    for k, (src, dst) in enumerate(((gathered_any, gathered), (repeat_any, repeat),
-                                    (cond_any, cond_taps), (spread_any, spread),
-                                    (field_any, fields), (index_any, index),
-                                    (table_any, table), (back_any, back))):
-        copies.append(pltpu.make_async_copy(src, dst, sems.at[k]))
-        copies[-1].start()
+    copies = scalar_copies(index_any, table_any, index, table, sems.at[0], sems.at[1])
+    copies.append(pltpu.make_async_copy(field_any, fields, sems.at[2]))
+    copies[-1].start()
     first_row = lax.axis_index("rows") * 16 - RIM
     first_col = member() * TW - RIM
     for ref in (w2, w2t, w3r, r2):
@@ -283,11 +306,9 @@
         return slice(at, at + 128)
 
     halves = (slice(0, 128), slice(128, 256))
-    copies[0].wait()
     for v in range(2):
         r1[halves[v], halves[v]] = block(12)
     w3[...] = block(11)
-    copies[1].wait()
     wide = dot(block(13), repeat[:, :9 * 128]).astype(bf16)
     for tap in range(TAPS):
         for v in range(2):
@@ -336,7 +357,6 @@
             x = value[:, halves[v]]
             put_pair(hid, 2 + v, k, n, cells(x * sigmoid(x)) * inside[...])
 
-    copies[2].wait()
     sweep(14, 7, reg_one)
     clear(hid)
 
@@ -346,13 +366,12 @@
             row = 3 + v
             mean = cells(value[:, halves[v]]).astype(bf16).astype(f32)
             both = dot(flat(some(fields, row, k, n, 3)[...]), spread[...])
-            rest = cells(both[:, halves[0]]) - mean
-            noised = rest + sigma * cells(both[:, halves[1]])
-            some(resid, row, k, n, 3)[...] = rest
+            noised = cells(both[:, halves[0]]) - mean
+            some(draw, row, k, n, 3)[...] = cells(both[:, halves[1]])
             some(noisy, row, k, n, 3)[...] = noised
             put_pair(inp, row, k, n, in_coef * noised * inside[...])
 
-    for copy in copies[3:]:
+    for copy in copies:
         copy.wait()
     level = index[0]
     sigma, skip, out_coef = table[level, 0], table[level, 1], table[level, 2]
@@ -392,9 +411,10 @@
         value = dot(stack_rows(two, 6, k, n), w3r[...])
         for v in range(2):
             row = 6 + v
-            full = skip * some(noisy, row, k, n, 3)[...] + out_coef * cells(value[:, halves[v]])
+            noised = some(noisy, row, k, n, 3)[...]
+            full = skip * noised + out_coef * cells(value[:, halves[v]])
             some(den, row, k, n, 6)[:, :PLANES] = full.astype(bf16)
-            delta = delta_coef * (full - some(resid, row, k, n, 3)[...])
+            delta = delta_coef * (full - (noised - sigma * some(draw, row, k, n, 3)[...]))
             put_pair(dlt, row, k, n, delta * inside[...])
 
     sweep(10, 5, conv_three)
@@ -529,15 +549,17 @@
 def shards(condition, target, noise_draw, sigma_index, reg_first, reg_second, first_kernel,
            second_kernel, third_kernel, film_scale):
     order, back, spread, repeat = place_constants()
+    table = jnp.asarray(coef_table())
     last, leading, packed = kernel_call(
-        pack_kernel, [ANY] * 9,
-        [((36, 8, 128), f32), ((36, 8, 128), f32), ((16, 112, 128), bf16)],
-        [pltpu.VMEM((3, COUT, 16, 256), f32), pltpu.VMEM((3, 3, 8, 24), bf16),
+        pack_kernel, [ANY] * 11,
+        [((36, 8, 128), bf16), ((36, 8, 128), bf16), ((16, 112, 128), bf16)],
+        [pltpu.SMEM((1,), jnp.int32), pltpu.SMEM((NSIG, 8), f32),
+         pltpu.VMEM((3, COUT, 16, 256), f32), pltpu.VMEM((3, 3, 8, 24), bf16),
          pltpu.VMEM((3, 3, 8, 128), bf16), pltpu.VMEM((3, 3, 8, 12), bf16),
          pltpu.VMEM((3, 3, 12, 16), bf16), pltpu.VMEM((3, 3, 16, 12), bf16),
-         pltpu.VMEM((1, 8), bf16), pltpu.SemaphoreType.DMA((9,))],
+         pltpu.VMEM((1, 8), bf16), pltpu.SemaphoreType.DMA((11,))],
         limit=60,
-    )(condition, target, noise_draw, jnp.swapaxes(first_kernel, 2, 3),
+    )(sigma_index, table, condition, target, noise_draw, jnp.swapaxes(first_kernel, 2, 3),
       jnp.swapaxes(second_kernel, 2, 3), third_kernel, reg_first, reg_second,
       film_scale.reshape(1, 8))
     up = [(i, i + 1) for i in range(lax.axis_size("rows") - 1)]
@@ -545,21 +567,20 @@
     after = lax.ppermute(leading, "rows", [(j, i) for i, j in up])
     gathered = lax.all_to_all(packed, GROUP, 0, 0, tiled=True)
     cond_taps, fields = kernel_call(
-        prep_kernel, [ANY] * 7,
+        prep_kernel, [ANY] * 5 + [VMEM] * 2 + [ANY] * 2,
         [((14, 2, PLANES, SUB, 128), bf16), ((13, 2, PLANES, SUB, 128), bf16)],
-        [pltpu.VMEM((48, 32, 128), f32), pltpu.VMEM((3, COUT, 16, 256), f32),
+        [pltpu.SMEM((1,), jnp.int32), pltpu.SMEM((NSIG, 8), f32),
+         pltpu.VMEM((48, 32, 128), f32), pltpu.VMEM((3, COUT, 16, 256), f32),
          planes(32, bf16, 7), pltpu.VMEM((30 * WIN, 128), bf16), pltpu.VMEM((WIN, 128), bf16), pltpu.VMEM((128, 128), bf16),
          pltpu.SemaphoreType.DMA((7,))],
-        limit=60,
+        limit=52,
         cost=pl.CostEstimate(flops=1 << 32, bytes_accessed=8 * MIB, transcendentals=0),
-    )(condition, target, noise_draw, before, after, jnp.asarray(order, bf16), jnp.asarray(spread[:, :128], bf16))
+    )(sigma_index, table, condition, target, noise_draw, before, after, jnp.asarray(order, bf16), jnp.asarray(spread[:, :128], bf16))
     wide = [pairs(32, bf16, PLANES + 2) for _ in range(6)]
     out, = kernel_call(
-        step_kernel, [ANY] * 8, [((16, 192, 128), bf16)],
-        [pltpu.SMEM((1,), jnp.int32), pltpu.SMEM((NSIG, 8), f32), pairs(28, bf16),
-         pairs(26, bf16), pltpu.VMEM((16, 112, 128), bf16), pltpu.VMEM((128, 1280), bf16),
-         pltpu.VMEM((128, 128), bf16), pltpu.VMEM((128, 256), bf16),
-         pltpu.SemaphoreType.DMA((8,)), pltpu.VMEM((256, 1536), bf16),
+        step_kernel, [ANY] * 3 + [VMEM] * 5, [((16, 192, 128), bf16)],
+        [pltpu.SMEM((1,), jnp.int32), pltpu.SMEM((NSIG, 8), f32), pairs(26, bf16),
+         pltpu.SemaphoreType.DMA((3,)), pltpu.VMEM((256, 1536), bf16),
          pltpu.VMEM((1536, 256), bf16), pltpu.VMEM((128, 256), bf16),
          pltpu.VMEM((128, 128), bf16), pltpu.VMEM((256, 256), bf16),
          pltpu.VMEM((1536, 256), bf16), pltpu.VMEM((256, 256), bf16),
@@ -569,9 +590,9 @@
            pairs(24, f32), pairs(22, f32), pairs(20, bf16, 8), pairs(16, bf16),
            pltpu.VMEM((8, 128), f32), pltpu.VMEM((256, 128), f32),
            pltpu.VMEM((PLANES, SUB, 128), f32)],
-        limit=60,
-    )(sigma_index, jnp.asarray(coef_table()), cond_taps, fields, gathered,
-      jnp.asarray(repeat, bf16), jnp.asarray(back, bf16), jnp.asarray(spread[:, 128:], bf16))
+        limit=52,
+    )(sigma_index, table, fields, cond_taps, gathered, jnp.asarray(repeat, bf16),
+      jnp.asarray(back, bf16), jnp.asarray(spread[:, 128:], bf16))
     parts = lax.all_to_all(out, GROUP, 0, 0, tiled=True)
     folded, = kernel_call(fold_kernel, [VMEM], [((8, 96, 128), bf16)])(parts)
     denoised, = kernel_call(

time: 72.4 us -> 71.6 us (0.989)
  waiting for transfers between devices: 12.4 us -> 14.5 us
  Pallas kernels: 19.1 us -> 17.4 us
  local copies, waits for them, and re-layouts: 1.43 us -> 0.04 us
    all_to_all x1, waiting for transfers between devices: 3.41 us -> 6.02 us  [shards(): gathered = lax.all_to_all(packed, GROUP, 0, 0, tiled=True)]
    pallas_call x3, Pallas kernels: 16.7 us -> 15 us  [the longest x1 9.32 us: shards(): kernel_call(step_kernel, [ANY] * 3 + [VMEM] * 5, [((16, 192, 128), bf16)]...]
    unnamed x6 -> x12, local copies, waits for them, and re-layouts: 1.43 us -> 0.04 us
  transfers between devices with their start and end apart: 4 -> 4, of which waited for: 3 -> 3; matrix products, arithmetic and copies ran while one was open for 0% -> 0% of each run, Pallas kernels for 7% -> 6%
where the time goes in v5:
time: 71.6 us; the launch traced here: 71.1 us
  starting transfers between devices  20.5 us (29%)
  Pallas kernels  17.4 us (24%)
  blocking collectives  17.3 us (24%)
  waiting for transfers between devices  14.5 us (20%)
  between operations  1.39 us (2%)
    all_to_all x1, blocking collectives, shards(): parts = lax.all_to_all(out, GROUP, 0, 0, tiled=True)  17.3 us
    pallas_call x1, Pallas kernels, shards(): kernel_call(step_kernel, [ANY] * 3 + [VMEM] * 5, [((16, 192, 128), bf16)]...  9.32 us
    all_to_all x1, starting transfers between devices, shards(): sums = lax.all_to_all(folded, 'rows', 0, 0, tiled=True)  8.56 us
    all_to_all x1, waiting for transfers between devices, shards(): sums = lax.all_to_all(folded, 'rows', 0, 0, tiled=True)  7.53 us
    all_to_all x1, waiting for transfers between devices, shards(): gathered = lax.all_to_all(packed, GROUP, 0, 0, tiled=True)  6.02 us
    all_to_all x1, starting transfers between devices, shards(): gathered = lax.all_to_all(packed, GROUP, 0, 0, tiled=True)  5.59 us
    ppermute x1, starting transfers between devices, shards(): before = lax.ppermute(last, 'rows', up)  5.01 us
    pallas_call x1, Pallas kernels, shards(): kernel_call(prep_kernel, [ANY] * 5 + [VMEM] * 2 + [ANY] * 2, [((14, 2, PL...  3.09 us
  transfers between devices with their start and end apart: 4, of which 3 were waited for; matrix products, arithmetic and copies ran while one was open for 0% of the time, Pallas kernels for 6%

profile of v5, /device:TPU:0, one launch (start us, length us, event | category | flops | bytes accessed | tf_op | source)
XLA Modules:
  0.0 71.1 jit_solution(4911582558631292881)
XLA Ops:
  1.3 2.6 %shard_map.191 = (bf16[36,8,128]{2,1,0:T(8,128)(2,1)}, bf16[36,8,128]{2,1,0:T(8,128)(2,1)}, bf16[16,112,128]{2,1,0:T(8,128)(2,1)}) custom-call(s32[1]{0:T(128)S(6)} %copy.21.index_any, f32[32,8]{1,0:T(8,128)} %constant.12.clone.table_any, f32[12,16,1024]{2,1,0:T(8,128)} %cond.3, f32[12,16,1024]{2,1,0:T(8,128)} %target.3, f32[12,16,1024]{2,1,0:T(8,128)} %noise.3, ...), custom_call_target="tpu_custom_call" | custom-call | tf_op jit(solution)/shard_map/pallas_call | solution.py:553
  3.9 5.0 %collective-permute-start = (bf16[36,8,128]{2,1,0:T(8,128)(2,1)}, bf16[36,8,128]{2,1,0:T(8,128)(2,1)S(1)}, u32[]{:S(2)}, u32[]{:S(2)}) collective-permute-start(bf16[36,8,128]{2,1,0:T(8,128)(2,1)} %get-tuple-element.14), channel_id=1, source_target_pairs={{0,8},{8,16},{16,24},{24,32},{32,40},{40,48},{48,56},{1,9},{9,17},... | collective-permute-start | bytes 221192 | tf_op jit(solution)/shard_map/ppermute | solution.py:566
  8.9 1.3 %collective-permute-start.1 = (bf16[36,8,128]{2,1,0:T(8,128)(2,1)}, bf16[36,8,128]{2,1,0:T(8,128)(2,1)S(1)}, u32[]{:S(2)}, u32[]{:S(2)}) collective-permute-start(bf16[36,8,128]{2,1,0:T(8,128)(2,1)} %get-tuple-element.15), channel_id=1, source_target_pairs={{8,0},{16,8},{24,16},{32,24},{40,32},{48,40},{56,48},{9,1},{17,9},... | collective-permute-start | bytes 221192 | tf_op jit(solution)/shard_map/ppermute | solution.py:567
  10.2 0.0 copy-start.1
  10.2 0.0 copy-start.4
  10.2 0.0 copy-start.5
  10.2 5.6 %all-to-all-start = ((bf16[16,112,128]{2,1,0:T(8,128)(2,1)}), bf16[16,112,128]{2,1,0:T(8,128)(2,1)S(1)}, u32[]{:S(2)}, u32[]{:S(2)}) async-start(bf16[16,112,128]{2,1,0:T(8,128)(2,1)} %get-tuple-element.18), calls=%async_computation | async-start | bytes 917504 | tf_op jit(solution)/shard_map/all_to_all | solution.py:568
  15.8 0.0 copy-start
  15.8 0.0 copy-start.2
  15.9 0.0 copy-start.3
  15.9 0.0 collective-permute-done.before
  15.9 1.0 %collective-permute-done.1.after = bf16[36,8,128]{2,1,0:T(8,128)(2,1)S(1)} collective-permute-done((bf16[36,8,128]{2,1,0:T(8,128)(2,1)}, bf16[36,8,128]{2,1,0:T(8,128)(2,1)S(1)}, u32[]{:S(2)}, u32[]{:S(2)}) %collective-permute-start.1) | collective-permute-done | bytes 73760 | tf_op jit(solution)/shard_map/ppermute | solution.py:567
  16.9 0.0 copy-done.1
  16.9 0.0 copy-done.4
  16.9 0.0 copy-done.5
  16.9 3.1 %shard_map.192 = (bf16[14,2,5,16,128]{4,3,2,1,0:T(8,128)(2,1)S(1)}, bf16[13,2,5,16,128]{4,3,2,1,0:T(8,128)(2,1)S(1)}) custom-call(s32[1]{0:T(128)S(6)} %copy.21.index_any, f32[32,8]{1,0:T(8,128)S(1)} %copy-done.1, f32[12,16,1024]{2,1,0:T(8,128)} %cond.3, f32[12,16,1024]{2,1,0:T(8,128)} %target.3, f32[12,16,1024]{2,1,0:T(8,128)} %noise.3, ...), custom_call_target="tpu_custom_call" | custom-call | flops 4294967296 | bytes 8388608 | tf_op jit(solution)/shard_map/pallas_call | solution.py:569
  20.0 6.0 %all-to-all-done.gathered = bf16[16,112,128]{2,1,0:T(8,128)(2,1)S(1)} async-done(((bf16[16,112,128]{2,1,0:T(8,128)(2,1)}), bf16[16,112,128]{2,1,0:T(8,128)(2,1)S(1)}, u32[]{:S(2)}, u32[]{:S(2)}) %all-to-all-start) | async-done | bytes 458784 | tf_op jit(solution)/shard_map/all_to_all | solution.py:568
  26.0 0.0 copy-done
  26.0 0.0 copy-done.2
  26.0 0.0 copy-done.3
  26.0 9.3 %shard_map.193 = bf16[16,192,128]{2,1,0:T(8,128)(2,1)} custom-call(s32[1]{0:T(128)S(6)} %copy.21.index_any, f32[32,8]{1,0:T(8,128)S(1)} %copy-done.1, bf16[13,2,5,16,128]{4,3,2,1,0:T(8,128)(2,1)S(1)} %get-tuple-element.16.field_any, bf16[14,2,5,16,128]{4,3,2,1,0:T(8,128)(2,1)S(1)} %get-tuple-element.17.cond_taps, ...), custom_call_target="tpu_custom_call" | custom-call | tf_op jit(solution)/shard_map/pallas_call | solution.py:580
  35.3 17.3 %all_to_all.15.parts = bf16[16,192,128]{2,1,0:T(8,128)(2,1)S(1)} all-to-all(bf16[16,192,128]{2,1,0:T(8,128)(2,1)} %shard_map.193), channel_id=1, replica_groups=mesh['section'=2,'rows'=8,'chan'=8] {'section','chan'}, dimensions={0} | all-to-all | bytes 1572864 | tf_op jit(solution)/shard_map/all_to_all | solution.py:596
  52.6 0.7 %shard_map.195 = bf16[8,96,128]{2,1,0:T(8,128)(2,1)} custom-call(bf16[16,192,128]{2,1,0:T(8,128)(2,1)S(1)} %all_to_all.15.parts), custom_call_target="tpu_custom_call" | custom-call | tf_op jit(solution)/shard_map/pallas_call | solution.py:597
  53.3 8.6 %all-to-all-start.2 = ((bf16[8,96,128]{2,1,0:T(8,128)(2,1)}), bf16[8,96,128]{2,1,0:T(8,128)(2,1)S(1)}, u32[]{:S(2)}, u32[]{:S(2)}) async-start(bf16[8,96,128]{2,1,0:T(8,128)(2,1)} %shard_map.195), calls=%async_computation.2 | async-start | bytes 393216 | tf_op jit(solution)/shard_map/all_to_all | solution.py:602
  61.9 0.9 %shard_map.194 = bf16[12,16,1024]{2,1,0:T(8,128)(2,1)} custom-call(bf16[16,192,128]{2,1,0:T(8,128)(2,1)S(1)} %all_to_all.15.parts), custom_call_target="tpu_custom_call" | custom-call | flops 67108864 | bytes 2097152 | tf_op jit(solution)/shard_map/pallas_call | solution.py:598
  62.8 7.5 %all-to-all-done.2.parts = bf16[8,96,128]{2,1,0:T(8,128)(2,1)S(1)} async-done(((bf16[8,96,128]{2,1,0:T(8,128)(2,1)}), bf16[8,96,128]{2,1,0:T(8,128)(2,1)S(1)}, u32[]{:S(2)}, u32[]{:S(2)}) %all-to-all-start.2) | async-done | bytes 196640 | tf_op jit(solution)/shard_map/all_to_all | solution.py:602
  70.4 0.7 %shard_map.196 = (f32[3,3,8,24]{3,2,1,0:T(8,128)}, f32[3,3,8,128]{3,2,1,0:T(8,128)}, f32[3,3,8,12]{3,2,1,0:T(8,128)}, f32[1,8]{1,0:T(1,128)}) custom-call(bf16[8,96,128]{2,1,0:T(8,128)(2,1)S(1)} %all-to-all-done.2.parts), custom_call_target="tpu_custom_call" | custom-call | tf_op jit(solution)/shard_map/pallas_call | solution.py:603
Async XLA Ops:
  3.9 12.0 %collective-permute-start = (bf16[36,8,128]{2,1,0:T(8,128)(2,1)}, bf16[36,8,128]{2,1,0:T(8,128)(2,1)S(1)}, u32[]{:S(2)}, u32[]{:S(2)}) collective-permute-start(bf16[36,8,128]{2,1,0:T(8,128)(2,1)} %get-tuple-element.14), channel_id=1, source_target_pairs={{0,8},{8,16},{16,24},{24,32},{32,40},{40,48},{48,56},{1,9},{9,17},... | collective-permute-start | bytes 221192 | tf_op jit(solution)/shard_map/ppermute | solution.py:566
  8.9 8.0 %collective-permute-start.1 = (bf16[36,8,128]{2,1,0:T(8,128)(2,1)}, bf16[36,8,128]{2,1,0:T(8,128)(2,1)S(1)}, u32[]{:S(2)}, u32[]{:S(2)}) collective-permute-start(bf16[36,8,128]{2,1,0:T(8,128)(2,1)} %get-tuple-element.15), channel_id=1, source_target_pairs={{8,0},{16,8},{24,16},{32,24},{40,32},{48,40},{56,48},{9,1},{17,9},... | collective-permute-start | bytes 221192 | tf_op jit(solution)/shard_map/ppermute | solution.py:567
  10.2 6.7 %copy-start.1 = (f32[32,8]{1,0:T(8,128)S(1)}, f32[32,8]{1,0:T(8,128)}, u32[]{:S(2)}) copy-start(f32[32,8]{1,0:T(8,128)} %constant.12.clone.table_any) | copy-start | bytes 3076
  10.2 6.7 %copy-start.4 = (bf16[128,128]{1,0:T(8,128)(2,1)S(1)}, bf16[128,128]{1,0:T(8,128)(2,1)}, u32[]{:S(2)}) copy-start(bf16[128,128]{1,0:T(8,128)(2,1)} %constant.14.clone.spread_any) | copy-start | bytes 98308
  10.2 6.6 %copy-start.5 = (bf16[80,128]{1,0:T(8,128)(2,1)S(1)}, bf16[80,128]{1,0:T(8,128)(2,1)}, u32[]{:S(2)}) copy-start(bf16[80,128]{1,0:T(8,128)(2,1)} %constant.13.clone.order_any) | copy-start | bytes 61444
  10.2 15.8 %all-to-all-start = ((bf16[16,112,128]{2,1,0:T(8,128)(2,1)}), bf16[16,112,128]{2,1,0:T(8,128)(2,1)S(1)}, u32[]{:S(2)}, u32[]{:S(2)}) async-start(bf16[16,112,128]{2,1,0:T(8,128)(2,1)} %get-tuple-element.18), calls=%async_computation | async-start | bytes 917504 | tf_op jit(solution)/shard_map/all_to_all | solution.py:568
  15.8 10.2 %copy-start = (bf16[128,1280]{1,0:T(8,128)(2,1)S(1)}, bf16[128,1280]{1,0:T(8,128)(2,1)}, u32[]{:S(2)}) copy-start(bf16[128,1280]{1,0:T(8,128)(2,1)} %constant.15.clone.repeat) | copy-start | bytes 983044
  15.8 10.1 %copy-start.2 = (bf16[128,256]{1,0:T(8,128)(2,1)S(1)}, bf16[128,256]{1,0:T(8,128)(2,1)}, u32[]{:S(2)}) copy-start(bf16[128,256]{1,0:T(8,128)(2,1)} %constant.17.clone.spread) | copy-start | bytes 196612
  15.9 10.1 %copy-start.3 = (bf16[128,128]{1,0:T(8,128)(2,1)S(1)}, bf16[128,128]{1,0:T(8,128)(2,1)}, u32[]{:S(2)}) copy-start(bf16[128,128]{1,0:T(8,128)(2,1)} %constant.16.clone.back) | copy-start | bytes 98308
  53.3 17.0 %all-to-all-start.2 = ((bf16[8,96,128]{2,1,0:T(8,128)(2,1)}), bf16[8,96,128]{2,1,0:T(8,128)(2,1)S(1)}, u32[]{:S(2)}, u32[]{:S(2)}) async-start(bf16[8,96,128]{2,1,0:T(8,128)(2,1)} %shard_map.195), calls=%async_computation.2 | async-start | bytes 393216 | tf_op jit(solution)/shard_map/all_to_all | solution.py:602

commit v6 on v5

--- a/solution.py
+++ b/solution.py
@@ -263,14 +263,17 @@
 
 def pick_pair(ref, row, k, n):
     lane = lax.broadcasted_iota(jnp.int32, (SUB, 128), 1)
-    total = None
+    parts = []
     for a in range(3):
         src = some(ref, row + a - 1, k, n)
         for b in range(3):
             low = (3 * a + b) * COUT
-            mask = jnp.where((lane >= low) & (lane < low + COUT), 1.0, 0.0).astype(bf16)
-            part = src[:, b:b + PLANES] * mask[None, None]
-            total = part if total is None else total + part
+            part = src[:, b:b + PLANES]
+            here = lane[None, None] < low + COUT
+            parts.append((part, here))
+    total = parts[8][0] * jnp.where(lane < TAPS * COUT, 1.0, 0.0).astype(bf16)[None, None]
+    for part, here in parts[7::-1]:
+        total = jnp.where(here, part, total)
     return total
 
 
@@ -284,8 +287,11 @@
     copies[-1].start()
     first_row = lax.axis_index("rows") * 16 - RIM
     first_col = member() * TW - RIM
-    for ref in (w2, w2t, w3r, r2):
-        ref[...] = jnp.zeros(ref.shape, bf16)
+    unused = (slice(9 * 128, 12 * 128), slice(0, 3 * 128))
+    for v in range(2):
+        w2[v * 128:(v + 1) * 128, unused[v]] = jnp.zeros((128, 384), bf16)
+        for ref in (w2t, w3r, r2):
+            ref[unused[v], v * 128:(v + 1) * 128] = jnp.zeros((384, 128), bf16)
     for ref in (r1, w3f):
         ref[...] = jnp.zeros(ref.shape, bf16)
     den[:, :, PLANES:] = jnp.zeros((10, 2, 8 - PLANES, SUB, 128), bf16)
@@ -342,13 +348,9 @@
             body(count // n * n, count % n)
 
     def clear(ref):
-        @pl.when(first_row < 0)
-        def _():
-            ref[0:4] = jnp.zeros((4, 2, PLANES + 2, SUB, 128), bf16)
-
-        @pl.when(first_row + 32 > NH)
-        def _():
-            ref[12:16] = jnp.zeros((4, 2, PLANES + 2, SUB, 128), bf16)
+        zero = jnp.zeros((4, 2, PLANES + 2, SUB, 128), bf16)
+        ref[pl.ds(jnp.where(first_row < 0, 0, 16), 4)] = zero
+        ref[pl.ds(jnp.where(first_row + 32 > NH, 12, 16), 4)] = zero
 
     def reg_one(k, n):
         both = jnp.concatenate([flat(some(cond_taps, 2 + v, k, n, 2)[...]) for v in range(2)], 1)
@@ -357,7 +359,7 @@
             x = value[:, halves[v]]
             put_pair(hid, 2 + v, k, n, cells(x * sigmoid(x)) * inside[...])
 
-    sweep(14, 7, reg_one)
+    sweep(14, 14, reg_one)
     clear(hid)
 
     def reg_two(k, n):
@@ -576,7 +578,7 @@
         limit=52,
         cost=pl.CostEstimate(flops=1 << 32, bytes_accessed=8 * MIB, transcendentals=0),
     )(sigma_index, table, condition, target, noise_draw, before, after, jnp.asarray(order, bf16), jnp.asarray(spread[:, :128], bf16))
-    wide = [pairs(32, bf16, PLANES + 2) for _ in range(6)]
+    wide = [pairs(40, bf16, PLANES + 2) for _ in range(6)]
     out, = kernel_call(
         step_kernel, [ANY] * 3 + [VMEM] * 5, [((16, 192, 128), bf16)],
         [pltpu.SMEM((1,), jnp.int32), pltpu.SMEM((NSIG, 8), f32), pairs(26, bf16),

time: 71.6 us -> 70.8 us (0.989)
  Pallas kernels: 17.4 us -> 16.5 us
    pallas_call x1, Pallas kernels: 9.32 us -> 8.42 us  [shards(): kernel_call(step_kernel, [ANY] * 3 + [VMEM] * 5, [((16, 192, 128), bf16)]...]
where the time goes in v6:
time: 70.8 us; the launch traced here: 70.3 us
  starting transfers between devices  20.6 us (29%)
  blocking collectives  17.3 us (24%)
  Pallas kernels  16.5 us (23%)
  waiting for transfers between devices  14.5 us (20%)
  between operations  1.39 us (2%)
    all_to_all x1, blocking collectives, shards(): parts = lax.all_to_all(out, GROUP, 0, 0, tiled=True)  17.3 us
    all_to_all x1, starting transfers between devices, shards(): sums = lax.all_to_all(folded, 'rows', 0, 0, tiled=True)  8.66 us
    pallas_call x1, Pallas kernels, shards(): kernel_call(step_kernel, [ANY] * 3 + [VMEM] * 5, [((16, 192, 128), bf16)]...  8.42 us
    all_to_all x1, waiting for transfers between devices, shards(): sums = lax.all_to_all(folded, 'rows', 0, 0, tiled=True)  7.53 us
    all_to_all x1, waiting for transfers between devices, shards(): gathered = lax.all_to_all(packed, GROUP, 0, 0, tiled=True)  6.02 us
    all_to_all x1, starting transfers between devices, shards(): gathered = lax.all_to_all(packed, GROUP, 0, 0, tiled=True)  5.59 us
    ppermute x1, starting transfers between devices, shards(): before = lax.ppermute(last, 'rows', up)  5.01 us
    pallas_call x1, Pallas kernels, shards(): kernel_call(prep_kernel, [ANY] * 5 + [VMEM] * 2 + [ANY] * 2, [((14, 2, PL...  3.09 us
  transfers between devices with their start and end apart: 4, of which 3 were waited for; matrix products, arithmetic and copies ran while one was open for 0% of the time, Pallas kernels for 6%

profile of v6, /device:TPU:0, one launch (start us, length us, event | category | flops | bytes accessed | tf_op | source)
XLA Modules:
  0.0 70.3 jit_solution(17656143000605868185)
XLA Ops:
  1.3 2.6 %shard_map.191 = (bf16[36,8,128]{2,1,0:T(8,128)(2,1)}, bf16[36,8,128]{2,1,0:T(8,128)(2,1)}, bf16[16,112,128]{2,1,0:T(8,128)(2,1)}) custom-call(s32[1]{0:T(128)S(6)} %copy.21.index_any, f32[32,8]{1,0:T(8,128)} %constant.12.clone.table_any, f32[12,16,1024]{2,1,0:T(8,128)} %cond.3, f32[12,16,1024]{2,1,0:T(8,128)} %target.3, f32[12,16,1024]{2,1,0:T(8,128)} %noise.3, ...), custom_call_target="tpu_custom_call" | custom-call | tf_op jit(solution)/shard_map/pallas_call | solution.py:555
  3.9 5.0 %collective-permute-start = (bf16[36,8,128]{2,1,0:T(8,128)(2,1)}, bf16[36,8,128]{2,1,0:T(8,128)(2,1)S(1)}, u32[]{:S(2)}, u32[]{:S(2)}) collective-permute-start(bf16[36,8,128]{2,1,0:T(8,128)(2,1)} %get-tuple-element.14), channel_id=1, source_target_pairs={{0,8},{8,16},{16,24},{24,32},{32,40},{40,48},{48,56},{1,9},{9,17},... | collective-permute-start | bytes 221192 | tf_op jit(solution)/shard_map/ppermute | solution.py:568
  8.9 1.3 %collective-permute-start.1 = (bf16[36,8,128]{2,1,0:T(8,128)(2,1)}, bf16[36,8,128]{2,1,0:T(8,128)(2,1)S(1)}, u32[]{:S(2)}, u32[]{:S(2)}) collective-permute-start(bf16[36,8,128]{2,1,0:T(8,128)(2,1)} %get-tuple-element.15), channel_id=1, source_target_pairs={{8,0},{16,8},{24,16},{32,24},{40,32},{48,40},{56,48},{9,1},{17,9},... | collective-permute-start | bytes 221192 | tf_op jit(solution)/shard_map/ppermute | solution.py:569
  10.2 0.0 copy-start.1
  10.2 0.0 copy-start.4
  10.2 0.0 copy-start.5
  10.2 5.6 %all-to-all-start = ((bf16[16,112,128]{2,1,0:T(8,128)(2,1)}), bf16[16,112,128]{2,1,0:T(8,128)(2,1)S(1)}, u32[]{:S(2)}, u32[]{:S(2)}) async-start(bf16[16,112,128]{2,1,0:T(8,128)(2,1)} %get-tuple-element.18), calls=%async_computation | async-start | bytes 917504 | tf_op jit(solution)/shard_map/all_to_all | solution.py:570
  15.8 0.0 copy-start
  15.8 0.0 copy-start.2
  15.9 0.0 copy-start.3
  15.9 0.0 collective-permute-done.before
  15.9 1.0 %collective-permute-done.1.after = bf16[36,8,128]{2,1,0:T(8,128)(2,1)S(1)} collective-permute-done((bf16[36,8,128]{2,1,0:T(8,128)(2,1)}, bf16[36,8,128]{2,1,0:T(8,128)(2,1)S(1)}, u32[]{:S(2)}, u32[]{:S(2)}) %collective-permute-start.1) | collective-permute-done | bytes 73760 | tf_op jit(solution)/shard_map/ppermute | solution.py:569
  16.9 0.0 copy-done.1
  16.9 0.0 copy-done.4
  16.9 0.0 copy-done.5
  16.9 3.1 %shard_map.192 = (bf16[14,2,5,16,128]{4,3,2,1,0:T(8,128)(2,1)S(1)}, bf16[13,2,5,16,128]{4,3,2,1,0:T(8,128)(2,1)S(1)}) custom-call(s32[1]{0:T(128)S(6)} %copy.21.index_any, f32[32,8]{1,0:T(8,128)S(1)} %copy-done.1, f32[12,16,1024]{2,1,0:T(8,128)} %cond.3, f32[12,16,1024]{2,1,0:T(8,128)} %target.3, f32[12,16,1024]{2,1,0:T(8,128)} %noise.3, ...), custom_call_target="tpu_custom_call" | custom-call | flops 4294967296 | bytes 8388608 | tf_op jit(solution)/shard_map/pallas_call | solution.py:571
  20.0 6.0 %all-to-all-done.gathered = bf16[16,112,128]{2,1,0:T(8,128)(2,1)S(1)} async-done(((bf16[16,112,128]{2,1,0:T(8,128)(2,1)}), bf16[16,112,128]{2,1,0:T(8,128)(2,1)S(1)}, u32[]{:S(2)}, u32[]{:S(2)}) %all-to-all-start) | async-done | bytes 458784 | tf_op jit(solution)/shard_map/all_to_all | solution.py:570
  26.0 0.0 copy-done
  26.0 0.0 copy-done.2
  26.0 0.0 copy-done.3
  26.0 8.4 %shard_map.193 = bf16[16,192,128]{2,1,0:T(8,128)(2,1)} custom-call(s32[1]{0:T(128)S(6)} %copy.21.index_any, f32[32,8]{1,0:T(8,128)S(1)} %copy-done.1, bf16[13,2,5,16,128]{4,3,2,1,0:T(8,128)(2,1)S(1)} %get-tuple-element.16.field_any, bf16[14,2,5,16,128]{4,3,2,1,0:T(8,128)(2,1)S(1)} %get-tuple-element.17.cond_taps, ...), custom_call_target="tpu_custom_call" | custom-call | tf_op jit(solution)/shard_map/pallas_call | solution.py:582
  34.4 17.3 %all_to_all.15.parts = bf16[16,192,128]{2,1,0:T(8,128)(2,1)S(1)} all-to-all(bf16[16,192,128]{2,1,0:T(8,128)(2,1)} %shard_map.193), channel_id=1, replica_groups=mesh['section'=2,'rows'=8,'chan'=8] {'section','chan'}, dimensions={0} | all-to-all | bytes 1572864 | tf_op jit(solution)/shard_map/all_to_all | solution.py:598
  51.7 0.7 %shard_map.195 = bf16[8,96,128]{2,1,0:T(8,128)(2,1)} custom-call(bf16[16,192,128]{2,1,0:T(8,128)(2,1)S(1)} %all_to_all.15.parts), custom_call_target="tpu_custom_call" | custom-call | tf_op jit(solution)/shard_map/pallas_call | solution.py:599
  52.4 8.7 %all-to-all-start.2 = ((bf16[8,96,128]{2,1,0:T(8,128)(2,1)}), bf16[8,96,128]{2,1,0:T(8,128)(2,1)S(1)}, u32[]{:S(2)}, u32[]{:S(2)}) async-start(bf16[8,96,128]{2,1,0:T(8,128)(2,1)} %shard_map.195), calls=%async_computation.2 | async-start | bytes 393216 | tf_op jit(solution)/shard_map/all_to_all | solution.py:604
  61.1 0.9 %shard_map.194 = bf16[12,16,1024]{2,1,0:T(8,128)(2,1)} custom-call(bf16[16,192,128]{2,1,0:T(8,128)(2,1)S(1)} %all_to_all.15.parts), custom_call_target="tpu_custom_call" | custom-call | flops 67108864 | bytes 2097152 | tf_op jit(solution)/shard_map/pallas_call | solution.py:600
  62.0 7.5 %all-to-all-done.2.parts = bf16[8,96,128]{2,1,0:T(8,128)(2,1)S(1)} async-done(((bf16[8,96,128]{2,1,0:T(8,128)(2,1)}), bf16[8,96,128]{2,1,0:T(8,128)(2,1)S(1)}, u32[]{:S(2)}, u32[]{:S(2)}) %all-to-all-start.2) | async-done | bytes 196640 | tf_op jit(solution)/shard_map/all_to_all | solution.py:604
  69.6 0.7 %shard_map.196 = (f32[3,3,8,24]{3,2,1,0:T(8,128)}, f32[3,3,8,128]{3,2,1,0:T(8,128)}, f32[3,3,8,12]{3,2,1,0:T(8,128)}, f32[1,8]{1,0:T(1,128)}) custom-call(bf16[8,96,128]{2,1,0:T(8,128)(2,1)S(1)} %all-to-all-done.2.parts), custom_call_target="tpu_custom_call" | custom-call | tf_op jit(solution)/shard_map/pallas_call | solution.py:605
Async XLA Ops:
  3.9 12.0 %collective-permute-start = (bf16[36,8,128]{2,1,0:T(8,128)(2,1)}, bf16[36,8,128]{2,1,0:T(8,128)(2,1)S(1)}, u32[]{:S(2)}, u32[]{:S(2)}) collective-permute-start(bf16[36,8,128]{2,1,0:T(8,128)(2,1)} %get-tuple-element.14), channel_id=1, source_target_pairs={{0,8},{8,16},{16,24},{24,32},{32,40},{40,48},{48,56},{1,9},{9,17},... | collective-permute-start | bytes 221192 | tf_op jit(solution)/shard_map/ppermute | solution.py:568
  8.9 8.0 %collective-permute-start.1 = (bf16[36,8,128]{2,1,0:T(8,128)(2,1)}, bf16[36,8,128]{2,1,0:T(8,128)(2,1)S(1)}, u32[]{:S(2)}, u32[]{:S(2)}) collective-permute-start(bf16[36,8,128]{2,1,0:T(8,128)(2,1)} %get-tuple-element.15), channel_id=1, source_target_pairs={{8,0},{16,8},{24,16},{32,24},{40,32},{48,40},{56,48},{9,1},{17,9},... | collective-permute-start | bytes 221192 | tf_op jit(solution)/shard_map/ppermute | solution.py:569
  10.2 6.7 %copy-start.1 = (f32[32,8]{1,0:T(8,128)S(1)}, f32[32,8]{1,0:T(8,128)}, u32[]{:S(2)}) copy-start(f32[32,8]{1,0:T(8,128)} %constant.12.clone.table_any) | copy-start | bytes 3076
  10.2 6.7 %copy-start.4 = (bf16[128,128]{1,0:T(8,128)(2,1)S(1)}, bf16[128,128]{1,0:T(8,128)(2,1)}, u32[]{:S(2)}) copy-start(bf16[128,128]{1,0:T(8,128)(2,1)} %constant.14.clone.spread_any) | copy-start | bytes 98308
  10.2 6.6 %copy-start.5 = (bf16[80,128]{1,0:T(8,128)(2,1)S(1)}, bf16[80,128]{1,0:T(8,128)(2,1)}, u32[]{:S(2)}) copy-start(bf16[80,128]{1,0:T(8,128)(2,1)} %constant.13.clone.order_any) | copy-start | bytes 61444
  10.2 15.8 %all-to-all-start = ((bf16[16,112,128]{2,1,0:T(8,128)(2,1)}), bf16[16,112,128]{2,1,0:T(8,128)(2,1)S(1)}, u32[]{:S(2)}, u32[]{:S(2)}) async-start(bf16[16,112,128]{2,1,0:T(8,128)(2,1)} %get-tuple-element.18), calls=%async_computation | async-start | bytes 917504 | tf_op jit(solution)/shard_map/all_to_all | solution.py:570
  15.8 10.2 %copy-start = (bf16[128,1280]{1,0:T(8,128)(2,1)S(1)}, bf16[128,1280]{1,0:T(8,128)(2,1)}, u32[]{:S(2)}) copy-start(bf16[128,1280]{1,0:T(8,128)(2,1)} %constant.15.clone.repeat) | copy-start | bytes 983044
  15.8 10.1 %copy-start.2 = (bf16[128,256]{1,0:T(8,128)(2,1)S(1)}, bf16[128,256]{1,0:T(8,128)(2,1)}, u32[]{:S(2)}) copy-start(bf16[128,256]{1,0:T(8,128)(2,1)} %constant.17.clone.spread) | copy-start | bytes 196612
  15.9 10.1 %copy-start.3 = (bf16[128,128]{1,0:T(8,128)(2,1)S(1)}, bf16[128,128]{1,0:T(8,128)(2,1)}, u32[]{:S(2)}) copy-start(bf16[128,128]{1,0:T(8,128)(2,1)} %constant.16.clone.back) | copy-start | bytes 98308
  52.4 17.1 %all-to-all-start.2 = ((bf16[8,96,128]{2,1,0:T(8,128)(2,1)}), bf16[8,96,128]{2,1,0:T(8,128)(2,1)S(1)}, u32[]{:S(2)}, u32[]{:S(2)}) async-start(bf16[8,96,128]{2,1,0:T(8,128)(2,1)} %shard_map.195), calls=%async_computation.2 | async-start | bytes 393216 | tf_op jit(solution)/shard_map/all_to_all | solution.py:604

commit v7 on v6

--- a/solution.py
+++ b/solution.py
@@ -114,27 +114,19 @@
 
 
 def pack_kernel(index_any, table_any, cond, target, noise, w1_any, w2_any, w3_any, r1_any,
-                r2_any, film_any, last, leading, packed,
-                index, table, scr, w1, w2, w3, r1, r2, film, sems):
+                r2_any, film_any, last_any, leading_any, packed_any,
+                last, leading, packed, index, table, scr, w1, w2, w3, r1, r2, film, sems):
     scalars = scalar_copies(index_any, table_any, index, table, sems.at[9], sems.at[10])
+    copies = [window_copy(src, scr.at[k], sems.at[6 + k])
+              for k, src in enumerate((target, noise, cond))]
     small = []
     for k, (src, dst) in enumerate(((w2_any, w2), (w1_any, w1), (w3_any, w3), (r1_any, r1),
                                     (r2_any, r2), (film_any, film))):
         small.append(pltpu.make_async_copy(src, dst, sems.at[k]))
         small[-1].start()
-    copies = [window_copy(src, scr.at[k], sems.at[6 + k])
-              for k, src in enumerate((target, noise, cond))]
     half = lax.axis_index("section") == 0
     eye = (lax.broadcasted_iota(jnp.int32, (8, 8), 0)
            == lax.broadcasted_iota(jnp.int32, (8, 8), 1)).astype(f32)
-    for copy in copies + scalars:
-        copy.wait()
-    draw = window(scr[1])
-    noised = window(scr[0]) + table[index[0], 0] * draw
-    low = window(scr[2])
-    row = lax.broadcasted_iota(jnp.int32, (COUT, 8, 128), 1)
-    send(last, jnp.where(row < 2, pltpu.roll(draw[:, 8:], 2, 1), noised[:, 8:]), low[:, 8:])
-    send(leading, jnp.where(row >= 6, pltpu.roll(draw[:, :8], 6, 1), noised[:, :8]), low[:, :8])
     for copy in small:
         copy.wait()
 
@@ -170,8 +162,24 @@
                jnp.where(half, reg_a[:8], reg_a[8:]), jnp.where(half, reg_b[:8], reg_b[8:])]
     for p in range(7):
         pair = jnp.concatenate(blocks[2 * p:2 * p + 2], axis=0).astype(bf16)
-        for q in range(16):
-            packed[q, p * 16:(p + 1) * 16, :] = pair
+        packed[p * 16:(p + 1) * 16, :] = pair
+    results = [pltpu.make_async_copy(packed, packed_any.at[q], sems.at[11 + q])
+               for q in range(16)]
+    for copy in results:
+        copy.start()
+    for copy in copies + scalars:
+        copy.wait()
+    draw = window(scr[1])
+    noised = window(scr[0]) + table[index[0], 0] * draw
+    low = window(scr[2])
+    row = lax.broadcasted_iota(jnp.int32, (COUT, 8, 128), 1)
+    send(last, jnp.where(row < 2, pltpu.roll(draw[:, 8:], 2, 1), noised[:, 8:]), low[:, 8:])
+    send(leading, jnp.where(row >= 6, pltpu.roll(draw[:, :8], 6, 1), noised[:, :8]), low[:, :8])
+    for k, (src, dst) in enumerate(((last, last_any), (leading, leading_any))):
+        results.append(pltpu.make_async_copy(src, dst, sems.at[27 + k]))
+        results[-1].start()
+    for copy in results:
+        copy.wait()
 
 
 def put(ref, at, n, value):
@@ -277,8 +285,8 @@
     return total
 
 
-def step_kernel(index_any, table_any, field_any, cond_taps, gathered, repeat, back, spread, out,
-                index, table, fields, sems,
+def step_kernel(index_any, table_any, field_any, cond_taps, gathered, repeat, back, spread,
+                out_any, out, index, table, fields, sems,
                 w2, w2t, w1, w3, w3f, w3r, r1, r2,
                 hid, inp, one, two, dlt, sdl, taps_in, taps_d, draw, noisy, act, slope,
                 den, grad1, film_sum, den_rows, inside):
@@ -421,6 +429,18 @@
 
     sweep(10, 5, conv_three)
     clear(dlt)
+    fields = (lax.broadcasted_iota(jnp.int32, (16, 128), 0)
+              == lax.broadcasted_iota(jnp.int32, (16, 128), 1)).astype(f32).astype(bf16)
+    turned = dot(fields, den[1:9].reshape(16 * 128, 128), 1, 1).astype(bf16)
+    turned = jnp.concatenate([turned[:, i * 128:(i + 1) * 128] for i in range(16)], axis=0)
+    den_rows[...] = dot(turned, back[...])
+    for c in range(6):
+        left = den_rows[pl.ds(c, 16, stride=16), :]
+        right = den_rows[pl.ds(c + 6, 16, stride=16), :]
+        piece = jnp.where(lane < TW, left, right).astype(bf16)
+        out[:, 96 + c * 16:96 + (c + 1) * 16, :] = jnp.broadcast_to(piece[None], (16, 16, 128))
+    den_out = pltpu.make_async_copy(out.at[:, 96:192], out_any.at[:, 96:192], sems.at[3])
+    den_out.start()
 
     def delta_two(k, n):
         parts = []
@@ -477,17 +497,10 @@
     for p in range(6):
         pair = [part.reshape(16, 8, 128) for part in parts[2 * p:2 * p + 2]]
         out[:, p * 16:(p + 1) * 16, :] = jnp.concatenate(pair, axis=1).astype(bf16)
-
-    fields = (lax.broadcasted_iota(jnp.int32, (16, 128), 0)
-              == lax.broadcasted_iota(jnp.int32, (16, 128), 1)).astype(f32).astype(bf16)
-    turned = dot(fields, den[1:9].reshape(16 * 128, 128), 1, 1).astype(bf16)
-    turned = jnp.concatenate([turned[:, i * 128:(i + 1) * 128] for i in range(16)], axis=0)
-    den_rows[...] = dot(turned, back[...])
-    for c in range(6):
-        left = den_rows[pl.ds(c, 16, stride=16), :]
-        right = den_rows[pl.ds(c + 6, 16, stride=16), :]
-        piece = jnp.where(lane < TW, left, right).astype(bf16)
-        out[:, 96 + c * 16:96 + (c + 1) * 16, :] = jnp.broadcast_to(piece[None], (16, 16, 128))
+    grads_out = pltpu.make_async_copy(out.at[:, 0:96], out_any.at[:, 0:96], sems.at[4])
+    grads_out.start()
+    grads_out.wait()
+    den_out.wait()
 
 
 def fold_kernel(parts, out):
@@ -528,11 +541,11 @@
 ANY = pl.BlockSpec(memory_space=pl.ANY)
 
 
-def kernel_call(body, ins, outs, scratch=(), limit=16, cost=None):
+def kernel_call(body, ins, outs, scratch=(), limit=16, cost=None, out_space=VMEM):
     return pl.pallas_call(
         body,
         in_specs=list(ins),
-        out_specs=[VMEM] * len(outs),
+        out_specs=[out_space] * len(outs),
         out_shape=[jax.ShapeDtypeStruct(shape, dtype) for shape, dtype in outs],
         scratch_shapes=list(scratch),
         compiler_params=pltpu.CompilerParams(vmem_limit_bytes=limit * MIB),
@@ -555,12 +568,13 @@
     last, leading, packed = kernel_call(
         pack_kernel, [ANY] * 11,
         [((36, 8, 128), bf16), ((36, 8, 128), bf16), ((16, 112, 128), bf16)],
-        [pltpu.SMEM((1,), jnp.int32), pltpu.SMEM((NSIG, 8), f32),
+        [pltpu.VMEM((36, 8, 128), bf16), pltpu.VMEM((36, 8, 128), bf16),
+         pltpu.VMEM((112, 128), bf16), pltpu.SMEM((1,), jnp.int32), pltpu.SMEM((NSIG, 8), f32),
          pltpu.VMEM((3, COUT, 16, 256), f32), pltpu.VMEM((3, 3, 8, 24), bf16),
          pltpu.VMEM((3, 3, 8, 128), bf16), pltpu.VMEM((3, 3, 8, 12), bf16),
          pltpu.VMEM((3, 3, 12, 16), bf16), pltpu.VMEM((3, 3, 16, 12), bf16),
-         pltpu.VMEM((1, 8), bf16), pltpu.SemaphoreType.DMA((11,))],
-        limit=60,
+         pltpu.VMEM((1, 8), bf16), pltpu.SemaphoreType.DMA((29,))],
+        limit=60, out_space=ANY,
     )(sigma_index, table, condition, target, noise_draw, jnp.swapaxes(first_kernel, 2, 3),
       jnp.swapaxes(second_kernel, 2, 3), third_kernel, reg_first, reg_second,
       film_scale.reshape(1, 8))
@@ -581,8 +595,9 @@
     wide = [pairs(40, bf16, PLANES + 2) for _ in range(6)]
     out, = kernel_call(
         step_kernel, [ANY] * 3 + [VMEM] * 5, [((16, 192, 128), bf16)],
-        [pltpu.SMEM((1,), jnp.int32), pltpu.SMEM((NSIG, 8), f32), pairs(26, bf16),
-         pltpu.SemaphoreType.DMA((3,)), pltpu.VMEM((256, 1536), bf16),
+        [pltpu.VMEM((16, 192, 128), bf16), pltpu.SMEM((1,), jnp.int32),
+         pltpu.SMEM((NSIG, 8), f32), pairs(26, bf16),
+         pltpu.SemaphoreType.DMA((5,)), pltpu.VMEM((256, 1536), bf16),
          pltpu.VMEM((1536, 256), bf16), pltpu.VMEM((128, 256), bf16),
          pltpu.VMEM((128, 128), bf16), pltpu.VMEM((256, 256), bf16),
          pltpu.VMEM((1536, 256), bf16), pltpu.VMEM((256, 256), bf16),
@@ -592,7 +607,7 @@
            pairs(24, f32), pairs(22, f32), pairs(20, bf16, 8), pairs(16, bf16),
            pltpu.VMEM((8, 128), f32), pltpu.VMEM((256, 128), f32),
            pltpu.VMEM((PLANES, SUB, 128), f32)],
-        limit=52,
+        limit=52, out_space=ANY,
     )(sigma_index, table, fields, cond_taps, gathered, jnp.asarray(repeat, bf16),
       jnp.asarray(back, bf16), jnp.asarray(spread[:, 128:], bf16))
     parts = lax.all_to_all(out, GROUP, 0, 0, tiled=True)

time: 70.8 us -> 70.6 us (level)
  no operation moved by 1% of the time
where the time goes in v7:
time: 70.6 us; the launch traced here: 70.1 us
  starting transfers between devices  20.6 us (29%)
  blocking collectives  17.3 us (25%)
  Pallas kernels  16.3 us (23%)
  waiting for transfers between devices  14.5 us (21%)
  between operations  1.39 us (2%)
    all_to_all x1, blocking collectives, shards(): parts = lax.all_to_all(out, GROUP, 0, 0, tiled=True)  17.3 us
    all_to_all x1, starting transfers between devices, shards(): sums = lax.all_to_all(folded, 'rows', 0, 0, tiled=True)  8.67 us
    pallas_call x1, Pallas kernels, shards(): kernel_call(step_kernel, [ANY] * 3 + [VMEM] * 5, [((16, 192, 128), bf16)]...  8.28 us
    all_to_all x1, waiting for transfers between devices, shards(): sums = lax.all_to_all(folded, 'rows', 0, 0, tiled=True)  7.53 us
    all_to_all x1, waiting for transfers between devices, shards(): gathered = lax.all_to_all(packed, GROUP, 0, 0, tiled=True)  6.02 us
    all_to_all x1, starting transfers between devices, shards(): gathered = lax.all_to_all(packed, GROUP, 0, 0, tiled=True)  5.59 us
    ppermute x1, starting transfers between devices, shards(): before = lax.ppermute(last, 'rows', up)  5.01 us
    pallas_call x1, Pallas kernels, shards(): kernel_call(prep_kernel, [ANY] * 5 + [VMEM] * 2 + [ANY] * 2, [((14, 2, PL...  3.09 us
  transfers between devices with their start and end apart: 4, of which 3 were waited for; matrix products, arithmetic and copies ran while one was open for 0% of the time, Pallas kernels for 6%

profile of v7, /device:TPU:0, one launch (start us, length us, event | category | flops | bytes accessed | tf_op | source)
XLA Modules:
  0.0 70.1 jit_solution(144176031696171857)
XLA Ops:
  1.3 2.5 %shard_map.191 = (bf16[36,8,128]{2,1,0:T(8,128)(2,1)}, bf16[36,8,128]{2,1,0:T(8,128)(2,1)}, bf16[16,112,128]{2,1,0:T(8,128)(2,1)}) custom-call(s32[1]{0:T(128)S(6)} %copy.21.index_any, f32[32,8]{1,0:T(8,128)} %constant.12.clone.table_any, f32[12,16,1024]{2,1,0:T(8,128)} %cond.3, f32[12,16,1024]{2,1,0:T(8,128)} %target.3, f32[12,16,1024]{2,1,0:T(8,128)} %noise.3, ...), custom_call_target="tpu_custom_call" | custom-call | tf_op jit(solution)/shard_map/pallas_call | solution.py:568
  3.8 5.0 %collective-permute-start = (bf16[36,8,128]{2,1,0:T(8,128)(2,1)}, bf16[36,8,128]{2,1,0:T(8,128)(2,1)S(1)}, u32[]{:S(2)}, u32[]{:S(2)}) collective-permute-start(bf16[36,8,128]{2,1,0:T(8,128)(2,1)} %get-tuple-element.14), channel_id=1, source_target_pairs={{0,8},{8,16},{16,24},{24,32},{32,40},{40,48},{48,56},{1,9},{9,17},... | collective-permute-start | bytes 221192 | tf_op jit(solution)/shard_map/ppermute | solution.py:582
  8.8 1.3 %collective-permute-start.1 = (bf16[36,8,128]{2,1,0:T(8,128)(2,1)}, bf16[36,8,128]{2,1,0:T(8,128)(2,1)S(1)}, u32[]{:S(2)}, u32[]{:S(2)}) collective-permute-start(bf16[36,8,128]{2,1,0:T(8,128)(2,1)} %get-tuple-element.15), channel_id=1, source_target_pairs={{8,0},{16,8},{24,16},{32,24},{40,32},{48,40},{56,48},{9,1},{17,9},... | collective-permute-start | bytes 221192 | tf_op jit(solution)/shard_map/ppermute | solution.py:583
  10.1 0.0 copy-start.1
  10.2 0.0 copy-start.4
  10.2 0.0 copy-start.5
  10.2 5.6 %all-to-all-start = ((bf16[16,112,128]{2,1,0:T(8,128)(2,1)}), bf16[16,112,128]{2,1,0:T(8,128)(2,1)S(1)}, u32[]{:S(2)}, u32[]{:S(2)}) async-start(bf16[16,112,128]{2,1,0:T(8,128)(2,1)} %get-tuple-element.18), calls=%async_computation | async-start | bytes 917504 | tf_op jit(solution)/shard_map/all_to_all | solution.py:584
  15.8 0.0 copy-start
  15.8 0.0 copy-start.2
  15.8 0.0 copy-start.3
  15.8 0.0 collective-permute-done.before
  15.8 1.0 %collective-permute-done.1.after = bf16[36,8,128]{2,1,0:T(8,128)(2,1)S(1)} collective-permute-done((bf16[36,8,128]{2,1,0:T(8,128)(2,1)}, bf16[36,8,128]{2,1,0:T(8,128)(2,1)S(1)}, u32[]{:S(2)}, u32[]{:S(2)}) %collective-permute-start.1) | collective-permute-done | bytes 73760 | tf_op jit(solution)/shard_map/ppermute | solution.py:583
  16.8 0.0 copy-done.1
  16.8 0.0 copy-done.4
  16.8 0.0 copy-done.5
  16.8 3.1 %shard_map.192 = (bf16[14,2,5,16,128]{4,3,2,1,0:T(8,128)(2,1)S(1)}, bf16[13,2,5,16,128]{4,3,2,1,0:T(8,128)(2,1)S(1)}) custom-call(s32[1]{0:T(128)S(6)} %copy.21.index_any, f32[32,8]{1,0:T(8,128)S(1)} %copy-done.1, f32[12,16,1024]{2,1,0:T(8,128)} %cond.3, f32[12,16,1024]{2,1,0:T(8,128)} %target.3, f32[12,16,1024]{2,1,0:T(8,128)} %noise.3, ...), custom_call_target="tpu_custom_call" | custom-call | flops 4294967296 | bytes 8388608 | tf_op jit(solution)/shard_map/pallas_call | solution.py:585
  19.9 6.0 %all-to-all-done.gathered = bf16[16,112,128]{2,1,0:T(8,128)(2,1)S(1)} async-done(((bf16[16,112,128]{2,1,0:T(8,128)(2,1)}), bf16[16,112,128]{2,1,0:T(8,128)(2,1)S(1)}, u32[]{:S(2)}, u32[]{:S(2)}) %all-to-all-start) | async-done | bytes 458784 | tf_op jit(solution)/shard_map/all_to_all | solution.py:584
  25.9 0.0 copy-done
  25.9 0.0 copy-done.2
  25.9 0.0 copy-done.3
  26.0 8.3 %shard_map.193 = bf16[16,192,128]{2,1,0:T(8,128)(2,1)} custom-call(s32[1]{0:T(128)S(6)} %copy.21.index_any, f32[32,8]{1,0:T(8,128)S(1)} %copy-done.1, bf16[13,2,5,16,128]{4,3,2,1,0:T(8,128)(2,1)S(1)} %get-tuple-element.16.field_any, bf16[14,2,5,16,128]{4,3,2,1,0:T(8,128)(2,1)S(1)} %get-tuple-element.17.cond_taps, ...), custom_call_target="tpu_custom_call" | custom-call | tf_op jit(solution)/shard_map/pallas_call | solution.py:596
  34.2 17.3 %all_to_all.15.parts = bf16[16,192,128]{2,1,0:T(8,128)(2,1)S(1)} all-to-all(bf16[16,192,128]{2,1,0:T(8,128)(2,1)} %shard_map.193), channel_id=1, replica_groups=mesh['section'=2,'rows'=8,'chan'=8] {'section','chan'}, dimensions={0} | all-to-all | bytes 1572864 | tf_op jit(solution)/shard_map/all_to_all | solution.py:613
  51.5 0.7 %shard_map.195 = bf16[8,96,128]{2,1,0:T(8,128)(2,1)} custom-call(bf16[16,192,128]{2,1,0:T(8,128)(2,1)S(1)} %all_to_all.15.parts), custom_call_target="tpu_custom_call" | custom-call | tf_op jit(solution)/shard_map/pallas_call | solution.py:614
  52.2 8.7 %all-to-all-start.2 = ((bf16[8,96,128]{2,1,0:T(8,128)(2,1)}), bf16[8,96,128]{2,1,0:T(8,128)(2,1)S(1)}, u32[]{:S(2)}, u32[]{:S(2)}) async-start(bf16[8,96,128]{2,1,0:T(8,128)(2,1)} %shard_map.195), calls=%async_computation.2 | async-start | bytes 393216 | tf_op jit(solution)/shard_map/all_to_all | solution.py:619
  60.9 0.9 %shard_map.194 = bf16[12,16,1024]{2,1,0:T(8,128)(2,1)} custom-call(bf16[16,192,128]{2,1,0:T(8,128)(2,1)S(1)} %all_to_all.15.parts), custom_call_target="tpu_custom_call" | custom-call | flops 67108864 | bytes 2097152 | tf_op jit(solution)/shard_map/pallas_call | solution.py:615
  61.8 7.5 %all-to-all-done.2.parts = bf16[8,96,128]{2,1,0:T(8,128)(2,1)S(1)} async-done(((bf16[8,96,128]{2,1,0:T(8,128)(2,1)}), bf16[8,96,128]{2,1,0:T(8,128)(2,1)S(1)}, u32[]{:S(2)}, u32[]{:S(2)}) %all-to-all-start.2) | async-done | bytes 196640 | tf_op jit(solution)/shard_map/all_to_all | solution.py:619
  69.4 0.7 %shard_map.196 = (f32[3,3,8,24]{3,2,1,0:T(8,128)}, f32[3,3,8,128]{3,2,1,0:T(8,128)}, f32[3,3,8,12]{3,2,1,0:T(8,128)}, f32[1,8]{1,0:T(1,128)}) custom-call(bf16[8,96,128]{2,1,0:T(8,128)(2,1)S(1)} %all-to-all-done.2.parts), custom_call_target="tpu_custom_call" | custom-call | tf_op jit(solution)/shard_map/pallas_call | solution.py:620
Async XLA Ops:
  3.8 12.0 %collective-permute-start = (bf16[36,8,128]{2,1,0:T(8,128)(2,1)}, bf16[36,8,128]{2,1,0:T(8,128)(2,1)S(1)}, u32[]{:S(2)}, u32[]{:S(2)}) collective-permute-start(bf16[36,8,128]{2,1,0:T(8,128)(2,1)} %get-tuple-element.14), channel_id=1, source_target_pairs={{0,8},{8,16},{16,24},{24,32},{32,40},{40,48},{48,56},{1,9},{9,17},... | collective-permute-start | bytes 221192 | tf_op jit(solution)/shard_map/ppermute | solution.py:582
  8.8 8.0 %collective-permute-start.1 = (bf16[36,8,128]{2,1,0:T(8,128)(2,1)}, bf16[36,8,128]{2,1,0:T(8,128)(2,1)S(1)}, u32[]{:S(2)}, u32[]{:S(2)}) collective-permute-start(bf16[36,8,128]{2,1,0:T(8,128)(2,1)} %get-tuple-element.15), channel_id=1, source_target_pairs={{8,0},{16,8},{24,16},{32,24},{40,32},{48,40},{56,48},{9,1},{17,9},... | collective-permute-start | bytes 221192 | tf_op jit(solution)/shard_map/ppermute | solution.py:583
  10.1 6.7 %copy-start.1 = (f32[32,8]{1,0:T(8,128)S(1)}, f32[32,8]{1,0:T(8,128)}, u32[]{:S(2)}) copy-start(f32[32,8]{1,0:T(8,128)} %constant.12.clone.table_any) | copy-start | bytes 3076
  10.2 6.7 %copy-start.4 = (bf16[128,128]{1,0:T(8,128)(2,1)S(1)}, bf16[128,128]{1,0:T(8,128)(2,1)}, u32[]{:S(2)}) copy-start(bf16[128,128]{1,0:T(8,128)(2,1)} %constant.14.clone.spread_any) | copy-start | bytes 98308
  10.2 6.6 %copy-start.5 = (bf16[80,128]{1,0:T(8,128)(2,1)S(1)}, bf16[80,128]{1,0:T(8,128)(2,1)}, u32[]{:S(2)}) copy-start(bf16[80,128]{1,0:T(8,128)(2,1)} %constant.13.clone.order_any) | copy-start | bytes 61444
  10.2 15.8 %all-to-all-start = ((bf16[16,112,128]{2,1,0:T(8,128)(2,1)}), bf16[16,112,128]{2,1,0:T(8,128)(2,1)S(1)}, u32[]{:S(2)}, u32[]{:S(2)}) async-start(bf16[16,112,128]{2,1,0:T(8,128)(2,1)} %get-tuple-element.18), calls=%async_computation | async-start | bytes 917504 | tf_op jit(solution)/shard_map/all_to_all | solution.py:584
  15.8 10.2 %copy-start = (bf16[128,1280]{1,0:T(8,128)(2,1)S(1)}, bf16[128,1280]{1,0:T(8,128)(2,1)}, u32[]{:S(2)}) copy-start(bf16[128,1280]{1,0:T(8,128)(2,1)} %constant.15.clone.repeat) | copy-start | bytes 983044
  15.8 10.1 %copy-start.2 = (bf16[128,256]{1,0:T(8,128)(2,1)S(1)}, bf16[128,256]{1,0:T(8,128)(2,1)}, u32[]{:S(2)}) copy-start(bf16[128,256]{1,0:T(8,128)(2,1)} %constant.17.clone.spread) | copy-start | bytes 196612
  15.8 10.1 %copy-start.3 = (bf16[128,128]{1,0:T(8,128)(2,1)S(1)}, bf16[128,128]{1,0:T(8,128)(2,1)}, u32[]{:S(2)}) copy-start(bf16[128,128]{1,0:T(8,128)(2,1)} %constant.16.clone.back) | copy-start | bytes 98308
  52.2 17.1 %all-to-all-start.2 = ((bf16[8,96,128]{2,1,0:T(8,128)(2,1)}), bf16[8,96,128]{2,1,0:T(8,128)(2,1)S(1)}, u32[]{:S(2)}, u32[]{:S(2)}) async-start(bf16[8,96,128]{2,1,0:T(8,128)(2,1)} %shard_map.195), calls=%async_computation.2 | async-start | bytes 393216 | tf_op jit(solution)/shard_map/all_to_all | solution.py:619

commit v8 on v7

--- a/solution.py
+++ b/solution.py
@@ -327,19 +327,6 @@
     for tap in range(TAPS):
         for v in range(2):
             r2[spot(tap, v), halves[v]] = wide[:, tap * 128:(tap + 1) * 128]
-    w1[:, :128] = block(9)
-    w1[:, 128:] = block(10)
-    for tap in range(TAPS):
-        part = block(tap)
-        for v in range(2):
-            w2[halves[v], spot(tap, v)] = part
-            w2t[spot(8 - tap, v), halves[v]] = part
-    wide = dot(w3[...], repeat[...]).astype(bf16)
-    for tap in range(TAPS):
-        for v in range(2):
-            w3r[spot(tap, v), halves[v]] = wide[:, tap * 128:(tap + 1) * 128]
-    for v in range(2):
-        w3f[halves[v], halves[v]] = wide[:, 9 * 128:]
 
     def cells(value):
         return value.reshape(-1, PLANES, SUB, 128)
@@ -348,9 +335,12 @@
         return value.reshape(-1, 128)
 
     def sweep(count, n, body):
-        @pl.loop(0, count // n)
-        def _(k):
-            body(k * n, n)
+        if count // n == 1:
+            body(0, n)
+        else:
+            @pl.loop(0, count // n)
+            def _(k):
+                body(k * n, n)
 
         if count % n:
             body(count // n * n, count % n)
@@ -389,6 +379,19 @@
     lane = lax.broadcasted_iota(jnp.int32, (16, 128), 1)
     pick_film = jnp.where(lane == FILM_LANE, 1.0, 0.0).astype(bf16)
     gain = 1.0 + noise_coef * dot(pick_film, w3[...], 1, 1)[0:1]
+    w1[:, :128] = block(9)
+    w1[:, 128:] = block(10)
+    for tap in range(TAPS):
+        part = block(tap)
+        for v in range(2):
+            w2[halves[v], spot(tap, v)] = part
+            w2t[spot(8 - tap, v), halves[v]] = part
+    wide = dot(w3[...], repeat[...]).astype(bf16)
+    for tap in range(TAPS):
+        for v in range(2):
+            w3r[spot(tap, v), halves[v]] = wide[:, tap * 128:(tap + 1) * 128]
+    for v in range(2):
+        w3f[halves[v], halves[v]] = wide[:, 9 * 128:]
     sweep(13, 13, reg_two)
     clear(inp)
 

time: 70.6 us -> 70.7 us (level)
  no operation moved by 1% of the time
where the time goes in v8:
time: 70.7 us; the launch traced here: 70.1 us
  starting transfers between devices  20.6 us (29%)
  blocking collectives  17.3 us (24%)
  Pallas kernels  16.4 us (23%)
  waiting for transfers between devices  14.5 us (21%)
  between operations  1.39 us (2%)
    all_to_all x1, blocking collectives, shards(): parts = lax.all_to_all(out, GROUP, 0, 0, tiled=True)  17.3 us
    all_to_all x1, starting transfers between devices, shards(): sums = lax.all_to_all(folded, 'rows', 0, 0, tiled=True)  8.66 us
    pallas_call x1, Pallas kernels, shards(): kernel_call(step_kernel, [ANY] * 3 + [VMEM] * 5, [((16, 192, 128), bf16)]...  8.32 us
    all_to_all x1, waiting for transfers between devices, shards(): sums = lax.all_to_all(folded, 'rows', 0, 0, tiled=True)  7.53 us
    all_to_all x1, waiting for transfers between devices, shards(): gathered = lax.all_to_all(packed, GROUP, 0, 0, tiled=True)  6.02 us
    all_to_all x1, starting transfers between devices, shards(): gathered = lax.all_to_all(packed, GROUP, 0, 0, tiled=True)  5.59 us
    ppermute x1, starting transfers between devices, shards(): before = lax.ppermute(last, 'rows', up)  5.01 us
    pallas_call x1, Pallas kernels, shards(): kernel_call(prep_kernel, [ANY] * 5 + [VMEM] * 2 + [ANY] * 2, [((14, 2, PL...  3.09 us
  transfers between devices with their start and end apart: 4, of which 3 were waited for; matrix products, arithmetic and copies ran while one was open for 0% of the time, Pallas kernels for 6%

profile of v8, /device:TPU:0, one launch (start us, length us, event | category | flops | bytes accessed | tf_op | source)
XLA Modules:
  0.0 70.1 jit_solution(11522327163550320724)
XLA Ops:
  1.3 2.5 %shard_map.191 = (bf16[36,8,128]{2,1,0:T(8,128)(2,1)}, bf16[36,8,128]{2,1,0:T(8,128)(2,1)}, bf16[16,112,128]{2,1,0:T(8,128)(2,1)}) custom-call(s32[1]{0:T(128)S(6)} %copy.21.index_any, f32[32,8]{1,0:T(8,128)} %constant.12.clone.table_any, f32[12,16,1024]{2,1,0:T(8,128)} %cond.3, f32[12,16,1024]{2,1,0:T(8,128)} %target.3, f32[12,16,1024]{2,1,0:T(8,128)} %noise.3, ...), custom_call_target="tpu_custom_call" | custom-call | tf_op jit(solution)/shard_map/pallas_call | solution.py:571
  3.8 5.0 %collective-permute-start = (bf16[36,8,128]{2,1,0:T(8,128)(2,1)}, bf16[36,8,128]{2,1,0:T(8,128)(2,1)S(1)}, u32[]{:S(2)}, u32[]{:S(2)}) collective-permute-start(bf16[36,8,128]{2,1,0:T(8,128)(2,1)} %get-tuple-element.14), channel_id=1, source_target_pairs={{0,8},{8,16},{16,24},{24,32},{32,40},{40,48},{48,56},{1,9},{9,17},... | collective-permute-start | bytes 221192 | tf_op jit(solution)/shard_map/ppermute | solution.py:585
  8.8 1.3 %collective-permute-start.1 = (bf16[36,8,128]{2,1,0:T(8,128)(2,1)}, bf16[36,8,128]{2,1,0:T(8,128)(2,1)S(1)}, u32[]{:S(2)}, u32[]{:S(2)}) collective-permute-start(bf16[36,8,128]{2,1,0:T(8,128)(2,1)} %get-tuple-element.15), channel_id=1, source_target_pairs={{8,0},{16,8},{24,16},{32,24},{40,32},{48,40},{56,48},{9,1},{17,9},... | collective-permute-start | bytes 221192 | tf_op jit(solution)/shard_map/ppermute | solution.py:586
  10.1 0.0 copy-start.1
  10.2 0.0 copy-start.4
  10.2 0.0 copy-start.5
  10.2 5.6 %all-to-all-start = ((bf16[16,112,128]{2,1,0:T(8,128)(2,1)}), bf16[16,112,128]{2,1,0:T(8,128)(2,1)S(1)}, u32[]{:S(2)}, u32[]{:S(2)}) async-start(bf16[16,112,128]{2,1,0:T(8,128)(2,1)} %get-tuple-element.18), calls=%async_computation | async-start | bytes 917504 | tf_op jit(solution)/shard_map/all_to_all | solution.py:587
  15.8 0.0 copy-start
  15.8 0.0 copy-start.2
  15.8 0.0 copy-start.3
  15.8 0.0 collective-permute-done.before
  15.8 1.0 %collective-permute-done.1.after = bf16[36,8,128]{2,1,0:T(8,128)(2,1)S(1)} collective-permute-done((bf16[36,8,128]{2,1,0:T(8,128)(2,1)}, bf16[36,8,128]{2,1,0:T(8,128)(2,1)S(1)}, u32[]{:S(2)}, u32[]{:S(2)}) %collective-permute-start.1) | collective-permute-done | bytes 73760 | tf_op jit(solution)/shard_map/ppermute | solution.py:586
  16.8 0.0 copy-done.1
  16.8 0.0 copy-done.4
  16.8 0.0 copy-done.5
  16.8 3.1 %shard_map.192 = (bf16[14,2,5,16,128]{4,3,2,1,0:T(8,128)(2,1)S(1)}, bf16[13,2,5,16,128]{4,3,2,1,0:T(8,128)(2,1)S(1)}) custom-call(s32[1]{0:T(128)S(6)} %copy.21.index_any, f32[32,8]{1,0:T(8,128)S(1)} %copy-done.1, f32[12,16,1024]{2,1,0:T(8,128)} %cond.3, f32[12,16,1024]{2,1,0:T(8,128)} %target.3, f32[12,16,1024]{2,1,0:T(8,128)} %noise.3, ...), custom_call_target="tpu_custom_call" | custom-call | flops 4294967296 | bytes 8388608 | tf_op jit(solution)/shard_map/pallas_call | solution.py:588
  19.9 6.0 %all-to-all-done.gathered = bf16[16,112,128]{2,1,0:T(8,128)(2,1)S(1)} async-done(((bf16[16,112,128]{2,1,0:T(8,128)(2,1)}), bf16[16,112,128]{2,1,0:T(8,128)(2,1)S(1)}, u32[]{:S(2)}, u32[]{:S(2)}) %all-to-all-start) | async-done | bytes 458784 | tf_op jit(solution)/shard_map/all_to_all | solution.py:587
  25.9 0.0 copy-done
  25.9 0.0 copy-done.2
  25.9 0.0 copy-done.3
  26.0 8.3 %shard_map.193 = bf16[16,192,128]{2,1,0:T(8,128)(2,1)} custom-call(s32[1]{0:T(128)S(6)} %copy.21.index_any, f32[32,8]{1,0:T(8,128)S(1)} %copy-done.1, bf16[13,2,5,16,128]{4,3,2,1,0:T(8,128)(2,1)S(1)} %get-tuple-element.16.field_any, bf16[14,2,5,16,128]{4,3,2,1,0:T(8,128)(2,1)S(1)} %get-tuple-element.17.cond_taps, ...), custom_call_target="tpu_custom_call" | custom-call | tf_op jit(solution)/shard_map/pallas_call | solution.py:599
  34.3 17.3 %all_to_all.15.parts = bf16[16,192,128]{2,1,0:T(8,128)(2,1)S(1)} all-to-all(bf16[16,192,128]{2,1,0:T(8,128)(2,1)} %shard_map.193), channel_id=1, replica_groups=mesh['section'=2,'rows'=8,'chan'=8] {'section','chan'}, dimensions={0} | all-to-all | bytes 1572864 | tf_op jit(solution)/shard_map/all_to_all | solution.py:616
  51.5 0.7 %shard_map.195 = bf16[8,96,128]{2,1,0:T(8,128)(2,1)} custom-call(bf16[16,192,128]{2,1,0:T(8,128)(2,1)S(1)} %all_to_all.15.parts), custom_call_target="tpu_custom_call" | custom-call | tf_op jit(solution)/shard_map/pallas_call | solution.py:617
  52.3 8.7 %all-to-all-start.2 = ((bf16[8,96,128]{2,1,0:T(8,128)(2,1)}), bf16[8,96,128]{2,1,0:T(8,128)(2,1)S(1)}, u32[]{:S(2)}, u32[]{:S(2)}) async-start(bf16[8,96,128]{2,1,0:T(8,128)(2,1)} %shard_map.195), calls=%async_computation.2 | async-start | bytes 393216 | tf_op jit(solution)/shard_map/all_to_all | solution.py:622
  60.9 0.9 %shard_map.194 = bf16[12,16,1024]{2,1,0:T(8,128)(2,1)} custom-call(bf16[16,192,128]{2,1,0:T(8,128)(2,1)S(1)} %all_to_all.15.parts), custom_call_target="tpu_custom_call" | custom-call | flops 67108864 | bytes 2097152 | tf_op jit(solution)/shard_map/pallas_call | solution.py:618
  61.9 7.5 %all-to-all-done.2.parts = bf16[8,96,128]{2,1,0:T(8,128)(2,1)S(1)} async-done(((bf16[8,96,128]{2,1,0:T(8,128)(2,1)}), bf16[8,96,128]{2,1,0:T(8,128)(2,1)S(1)}, u32[]{:S(2)}, u32[]{:S(2)}) %all-to-all-start.2) | async-done | bytes 196640 | tf_op jit(solution)/shard_map/all_to_all | solution.py:622
  69.4 0.7 %shard_map.196 = (f32[3,3,8,24]{3,2,1,0:T(8,128)}, f32[3,3,8,128]{3,2,1,0:T(8,128)}, f32[3,3,8,12]{3,2,1,0:T(8,128)}, f32[1,8]{1,0:T(1,128)}) custom-call(bf16[8,96,128]{2,1,0:T(8,128)(2,1)S(1)} %all-to-all-done.2.parts), custom_call_target="tpu_custom_call" | custom-call | tf_op jit(solution)/shard_map/pallas_call | solution.py:623
Async XLA Ops:
  3.8 12.0 %collective-permute-start = (bf16[36,8,128]{2,1,0:T(8,128)(2,1)}, bf16[36,8,128]{2,1,0:T(8,128)(2,1)S(1)}, u32[]{:S(2)}, u32[]{:S(2)}) collective-permute-start(bf16[36,8,128]{2,1,0:T(8,128)(2,1)} %get-tuple-element.14), channel_id=1, source_target_pairs={{0,8},{8,16},{16,24},{24,32},{32,40},{40,48},{48,56},{1,9},{9,17},... | collective-permute-start | bytes 221192 | tf_op jit(solution)/shard_map/ppermute | solution.py:585
  8.8 8.0 %collective-permute-start.1 = (bf16[36,8,128]{2,1,0:T(8,128)(2,1)}, bf16[36,8,128]{2,1,0:T(8,128)(2,1)S(1)}, u32[]{:S(2)}, u32[]{:S(2)}) collective-permute-start(bf16[36,8,128]{2,1,0:T(8,128)(2,1)} %get-tuple-element.15), channel_id=1, source_target_pairs={{8,0},{16,8},{24,16},{32,24},{40,32},{48,40},{56,48},{9,1},{17,9},... | collective-permute-start | bytes 221192 | tf_op jit(solution)/shard_map/ppermute | solution.py:586
  10.1 6.7 %copy-start.1 = (f32[32,8]{1,0:T(8,128)S(1)}, f32[32,8]{1,0:T(8,128)}, u32[]{:S(2)}) copy-start(f32[32,8]{1,0:T(8,128)} %constant.12.clone.table_any) | copy-start | bytes 3076
  10.2 6.7 %copy-start.4 = (bf16[128,128]{1,0:T(8,128)(2,1)S(1)}, bf16[128,128]{1,0:T(8,128)(2,1)}, u32[]{:S(2)}) copy-start(bf16[128,128]{1,0:T(8,128)(2,1)} %constant.14.clone.spread_any) | copy-start | bytes 98308
  10.2 6.6 %copy-start.5 = (bf16[80,128]{1,0:T(8,128)(2,1)S(1)}, bf16[80,128]{1,0:T(8,128)(2,1)}, u32[]{:S(2)}) copy-start(bf16[80,128]{1,0:T(8,128)(2,1)} %constant.13.clone.order_any) | copy-start | bytes 61444
  10.2 15.8 %all-to-all-start = ((bf16[16,112,128]{2,1,0:T(8,128)(2,1)}), bf16[16,112,128]{2,1,0:T(8,128)(2,1)S(1)}, u32[]{:S(2)}, u32[]{:S(2)}) async-start(bf16[16,112,128]{2,1,0:T(8,128)(2,1)} %get-tuple-element.18), calls=%async_computation | async-start | bytes 917504 | tf_op jit(solution)/shard_map/all_to_all | solution.py:587
  15.8 10.2 %copy-start = (bf16[128,1280]{1,0:T(8,128)(2,1)S(1)}, bf16[128,1280]{1,0:T(8,128)(2,1)}, u32[]{:S(2)}) copy-start(bf16[128,1280]{1,0:T(8,128)(2,1)} %constant.15.clone.repeat) | copy-start | bytes 983044
  15.8 10.1 %copy-start.2 = (bf16[128,256]{1,0:T(8,128)(2,1)S(1)}, bf16[128,256]{1,0:T(8,128)(2,1)}, u32[]{:S(2)}) copy-start(bf16[128,256]{1,0:T(8,128)(2,1)} %constant.17.clone.spread) | copy-start | bytes 196612
  15.8 10.1 %copy-start.3 = (bf16[128,128]{1,0:T(8,128)(2,1)S(1)}, bf16[128,128]{1,0:T(8,128)(2,1)}, u32[]{:S(2)}) copy-start(bf16[128,128]{1,0:T(8,128)(2,1)} %constant.16.clone.back) | copy-start | bytes 98308
  52.3 17.1 %all-to-all-start.2 = ((bf16[8,96,128]{2,1,0:T(8,128)(2,1)}), bf16[8,96,128]{2,1,0:T(8,128)(2,1)S(1)}, u32[]{:S(2)}, u32[]{:S(2)}) async-start(bf16[8,96,128]{2,1,0:T(8,128)(2,1)} %shard_map.195), calls=%async_computation.2 | async-start | bytes 393216 | tf_op jit(solution)/shard_map/all_to_all | solution.py:622
